TPU v7x, 256 devices: a whole 4x4x8 slice. The times are simulated.
256 devices in a mesh: gx: 32 (over y, z_lo, x), gy: 8 (over z_hi, core).
Axes of the slice: x: 4, y: 4, z: 8 (z_hi: 4, z_lo: 2; z = z_hi * 2 + z_lo), core: 2. Of those that a mesh axis runs over, the one named last changes fastest.
Arguments:
- features: bfloat16 [32, 8, 2, 512, 128], P('gx', 'gy'), may hold values from -6 to 6
- cotangent: bfloat16 [32, 8, 2, 512, 128], P('gx', 'gy'), may hold values from -6 to 6
- neighbours: int32 [32, 8, 2, 27], P('gx', 'gy'), may hold values from -1 to 17, as said below
- weights: bfloat16 [27, 128, 128], replicated, may hold values from -0.109375 to 0.109375
- channel_gain: float32 [128], replicated, may hold values from 0.5 to 2
Outputs:
- output: bfloat16 [32, 8, 2, 512, 128], P('gx', 'gy')
- input_grad: bfloat16 [32, 8, 2, 512, 128], P('gx', 'gy')
- weight_grad: float32 [27, 128, 128], replicated
- gain_grad: float32 [128], replicated
Inputs may be any that keep to these rules, and one draw needn't show every extreme that they name: `neighbours`: entry [i, j, s, k] names, for slot s of device (i, j) and direction k = 9 (a + 1) + 3 (b + 1) + (c + 1), the block at block offset (a, b, c): the code (3 (i2 - i + 1) + (j2 - j + 1)) * 2 + s2 for slot s2 of device (i2, j2), always equal or beside (i, j), with i2 - i equal to 0 or a and j2 - j equal to 0 or b, or -1 where no occupied block lies. Codes are therefore at most 17. Entry 13 is 8 + s for an occupied slot; an empty slot has -1 everywhere. The relation is symmetric: the block named in direction k names the first one back in direction 26 - k. Some device has all 2 slots occupied.
All inputs are finite; a program needn't handle non-finite values.
Results may differ from a plain program's by a relative error of at most 0.0042.
Values may be sent and summed in bfloat16 or wider, within the bound.
No kernel may reach another device: no remote copies, remote signals or barrier semaphores. Data moves between devices by JAX's collectives and lax.ppermute only.
A program may use at most 64 MiB of HBM per device.

v0:
```python
from functools import partial

import jax
import jax.numpy as jnp
from jax import lax
from jax.sharding import PartitionSpec as P

DIRECTIONS = [(a, b, c) for a in (-1, 0, 1) for b in (-1, 0, 1) for c in (-1, 0, 1)]


def padded(value, sides, width):
    for axis, dim in sides:
        count, length = (lax.axis_size(axis), value.shape[dim])
        up = [(i, (i + 1) % count) for i in range(count - 1)]
        down = [(j, i) for i, j in up]
        last = lax.slice_in_dim(value, length - width, length, axis=dim)
        leading = lax.slice_in_dim(value, 0, width, axis=dim)
        before = lax.ppermute(last, axis, up)
        after = lax.ppermute(leading, axis, down)
        value = jnp.concatenate([before, value, after], axis=dim)
    return value


def rim_bounds(d):
    if d < 0:
        return (7, 8)
    if d == 0:
        return (0, 8)
    return (0, 1)


def rim_range(d):
    lower, upper = rim_bounds(d)
    return slice(lower, upper)


def region_of(gathered_table, use_faces, a, b, c):
    return gathered_table[:, rim_range(a), rim_range(b), rim_range(c)]


def assemble(own_blocks, region_fn, slot_codes):
    planes = []
    for a in (-1, 0, 1):
        row_parts = []
        for b in (-1, 0, 1):
            col_parts = []
            for c in (-1, 0, 1):
                k = (a + 1) * 9 + (b + 1) * 3 + (c + 1)
                if k == 13:
                    block_piece = own_blocks
                else:
                    region = region_fn(a, b, c)
                    block_piece = jnp.take(region, jnp.maximum(slot_codes[:, k], 0), axis=0)
                    present = (slot_codes[:, k] >= 0)[:, None, None, None, None]
                    block_piece = jnp.where(present, block_piece, jnp.zeros((), block_piece.dtype))
                col_parts.append(block_piece)
            row_parts.append(jnp.concatenate(col_parts, axis=3))
        planes.append(jnp.concatenate(row_parts, axis=2))
    return jnp.concatenate(planes, axis=1)


def window(padded_tile, a, b, c):
    capacity = padded_tile.shape[0]
    channels = padded_tile.shape[-1]
    return padded_tile[:, 1 + a : 9 + a, 1 + b : 9 + b, 1 + c : 9 + c].reshape(
        capacity * 512, channels
    )


def convolve(padded_tile, weights):
    total = None
    for k in range(27):
        a, b, c = DIRECTIONS[k]
        term = jnp.dot(window(padded_tile, a, b, c), weights[k], preferred_element_type=jnp.float32)
        total = term if total is None else total + term
    return total


def convolve_adjoint(padded_tile, weights):
    total = None
    for k in range(27):
        a, b, c = DIRECTIONS[k]
        term = lax.dot_general(
            window(padded_tile, -a, -b, -c),
            weights[k],
            (((1,), (1,)), ((), ())),
            preferred_element_type=jnp.float32,
        )
        total = term if total is None else total + term
    return total


def weight_terms(padded_tile, scaled):
    terms = []
    for k in range(27):
        a, b, c = DIRECTIONS[k]
        terms.append(
            lax.dot_general(
                window(padded_tile, a, b, c),
                scaled,
                (((0,), (0,)), ((), ())),
                preferred_element_type=jnp.float32,
            )
        )
    return jnp.stack(terms, axis=0)


def forward_table(own_blocks):
    capacity = own_blocks.shape[0]
    channels = own_blocks.shape[-1]
    sent = own_blocks.reshape(1, 1, capacity, 512, channels)
    received = padded(sent, (("gx", 0), ("gy", 1)), 1)
    return partial(region_of, received.reshape(9 * capacity, 8, 8, 8, channels), False)


def backward_table(own_blocks):
    capacity = own_blocks.shape[0]
    channels = own_blocks.shape[-1]
    sent = own_blocks.reshape(1, 1, capacity, 512, channels)
    received = padded(sent, (("gx", 0), ("gy", 1)), 1)
    return partial(region_of, received.reshape(9 * capacity, 8, 8, 8, channels), False)


def on_device(features, cotangent, neighbours, weights, channel_gain):
    slot_codes = neighbours[0, 0]
    capacity = features.shape[2]
    channels = features.shape[-1]
    occupied = (slot_codes[:, 13] >= 0)[:, None, None]
    own_x = jnp.where(occupied, features[0, 0], jnp.zeros((), features.dtype)).reshape(
        capacity, 8, 8, 8, channels
    )
    regions_x = forward_table(own_x)
    tile_x = assemble(own_x, regions_x, slot_codes)
    conv_out = convolve(tile_x, weights)
    pre_act = own_x.reshape(-1, channels).astype(jnp.float32) + channel_gain * conv_out
    sigmoid_value = jax.nn.sigmoid(pre_act)
    result = (pre_act * sigmoid_value).astype(jnp.bfloat16)
    upstream = (
        jnp.where(occupied, cotangent[0, 0], jnp.zeros((), cotangent.dtype))
        .reshape(-1, channels)
        .astype(jnp.float32)
    )
    pre_grad = upstream * sigmoid_value * (1.0 + pre_act * (1.0 - sigmoid_value))
    scaled = (channel_gain * pre_grad).astype(jnp.bfloat16)
    own_u = scaled.reshape(capacity, 8, 8, 8, channels)
    regions_u = backward_table(own_u)
    tile_u = assemble(own_u, regions_u, slot_codes)
    grad_here = (pre_grad + convolve_adjoint(tile_u, weights)).astype(jnp.bfloat16)
    local_weight = weight_terms(tile_x, scaled)
    local_gain = jnp.sum(pre_grad * conv_out, axis=0)
    weight_grad, gain_grad = lax.psum((local_weight, local_gain), ("gx", "gy"))
    return (
        result.reshape(1, 1, capacity, 512, channels),
        grad_here.reshape(1, 1, capacity, 512, channels),
        weight_grad,
        gain_grad,
    )


def solution(mesh):
    in_specs = (
        P("gx", "gy", None, None, None),
        P("gx", "gy", None, None, None),
        P("gx", "gy", None, None),
        P(),
        P(),
    )
    out_specs = (P("gx", "gy", None, None, None), P("gx", "gy", None, None, None), P(), P())
    return jax.shard_map(
        on_device, mesh=mesh, in_specs=in_specs, out_specs=out_specs, check_vma=False
    )
```

profile of v0, /device:TPU:33, one launch (start us, length us, event | category | flops | bytes accessed | tf_op | source)
XLA Modules:
  0.0 454.4 jit_solution(3340476629180122430)
XLA Ops:
  7.2 1.8 compare_reduce_fusion.25
  9.0 1.0 broadcast_select_fusion.1
  10.1 3.1 collective-permute-start
  13.2 4.3 collective-permute-start.1
  17.5 1.9 maximum_reduce_fusion.8
  19.4 2.5 compare_reduce_fusion.8
  32.0 1.2 maximum_reduce_fusion.6
  49.8 6.0 %collective-permute-start.2 = (bf16[3,1,2,512,128]{4,3,2,1,0:T(8,128)(2,1)S(1)}, bf16[3,1,2,512,128]{4,3,2,1,0:T(8,128)(2,1)S(1)}, u32[]{:S(2)}, u32[]{:S(2)}) collective-permute-start(bf16[3,1,2,512,128]{4,3,2,1,0:T(8,128)(2,1)S(1)} %pad_maximum_fusion.2), channel_id=1, source_target_pairs={{0,1},{1,2},{2,3},{3,4},{4,5},{5,6},{6,7},{8,9},{9,10},{10,11},{11... | collective-permute-start | bytes 2359304 | tf_op jit(solution)/shard_map/ppermute | solution.py:18
  55.8 2.1 collective-permute-start.3
  59.7 9.8 %collective-permute-done.2 = bf16[3,1,2,512,128]{4,3,2,1,0:T(8,128)(2,1)S(1)} collective-permute-done((bf16[3,1,2,512,128]{4,3,2,1,0:T(8,128)(2,1)S(1)}, bf16[3,1,2,512,128]{4,3,2,1,0:T(8,128)(2,1)S(1)}, u32[]{:S(2)}, u32[]{:S(2)}) %collective-permute-start.2) | collective-permute-done | bytes 786464 | tf_op jit(solution)/shard_map/ppermute | solution.py:18
  69.5 4.4 collective-permute-done.3
  74.5 1.2 fusion.182
  88.9 1.2 gather_fusion.8
  99.4 1.5 copy.266
  100.9 1.4 gather_fusion.3
  103.7 1.4 gather_fusion.5
  116.8 1.4 gather_fusion.7
  118.2 1.4 gather_fusion.1
  119.7 1.6 gather_fusion.4
  121.3 1.5 gather_fusion.18
  140.4 0.9 multiply_convert_fusion
  141.3 0.9 fusion.28
  142.2 1.9 collective-permute-start.4
  144.1 6.6 %collective-permute-start.5 = (bf16[1,1,2,512,128]{4,3,2,1,0:T(8,128)(2,1)S(1)}, bf16[1,1,2,512,128]{4,3,2,1,0:T(8,128)(2,1)S(1)}, u32[]{:S(2)}, u32[]{:S(2)}) collective-permute-start(bf16[1,1,2,512,128]{4,3,2,1,0:T(8,128)(2,1)S(1)} %bitcast.837), channel_id=1, source_target_pairs={{8,0},{16,8},{24,16},{32,24},{40,32},{48,40},{56,48},{64,56},{72,6... | collective-permute-start | bytes 786440 | tf_op jit(solution)/shard_map/ppermute | solution.py:19
  150.7 0.9 fusion.27
  151.7 0.9 fusion.26
  152.6 0.9 fusion.25
  153.5 0.9 fusion.24
  154.4 0.9 fusion.23
  155.3 0.9 fusion.22
  156.2 0.9 fusion.21
  157.1 0.9 fusion.20
  158.0 0.9 fusion.19
  160.7 0.9 fusion.16
  163.4 0.9 fusion.13
  164.3 0.9 fusion.12
  165.2 0.9 fusion.11
  166.1 0.9 fusion.10
  167.0 0.9 fusion.9
  167.9 0.9 fusion.8
  168.8 0.9 fusion.7
  169.7 0.9 fusion.6
  170.6 1.0 pad_maximum_fusion.3
  171.5 2.0 collective-permute-start.6
  173.6 2.3 collective-permute-start.7
  175.9 0.9 fusion.5
  176.8 0.9 fusion.4
  177.7 0.9 fusion.3
  178.6 0.9 fusion.2
  179.6 83.4 %psum.15 = f32[128]{0:T(128)} all-reduce(f32[128]{0:T(128)S(1)} %get-tuple-element.64), channel_id=1, replica_groups=mesh['gx'=32,'gy'=8] {'gx','gy'}, use_global_device_ids=true, to_apply=%region_2.10 | all-reduce | flops 128 | bytes 1024 | tf_op jit(solution)/shard_map/psum | solution.py:151
  263.0 1.3 pad_maximum_fusion.1
  264.3 1.2 fusion.178
  266.4 0.9 slice_bitcast_fusion.3
  275.4 1.6 gather_fusion.27
  281.5 1.0 pad_maximum_fusion.8
  283.4 1.0 fusion.188
  286.5 1.4 gather_fusion.35
  291.8 1.4 gather_fusion.50
  293.3 1.4 gather_fusion.41
  294.7 1.6 gather_fusion.38
  300.7 1.4 gather_fusion.44
  317.1 0.9 fusion.1
  318.1 126.6 %all-reduce.2.cloned.1.call-done = f32[27,128,128]{2,1,0:T(8,128)} async-done(((f32[27,128,128]{2,1,0:T(8,128)}), f32[27,128,128]{2,1,0:T(8,128)}) %all-reduce.2.cloned.1.call-update) | async-done | bytes 1769488 | tf_op jit(solution)/shard_map/psum | solution.py:151
  444.6 2.9 copy.308
  (444 shorter events, 124.0 us)
Async XLA Ops:
  7.2 52.5 %copy-start.1 = (bf16[1,1,2,512,128]{4,3,2,1,0:T(8,128)(2,1)S(1)}, bf16[1,1,2,512,128]{4,3,2,1,0:T(8,128)(2,1)}, u32[]{:S(2)}) copy-start(bf16[1,1,2,512,128]{4,3,2,1,0:T(8,128)(2,1)} %param.19) | copy-start | bytes 786436
  7.2 437.5 %all-reduce.2.cloned.1.call-start = ((), (), s32[]{:S(2)}) async-start(), calls=%async_computation | async-start | bytes 3538944 | tf_op jit(solution)/shard_map/psum | solution.py:151
  10.1 39.6 %collective-permute-start = (bf16[1,1,2,512,128]{4,3,2,1,0:T(8,128)(2,1)S(1)}, bf16[1,1,2,512,128]{4,3,2,1,0:T(8,128)(2,1)S(1)}, u32[]{:S(2)}, u32[]{:S(2)}) collective-permute-start(bf16[1,1,2,512,128]{4,3,2,1,0:T(8,128)(2,1)S(1)} %broadcast_select_fusion.1), channel_id=1, source_target_pairs={{0,8},{8,16},{16,24},{24,32},{32,40},{40,48},{48,56},{56,64},{64,7... | collective-permute-start | bytes 786440 | tf_op jit(solution)/shard_map/ppermute | solution.py:18
  13.2 36.5 %collective-permute-start.1 = (bf16[1,1,2,512,128]{4,3,2,1,0:T(8,128)(2,1)S(1)}, bf16[1,1,2,512,128]{4,3,2,1,0:T(8,128)(2,1)S(1)}, u32[]{:S(2)}, u32[]{:S(2)}) collective-permute-start(bf16[1,1,2,512,128]{4,3,2,1,0:T(8,128)(2,1)S(1)} %broadcast_select_fusion.1), channel_id=1, source_target_pairs={{8,0},{16,8},{24,16},{32,24},{40,32},{48,40},{56,48},{64,56},{72,6... | collective-permute-start | bytes 786440 | tf_op jit(solution)/shard_map/ppermute | solution.py:19
  19.4 59.9 %copy-start.45 = (pred[2]{0:T(512)(128)(4,1)}, pred[2]{0:T(512)(128)(4,1)S(1)}, u32[]{:S(2)}) copy-start(pred[2]{0:T(512)(128)(4,1)S(1)} %compare_and_fusion.16) | copy-start | bytes 10
  21.9 57.5 %copy-start.33 = (pred[2]{0:T(512)(128)(4,1)}, pred[2]{0:T(512)(128)(4,1)S(1)}, u32[]{:S(2)}) copy-start(pred[2]{0:T(512)(128)(4,1)S(1)} %get-tuple-element.46) | copy-start | bytes 10
  21.9 58.1 %copy-start.31 = (pred[2]{0:T(512)(128)(4,1)}, pred[2]{0:T(512)(128)(4,1)S(1)}, u32[]{:S(2)}) copy-start(pred[2]{0:T(512)(128)(4,1)S(1)} %get-tuple-element.44) | copy-start | bytes 10
  35.9 42.8 %copy-start.20 = (s32[1024]{0:T(1024)}, s32[1024]{0:T(1024)S(1)}, u32[]{:S(2)}) copy-start(s32[1024]{0:T(1024)S(1)} %pad_clamp_fusion.16) | copy-start | bytes 12292
  35.9 43.5 %copy-start.19 = (s32[1024]{0:T(1024)}, s32[1024]{0:T(1024)S(1)}, u32[]{:S(2)}) copy-start(s32[1024]{0:T(1024)S(1)} %pad_clamp_fusion.14) | copy-start | bytes 12292
  36.6 43.6 %copy-start.18 = (s32[1024]{0:T(1024)}, s32[1024]{0:T(1024)S(1)}, u32[]{:S(2)}) copy-start(s32[1024]{0:T(1024)S(1)} %pad_clamp_fusion.11) | copy-start | bytes 12292
  49.8 19.7 %collective-permute-start.2 = (bf16[3,1,2,512,128]{4,3,2,1,0:T(8,128)(2,1)S(1)}, bf16[3,1,2,512,128]{4,3,2,1,0:T(8,128)(2,1)S(1)}, u32[]{:S(2)}, u32[]{:S(2)}) collective-permute-start(bf16[3,1,2,512,128]{4,3,2,1,0:T(8,128)(2,1)S(1)} %pad_maximum_fusion.2), channel_id=1, source_target_pairs={{0,1},{1,2},{2,3},{3,4},{4,5},{5,6},{6,7},{8,9},{9,10},{10,11},{11... | collective-permute-start | bytes 2359304 | tf_op jit(solution)/shard_map/ppermute | solution.py:18
  55.8 18.0 %collective-permute-start.3 = (bf16[3,1,2,512,128]{4,3,2,1,0:T(8,128)(2,1)S(1)}, bf16[3,1,2,512,128]{4,3,2,1,0:T(8,128)(2,1)S(1)}, u32[]{:S(2)}, u32[]{:S(2)}) collective-permute-start(bf16[3,1,2,512,128]{4,3,2,1,0:T(8,128)(2,1)S(1)} %pad_maximum_fusion.2), channel_id=1, source_target_pairs={{1,0},{2,1},{3,2},{4,3},{5,4},{6,5},{7,6},{9,8},{10,9},{11,10},{12... | collective-permute-start | bytes 2359304 | tf_op jit(solution)/shard_map/ppermute | solution.py:19
  75.8 4.2 copy-start.47
  75.8 4.9 %copy-start.30 = (pred[2]{0:T(512)(128)(4,1)S(1)}, pred[2]{0:T(512)(128)(4,1)}, u32[]{:S(2)}) copy-start(pred[2]{0:T(512)(128)(4,1)} %get-tuple-element.41) | copy-start | bytes 10
  75.8 4.9 %copy-start.43 = (pred[2]{0:T(512)(128)(4,1)S(1)}, pred[2]{0:T(512)(128)(4,1)}, u32[]{:S(2)}) copy-start(pred[2]{0:T(512)(128)(4,1)} %compare_and_fusion.11) | copy-start | bytes 10
  75.8 5.7 %copy-start.29 = (pred[2]{0:T(512)(128)(4,1)S(1)}, pred[2]{0:T(512)(128)(4,1)}, u32[]{:S(2)}) copy-start(pred[2]{0:T(512)(128)(4,1)} %get-tuple-element.39) | copy-start | bytes 10
  75.8 5.7 %copy-start.44 = (pred[2]{0:T(512)(128)(4,1)S(1)}, pred[2]{0:T(512)(128)(4,1)}, u32[]{:S(2)}) copy-start(pred[2]{0:T(512)(128)(4,1)} %compare_and_fusion.9) | copy-start | bytes 10
  87.9 1.0 copy-start.15
  87.9 2.2 copy-start.35
  87.9 14.4 %copy-start.38 = (pred[2]{0:T(512)(128)(4,1)S(1)}, pred[2]{0:T(512)(128)(4,1)}, u32[]{:S(2)}) copy-start(pred[2]{0:T(512)(128)(4,1)} %get-tuple-element.60) | copy-start | bytes 10
  87.9 20.6 %copy-start.12 = (bf16[18,1,1,1,128]{4,3,2,1,0:T(2,128)(2,1)S(1)}, bf16[18,1,1,1,128]{4,3,2,1,0:T(2,128)(2,1)}, u32[]{:S(2)}) copy-start(bf16[18,1,1,1,128]{4,3,2,1,0:T(2,128)(2,1)} %get-tuple-element.100) | copy-start | bytes 13828
  87.9 22.6 %copy-start.11 = (bf16[18,1,1,1,128]{4,3,2,1,0:T(2,128)(2,1)S(1)}, bf16[18,1,1,1,128]{4,3,2,1,0:T(2,128)(2,1)}, u32[]{:S(2)}) copy-start(bf16[18,1,1,1,128]{4,3,2,1,0:T(2,128)(2,1)} %get-tuple-element.98) | copy-start | bytes 13828
  132.7 1.2 copy-start
  138.9 0.7 copy-start.50
  138.9 0.7 copy-start.51
  138.9 1.0 copy-start.52
  142.2 28.4 %collective-permute-start.4 = (bf16[1,1,2,512,128]{4,3,2,1,0:T(8,128)(2,1)S(1)}, bf16[1,1,2,512,128]{4,3,2,1,0:T(8,128)(2,1)S(1)}, u32[]{:S(2)}, u32[]{:S(2)}) collective-permute-start(bf16[1,1,2,512,128]{4,3,2,1,0:T(8,128)(2,1)S(1)} %bitcast.836), channel_id=1, source_target_pairs={{0,8},{8,16},{16,24},{24,32},{32,40},{40,48},{48,56},{56,64},{64,7... | collective-permute-start | bytes 786440 | tf_op jit(solution)/shard_map/ppermute | solution.py:18
  144.1 26.5 %collective-permute-start.5 = (bf16[1,1,2,512,128]{4,3,2,1,0:T(8,128)(2,1)S(1)}, bf16[1,1,2,512,128]{4,3,2,1,0:T(8,128)(2,1)S(1)}, u32[]{:S(2)}, u32[]{:S(2)}) collective-permute-start(bf16[1,1,2,512,128]{4,3,2,1,0:T(8,128)(2,1)S(1)} %bitcast.837), channel_id=1, source_target_pairs={{8,0},{16,8},{24,16},{32,24},{40,32},{48,40},{56,48},{64,56},{72,6... | collective-permute-start | bytes 786440 | tf_op jit(solution)/shard_map/ppermute | solution.py:19
  171.5 91.4 %collective-permute-start.6 = (bf16[3,1,2,512,128]{4,3,2,1,0:T(8,128)(2,1)}, bf16[3,1,2,512,128]{4,3,2,1,0:T(8,128)(2,1)S(1)}, u32[]{:S(2)}, u32[]{:S(2)}) collective-permute-start(bf16[3,1,2,512,128]{4,3,2,1,0:T(8,128)(2,1)} %pad_maximum_fusion.3), channel_id=1, source_target_pairs={{0,1},{1,2},{2,3},{3,4},{4,5},{5,6},{6,7},{8,9},{9,10},{10,11},{11... | collective-permute-start | bytes 2359304 | tf_op jit(solution)/shard_map/ppermute | solution.py:18
  173.6 89.4 %collective-permute-start.7 = (bf16[3,1,2,512,128]{4,3,2,1,0:T(8,128)(2,1)}, bf16[3,1,2,512,128]{4,3,2,1,0:T(8,128)(2,1)}, u32[]{:S(2)}, u32[]{:S(2)}) collective-permute-start(bf16[3,1,2,512,128]{4,3,2,1,0:T(8,128)(2,1)} %pad_maximum_fusion.3), channel_id=1, source_target_pairs={{1,0},{2,1},{3,2},{4,3},{5,4},{6,5},{7,6},{9,8},{10,9},{11,10},{12... | collective-permute-start | bytes 2359304 | tf_op jit(solution)/shard_map/ppermute | solution.py:19
  268.7 3.1 copy-start.23
  268.7 3.1 copy-start.24
  268.7 3.2 copy-start.39
  268.7 3.2 copy-start.40
  269.6 5.7 %copy-start.32 = (pred[2]{0:T(512)(128)(4,1)S(1)}, pred[2]{0:T(512)(128)(4,1)}, u32[]{:S(2)}) copy-start(pred[2]{0:T(512)(128)(4,1)} %copy-done.31) | copy-start | bytes 10
  269.6 5.7 %copy-start.34 = (pred[2]{0:T(512)(128)(4,1)S(1)}, pred[2]{0:T(512)(128)(4,1)}, u32[]{:S(2)}) copy-start(pred[2]{0:T(512)(128)(4,1)} %copy-done.33) | copy-start | bytes 10
  269.6 5.7 %copy-start.46 = (pred[2]{0:T(512)(128)(4,1)S(1)}, pred[2]{0:T(512)(128)(4,1)}, u32[]{:S(2)}) copy-start(pred[2]{0:T(512)(128)(4,1)} %copy-done.45) | copy-start | bytes 10
  269.6 5.7 %copy-start.48 = (pred[2]{0:T(512)(128)(4,1)S(1)}, pred[2]{0:T(512)(128)(4,1)}, u32[]{:S(2)}) copy-start(pred[2]{0:T(512)(128)(4,1)} %compare_and_fusion.14) | copy-start | bytes 10
  270.4 10.4 %copy-start.22 = (pred[2]{0:T(512)(128)(4,1)S(1)}, pred[2]{0:T(512)(128)(4,1)}, u32[]{:S(2)}) copy-start(pred[2]{0:T(512)(128)(4,1)} %get-tuple-element.40) | copy-start | bytes 10
  282.5 1.9 copy-start.14
  282.5 2.6 copy-start.13
  282.5 3.3 copy-start.36
  282.5 3.3 copy-start.37
  282.5 5.5 %copy-start.28 = (pred[2]{0:T(512)(128)(4,1)S(1)}, pred[2]{0:T(512)(128)(4,1)}, u32[]{:S(2)}) copy-start(pred[2]{0:T(512)(128)(4,1)} %get-tuple-element.38) | copy-start | bytes 10
  282.5 5.5 %copy-start.41 = (pred[2]{0:T(512)(128)(4,1)S(1)}, pred[2]{0:T(512)(128)(4,1)}, u32[]{:S(2)}) copy-start(pred[2]{0:T(512)(128)(4,1)} %compare_and_fusion.7) | copy-start | bytes 10
  282.5 5.6 %copy-start.8 = (bf16[18,1,8,1,128]{4,3,2,1,0:T(2,128)(2,1)S(1)}, bf16[18,1,8,1,128]{4,3,2,1,0:T(2,128)(2,1)}, u32[]{:S(2)}) copy-start(bf16[18,1,8,1,128]{4,3,2,1,0:T(2,128)(2,1)} %get-tuple-element.81) | copy-start | bytes 110596
  282.6 6.1 %copy-start.7 = (bf16[18,1,8,1,128]{4,3,2,1,0:T(2,128)(2,1)S(1)}, bf16[18,1,8,1,128]{4,3,2,1,0:T(2,128)(2,1)}, u32[]{:S(2)}) copy-start(bf16[18,1,8,1,128]{4,3,2,1,0:T(2,128)(2,1)} %get-tuple-element.80) | copy-start | bytes 110596
  282.7 6.8 %copy-start.26 = (pred[2]{0:T(512)(128)(4,1)S(1)}, pred[2]{0:T(512)(128)(4,1)}, u32[]{:S(2)}) copy-start(pred[2]{0:T(512)(128)(4,1)} %get-tuple-element.34) | copy-start | bytes 10
  282.7 6.8 %copy-start.27 = (pred[2]{0:T(512)(128)(4,1)S(1)}, pred[2]{0:T(512)(128)(4,1)}, u32[]{:S(2)}) copy-start(pred[2]{0:T(512)(128)(4,1)} %get-tuple-element.36) | copy-start | bytes 10
  282.7 6.8 %copy-start.42 = (pred[2]{0:T(512)(128)(4,1)S(1)}, pred[2]{0:T(512)(128)(4,1)}, u32[]{:S(2)}) copy-start(pred[2]{0:T(512)(128)(4,1)} %compare_and_fusion.5) | copy-start | bytes 10
  282.7 6.8 %copy-start.49 = (pred[2]{0:T(512)(128)(4,1)S(1)}, pred[2]{0:T(512)(128)(4,1)}, u32[]{:S(2)}) copy-start(pred[2]{0:T(512)(128)(4,1)} %compare_and_fusion.3) | copy-start | bytes 10
  282.7 7.0 %copy-start.10 = (bf16[18,1,1,1,128]{4,3,2,1,0:T(2,128)(2,1)S(1)}, bf16[18,1,1,1,128]{4,3,2,1,0:T(2,128)(2,1)}, u32[]{:S(2)}) copy-start(bf16[18,1,1,1,128]{4,3,2,1,0:T(2,128)(2,1)} %get-tuple-element.69) | copy-start | bytes 13828
  282.7 7.6 %copy-start.9 = (bf16[18,1,1,1,128]{4,3,2,1,0:T(2,128)(2,1)S(1)}, bf16[18,1,1,1,128]{4,3,2,1,0:T(2,128)(2,1)}, u32[]{:S(2)}) copy-start(bf16[18,1,1,1,128]{4,3,2,1,0:T(2,128)(2,1)} %get-tuple-element.68) | copy-start | bytes 13828
  282.7 13.7 %copy-start.21 = (pred[2]{0:T(512)(128)(4,1)S(1)}, pred[2]{0:T(512)(128)(4,1)}, u32[]{:S(2)}) copy-start(pred[2]{0:T(512)(128)(4,1)} %get-tuple-element.35) | copy-start | bytes 10
  282.7 16.5 %copy-start.16 = (bf16[18,1,1,1,128]{4,3,2,1,0:T(2,128)(2,1)S(1)}, bf16[18,1,1,1,128]{4,3,2,1,0:T(2,128)(2,1)}, u32[]{:S(2)}) copy-start(bf16[18,1,1,1,128]{4,3,2,1,0:T(2,128)(2,1)} %get-tuple-element.67) | copy-start | bytes 13828
  282.7 16.5 %copy-start.17 = (bf16[18,1,1,1,128]{4,3,2,1,0:T(2,128)(2,1)S(1)}, bf16[18,1,1,1,128]{4,3,2,1,0:T(2,128)(2,1)}, u32[]{:S(2)}) copy-start(bf16[18,1,1,1,128]{4,3,2,1,0:T(2,128)(2,1)} %get-tuple-element.72) | copy-start | bytes 13828
  282.7 20.1 %copy-start.6 = (bf16[18,1,8,1,128]{4,3,2,1,0:T(2,128)(2,1)S(1)}, bf16[18,1,8,1,128]{4,3,2,1,0:T(2,128)(2,1)}, u32[]{:S(2)}) copy-start(bf16[18,1,8,1,128]{4,3,2,1,0:T(2,128)(2,1)} %get-tuple-element.82) | copy-start | bytes 110596
  282.8 24.4 %copy-start.25 = (pred[2]{0:T(512)(128)(4,1)S(1)}, pred[2]{0:T(512)(128)(4,1)}, u32[]{:S(2)}) copy-start(pred[2]{0:T(512)(128)(4,1)} %get-tuple-element.59) | copy-start | bytes 10
  311.3 1.0 copy-start.5
  311.5 1.0 copy-start.4
  311.8 1.0 copy-start.3
  312.2 1.0 copy-start.2
Sparse Core Ops, SparseCore 0:
  179.7 264.9 all-reduce.1
where the time goes:
time: 460 us; the launch traced here: 454 us
  waiting for transfers between devices  141 us (31%)
  blocking collectives  83.4 us (18%)
  local copies, waits for them, and re-layouts  76.8 us (17%)
  other arithmetic  72.2 us (16%)
  matrix products  37.1 us (8%)
  starting transfers between devices  28.5 us (6%)
  between operations  15.7 us (3%)
    psum x1, waiting for transfers between devices, on_device(): weight_grad, gain_grad = lax.psum((local_weight, local_gain), ('gx', 'gy'))  127 us
    psum x1, blocking collectives, on_device(): weight_grad, gain_grad = lax.psum((local_weight, local_gain), ('gx', 'gy'))  83.4 us
    gather x52, local copies, waits for them, and re-layouts, assemble(): block_piece = jnp.take(region, jnp.maximum(slot_codes[:, k], 0), axis=0)  45.4 us
    select_n x42, other arithmetic, assemble(): jnp.where(present, block_piece, jnp.zeros((), block_piece.dtype))  25.5 us
    dot_general x27, matrix products, weight_terms(): lax.dot_general(window(padded_tile, a, b, c), scaled, (((0,), (0,)), ((),...  24.3 us
    ppermute x4, starting transfers between devices, padded(): after = lax.ppermute(leading, axis, down)  15.4 us
    and x26, other arithmetic, assemble(): block_piece = jnp.take(region, jnp.maximum(slot_codes[:, k], 0), axis=0)  13.8 us
    gather x26, other arithmetic  13.7 us
  transfers between devices with their start and end apart: 9, of which 3 were waited for; matrix products, arithmetic and copies ran while one was open for 24% of the time, Pallas kernels for 0%

commit v1 on v0

v1 whole, which is shorter than its diff:
```python
import jax
import jax.numpy as jnp
from jax import lax
from jax.experimental import pallas as pl
from jax.experimental.pallas import tpu as pltpu
from jax.sharding import PartitionSpec as P

C = 128
CAP = 2
SIDE = (-1, 0, 1)
EMPTY = 9 * CAP
VMEM = pltpu.VMEM
f32 = jnp.float32
bf16 = jnp.bfloat16


def rim(d):
    return {-1: (7, 1), 0: (0, 8), 1: (0, 1)}[d]


def place(d):
    return {-1: (0, 1), 0: (1, 8), 1: (9, 1)}[d]


def write_rims(value, out):
    x_low, x_high, y_low, y_high, edge_ll, edge_lh, edge_hl, edge_hh = out
    for ref, x in ((x_low, 0), (x_high, 7)):
        ref[...] = value[:, x].reshape(CAP * 64, C).astype(bf16)
    for ref, y in ((y_low, 0), (y_high, 7)):
        ref[...] = value[:, :, y].reshape(CAP * 64, C).astype(bf16)
    for ref, x, y in ((edge_ll, 0, 0), (edge_lh, 0, 7), (edge_hl, 7, 0), (edge_hh, 7, 7)):
        ref[...] = value[:, x, y].reshape(CAP * 8, C).astype(bf16)


def rim_shapes():
    return [jax.ShapeDtypeStruct((CAP * 64, C), bf16)] * 4 + [jax.ShapeDtypeStruct((CAP * 8, C), bf16)] * 4


def rims_kernel(x_ref, *out):
    write_rims(x_ref[...].astype(f32).reshape(CAP, 8, 8, 8, C), out)


def rims_of(x):
    return pl.pallas_call(
        rims_kernel,
        out_shape=rim_shapes(),
        in_specs=[pl.BlockSpec(memory_space=VMEM)],
        out_specs=[pl.BlockSpec(memory_space=VMEM)] * 8,
    )(x)


def exchange(rims):
    x_low, x_high, y_low, y_high, edge_ll, edge_lh, edge_hl, edge_hh = rims
    nx, ny = lax.axis_size("gx"), lax.axis_size("gy")

    def shift(value, dx, dy):
        pairs = []
        for i in range(nx):
            for j in range(ny):
                if 0 <= i + dx < nx and 0 <= j + dy < ny:
                    pairs.append((i * ny + j, (i + dx) * ny + j + dy))
        return lax.ppermute(value, ("gx", "gy"), pairs)

    return (
        shift(x_high, 1, 0),
        shift(x_low, -1, 0),
        shift(y_high, 0, 1),
        shift(y_low, 0, -1),
        shift(edge_hh, 1, 1),
        shift(edge_hl, 1, -1),
        shift(edge_lh, -1, 1),
        shift(edge_ll, -1, -1),
    )


def fill_table(table, own, halo):
    from_xm, from_xp, from_ym, from_yp, from_mm, from_mp, from_pm, from_pp = halo
    table[4 * CAP : 5 * CAP] = own.astype(f32).reshape(CAP, 8, 64, C)
    table[EMPTY] = jnp.zeros((8, 64, C), f32)
    for ref, device, x in ((from_xm, 1, 7), (from_xp, 7, 0)):
        table[device * CAP : (device + 1) * CAP, x] = ref[...].astype(f32).reshape(CAP, 64, C)
    for ref, device, y in ((from_ym, 3, 7), (from_yp, 5, 0)):
        table[device * CAP : (device + 1) * CAP, :, 8 * y : 8 * y + 8] = ref[...].astype(f32).reshape(CAP, 8, 8, C)
    for ref, device, x, y in ((from_mm, 0, 7, 7), (from_mp, 2, 7, 0), (from_pm, 6, 0, 7), (from_pp, 8, 0, 0)):
        table[device * CAP : (device + 1) * CAP, x, 8 * y : 8 * y + 8] = ref[...].astype(f32).reshape(CAP, 8, C)


def unfold(codes, table, planes, unfolded):
    height = lax.broadcasted_iota(jnp.int32, (1, 8, C), 1)
    for s in range(CAP):
        for a in SIDE:
            for b in SIDE:
                (xs, nx), (ys, ny) = rim(a), rim(b)
                (xd, _), (yd, _) = place(a), place(b)
                parts = []
                for c in SIDE:
                    code = codes[s, 9 * (a + 1) + 3 * (b + 1) + (c + 1)]
                    code = jnp.where(code < 0, EMPTY, code)
                    part = table[code, xs : xs + nx, 8 * ys : 8 * (ys + ny), :]
                    parts.append(part.reshape(nx * ny, 8, C))
                below, here, above = parts
                down = pltpu.roll(jnp.where(height == 7, below, here), 1, 1)
                up = pltpu.roll(jnp.where(height == 0, above, here), 7, 1)
                for i, part in enumerate((down, here, up)):
                    planes[i, xd : xd + nx, 8 * yd : 8 * (yd + ny), :] = part.reshape(nx, ny * 8, C)
        for b in SIDE:
            for c in SIDE:
                at = C * (3 * (b + 1) + (c + 1))
                unfolded[s, :, :, at : at + C] = planes[c + 1, :, 8 * (1 + b) : 8 * (1 + b) + 64, :].astype(bf16)


def forward_kernel(codes, x_ref, dy_ref, w_ref, gain_ref, *refs):
    halo, refs = refs[:8], refs[8:]
    out_ref, pre_grad_ref, scaled_ref, terms_ref = refs[:4]
    rim_refs, refs = refs[4:12], refs[12:]
    table, planes, unfolded, shifted = refs
    fill_table(table, x_ref[...], halo)
    unfold(codes, table, planes, unfolded)
    gain = gain_ref[...]
    gain_sum = jnp.zeros((1, C), f32)
    rim_values = []
    for s in range(CAP):
        conv = jnp.zeros((512, C), f32)
        for a in range(3):
            conv = conv + jnp.dot(
                unfolded[s, a : a + 8].reshape(512, 9 * C), w_ref[a], preferred_element_type=f32
            )
        occupied = codes[s, 13] >= 0
        own = jnp.where(occupied, x_ref[s].astype(f32), 0.0)
        upstream = jnp.where(occupied, dy_ref[s].astype(f32), 0.0)
        pre_act = own + gain * conv
        sig = jax.nn.sigmoid(pre_act)
        out_ref[s] = (pre_act * sig).astype(bf16)
        pre_grad = upstream * sig * (1.0 + pre_act * (1.0 - sig))
        pre_grad_ref[s] = pre_grad
        scaled = (gain * pre_grad).astype(bf16)
        scaled_ref[s] = scaled
        rim_values.append(scaled.astype(f32).reshape(1, 8, 8, 8, C))
        gain_sum = gain_sum + jnp.sum(pre_grad * conv, axis=0, keepdims=True)
        for a in range(3):
            at = C * a
            shifted[s, a : a + 8, :, at : at + C] = scaled.reshape(8, 64, C)
            for x in range(10):
                if not a <= x < a + 8:
                    shifted[s, x, :, at : at + C] = jnp.zeros((64, C), bf16)
    write_rims(jnp.concatenate(rim_values, axis=0), rim_refs)
    rhs = shifted[...].reshape(CAP * 640, 3 * C)
    for bc in range(9):
        lhs = unfolded[:, :, :, C * bc : C * bc + C].reshape(CAP * 640, C)
        term = lax.dot_general(lhs, rhs, (((0,), (0,)), ((), ())), preferred_element_type=f32)
        for a in range(3):
            terms_ref[9 * a + bc] = term[:, C * a : C * a + C]
    terms_ref[27] = jnp.concatenate([gain_sum, jnp.zeros((C - 1, C), f32)], axis=0)


def forward(codes, x, dy, weights, gain, halo):
    block = jax.ShapeDtypeStruct((CAP, 512, C), bf16)
    vmem = pl.BlockSpec(memory_space=VMEM)
    return pl.pallas_call(
        forward_kernel,
        out_shape=[
            block,
            jax.ShapeDtypeStruct((CAP, 512, C), f32),
            block,
            jax.ShapeDtypeStruct((28, C, C), f32),
            *rim_shapes(),
        ],
        in_specs=[pl.BlockSpec(memory_space=pltpu.SMEM)] + [vmem] * 12,
        out_specs=[vmem] * 12,
        scratch_shapes=[
            VMEM((EMPTY + 1, 8, 64, C), f32),
            VMEM((3, 10, 80, C), f32),
            VMEM((CAP, 10, 64, 9 * C), bf16),
            VMEM((CAP, 10, 64, 3 * C), bf16),
        ],
        compiler_params=pltpu.CompilerParams(vmem_limit_bytes=40 * 2**20),
    )(codes, x, dy, weights, gain, *halo)


def backward_kernel(codes, scaled_ref, w_ref, pre_grad_ref, *refs):
    halo, (grad_ref, table, planes, unfolded) = refs[:8], refs[8:]
    fill_table(table, scaled_ref[...], halo)
    unfold(codes, table, planes, unfolded)
    for s in range(CAP):
        total = pre_grad_ref[s]
        for a in range(3):
            total = total + jnp.dot(
                unfolded[s, a : a + 8].reshape(512, 9 * C), w_ref[a], preferred_element_type=f32
            )
        grad_ref[s] = total.astype(bf16)


def backward(codes, scaled, weights, pre_grad, halo):
    vmem = pl.BlockSpec(memory_space=VMEM)
    return pl.pallas_call(
        backward_kernel,
        out_shape=jax.ShapeDtypeStruct((CAP, 512, C), bf16),
        in_specs=[pl.BlockSpec(memory_space=pltpu.SMEM)] + [vmem] * 11,
        out_specs=vmem,
        scratch_shapes=[
            VMEM((EMPTY + 1, 8, 64, C), f32),
            VMEM((3, 10, 80, C), f32),
            VMEM((CAP, 10, 64, 9 * C), bf16),
        ],
        compiler_params=pltpu.CompilerParams(vmem_limit_bytes=40 * 2**20),
    )(codes, scaled, weights, pre_grad, *halo)


def on_device(features, cotangent, neighbours, weights, channel_gain):
    codes = neighbours[0, 0]
    x = features[0, 0]
    dy = cotangent[0, 0]
    halo = exchange(rims_of(x))
    result, pre_grad, scaled, terms, *rims = forward(
        codes, x, dy, weights.reshape(3, 9 * C, C), channel_gain.reshape(1, C), halo
    )
    adjoint = jnp.swapaxes(weights[::-1], 1, 2).reshape(3, 9 * C, C)
    grad = backward(codes, scaled, adjoint, pre_grad, exchange(rims))
    total = lax.psum(terms, ("gx", "gy"))
    return (result[None, None], grad[None, None], total[:27], total[27, 0])


def solution(mesh):
    split = P("gx", "gy", None, None, None)
    return jax.shard_map(
        on_device,
        mesh=mesh,
        in_specs=(split, split, P("gx", "gy", None, None), P(), P()),
        out_specs=(split, split, P(), P()),
        check_vma=False,
    )
```

time: 460 us -> 342 us (0.74)
  waiting for transfers between devices: 141 us -> 247 us
  blocking collectives: 83.4 us -> 0 us
  other arithmetic: 72.2 us -> 0 us
  local copies, waits for them, and re-layouts: 76.8 us -> 9.87 us
  matrix products: 37.1 us -> 0 us
  starting transfers between devices: 28.5 us -> 57.3 us
  Pallas kernels: 0 us -> 10.8 us
    psum x1, waiting for transfers between devices: 127 us -> 225 us  [on_device(): total = lax.psum(terms, ('gx', 'gy'))]
    psum x1 -> x0, blocking collectives: 83.4 us -> none  [on_device(): weight_grad, gain_grad = lax.psum((local_weight, local_gain), ('gx', 'gy'))]
    gather x52 -> x0, local copies, waits for them, and re-layouts: 45.4 us -> none  [assemble(): block_piece = jnp.take(region, jnp.maximum(slot_codes[:, k], 0), axis=0)]
    dot_general x81 -> x0, matrix products: 37.1 us -> none  [the longest x27 24.3 us: weight_terms(): lax.dot_general(window(padded_tile, a, b, c), scaled, (((0,), (0,)), ((),...]
    ppermute x8 -> x16, starting transfers between devices: 28.4 us -> 57.2 us  [shift(): return lax.ppermute(value, ('gx', 'gy'), pairs)]
    select_n x70 -> x0, other arithmetic: 26.7 us -> none  [the longest x42 25.5 us: assemble(): jnp.where(present, block_piece, jnp.zeros((), block_piece.dtype))]
    and x26 -> x0, other arithmetic: 13.8 us -> none  [assemble(): block_piece = jnp.take(region, jnp.maximum(slot_codes[:, k], 0), axis=0)]
    gather x26 -> x0, other arithmetic: 13.7 us -> none
  transfers between devices with their start and end apart: 9 -> 17, of which waited for: 3 -> 6; matrix products, arithmetic and copies ran while one was open for 24% -> 0% of each run, Pallas kernels for 0% -> 1%
where the time goes in v1:
time: 342 us; the launch traced here: 339 us
  waiting for transfers between devices  247 us (72%)
  starting transfers between devices  57.3 us (17%)
  between operations  14.3 us (4%)
  Pallas kernels  10.8 us (3%)
  local copies, waits for them, and re-layouts  9.87 us (3%)
    psum x1, waiting for transfers between devices, on_device(): total = lax.psum(terms, ('gx', 'gy'))  225 us
    ppermute x16, starting transfers between devices, shift(): return lax.ppermute(value, ('gx', 'gy'), pairs)  57.2 us
    ppermute x16, waiting for transfers between devices, shift(): return lax.ppermute(value, ('gx', 'gy'), pairs)  21.8 us
  transfers between devices with their start and end apart: 17, of which 6 were waited for; matrix products, arithmetic and copies ran while one was open for 0% of the time, Pallas kernels for 1%

profile of v1, /device:TPU:33, one launch (start us, length us, event | category | flops | bytes accessed | tf_op | source)
XLA Modules:
  0.0 339.4 jit_solution(5216504437819558856)
XLA Ops:
  7.2 0.0 all-reduce.2.cloned.1.call-start
  7.2 1.6 shard_map.84
  8.8 3.1 collective-permute-start
  12.0 4.3 %collective-permute-start.1 = (bf16[128,128]{1,0:T(8,128)(2,1)}, bf16[128,128]{1,0:T(8,128)(2,1)S(1)}, u32[]{:S(2)}, u32[]{:S(2)}) collective-permute-start(bf16[128,128]{1,0:T(8,128)(2,1)} %get-tuple-element.25), channel_id=1, source_target_pairs={{8,0},{9,1},{10,2},{11,3},{12,4},{13,5},{14,6},{15,7},{16,8},{17,9... | collective-permute-start | bytes 98312 | tf_op jit(solution)/shard_map/ppermute | solution.py:62
  16.2 6.0 %collective-permute-start.2 = (bf16[128,128]{1,0:T(8,128)(2,1)}, bf16[128,128]{1,0:T(8,128)(2,1)S(1)}, u32[]{:S(2)}, u32[]{:S(2)}) collective-permute-start(bf16[128,128]{1,0:T(8,128)(2,1)} %get-tuple-element.26), channel_id=1, source_target_pairs={{0,1},{1,2},{2,3},{3,4},{4,5},{5,6},{6,7},{8,9},{9,10},{10,11},{11... | collective-permute-start | bytes 98312 | tf_op jit(solution)/shard_map/ppermute | solution.py:62
  22.3 1.9 collective-permute-start.3
  24.2 3.4 collective-permute-start.4
  27.6 3.9 %collective-permute-done.4.refs_4_ = bf16[16,128]{1,0:T(8,128)(2,1)S(1)} collective-permute-done((bf16[16,128]{1,0:T(8,128)(2,1)}, bf16[16,128]{1,0:T(8,128)(2,1)S(1)}, u32[]{:S(2)}, u32[]{:S(2)}) %collective-permute-start.4) | collective-permute-done | bytes 4128 | tf_op jit(solution)/shard_map/ppermute | solution.py:62
  31.4 1.9 collective-permute-start.5
  33.4 5.3 %collective-permute-done.5.refs_5_ = bf16[16,128]{1,0:T(8,128)(2,1)S(1)} collective-permute-done((bf16[16,128]{1,0:T(8,128)(2,1)}, bf16[16,128]{1,0:T(8,128)(2,1)S(1)}, u32[]{:S(2)}, u32[]{:S(2)}) %collective-permute-start.5) | collective-permute-done | bytes 4128 | tf_op jit(solution)/shard_map/ppermute | solution.py:62
  38.7 1.9 collective-permute-start.6
  40.6 3.2 collective-permute-done.6.refs_6_
  43.8 1.9 collective-permute-start.7
  45.7 6.0 %collective-permute-done.7.refs_7_ = bf16[16,128]{1,0:T(8,128)(2,1)S(1)} collective-permute-done((bf16[16,128]{1,0:T(8,128)(2,1)}, bf16[16,128]{1,0:T(8,128)(2,1)S(1)}, u32[]{:S(2)}, u32[]{:S(2)}) %collective-permute-start.7) | collective-permute-done | bytes 4128 | tf_op jit(solution)/shard_map/ppermute | solution.py:62
  51.8 0.0 collective-permute-done.refs_0_
  51.8 0.0 collective-permute-done.1.refs_1_
  51.8 0.0 collective-permute-done.2.refs_2_
  51.8 0.0 collective-permute-done.3.refs_3_
  51.8 0.0 copy-start
  51.8 1.2 copy-done
  53.0 0.0 copy-start.2
  53.0 0.9 copy-done.2
  53.9 0.0 copy-start.3
  53.9 0.9 copy-done.3
  54.9 0.0 copy-start.4
  54.9 0.7 copy-done.4
  55.5 0.0 copy-start.6
  55.5 0.7 copy-done.6
  56.2 0.0 copy-start.1
  56.2 5.7 %shard_map.85 = (bf16[2,512,128]{2,1,0:T(8,128)(2,1)}, f32[2,512,128]{2,1,0:T(8,128)S(1)}, bf16[2,512,128]{2,1,0:T(8,128)(2,1)S(1)}, f32[28,128,128]{2,1,0:T(8,1...) custom-call(s32[2,27]{1,0:T(2,128)S(1)} %bitcast.17, ...), custom_call_target="tpu_custom_call" | custom-call | tf_op jit(solution)/shard_map/pallas_call | solution.py:159
  61.9 0.0 all-reduce.2.cloned.1.call-update
  61.9 0.0 copy-start.5
  61.9 3.6 %collective-permute-start.12 = (bf16[16,128]{1,0:T(8,128)(2,1)S(1)}, bf16[16,128]{1,0:T(8,128)(2,1)S(1)}, u32[]{:S(2)}, u32[]{:S(2)}) collective-permute-start(bf16[16,128]{1,0:T(8,128)(2,1)S(1)} %get-tuple-element.39), channel_id=1, source_target_pairs={{0,9},{1,10},{2,11},{3,12},{4,13},{5,14},{6,15},{8,17},{9,18},{10,... | collective-permute-start | bytes 12296 | tf_op jit(solution)/shard_map/ppermute | solution.py:62
  65.6 4.8 %collective-permute-start.13 = (bf16[16,128]{1,0:T(8,128)(2,1)S(1)}, bf16[16,128]{1,0:T(8,128)(2,1)S(1)}, u32[]{:S(2)}, u32[]{:S(2)}) collective-permute-start(bf16[16,128]{1,0:T(8,128)(2,1)S(1)} %get-tuple-element.40), channel_id=1, source_target_pairs={{1,8},{2,9},{3,10},{4,11},{5,12},{6,13},{7,14},{9,16},{10,17},{11,... | collective-permute-start | bytes 12296 | tf_op jit(solution)/shard_map/ppermute | solution.py:62
  70.5 5.2 %collective-permute-start.14 = (bf16[16,128]{1,0:T(8,128)(2,1)S(1)}, bf16[16,128]{1,0:T(8,128)(2,1)S(1)}, u32[]{:S(2)}, u32[]{:S(2)}) collective-permute-start(bf16[16,128]{1,0:T(8,128)(2,1)S(1)} %get-tuple-element.41), channel_id=1, source_target_pairs={{8,1},{9,2},{10,3},{11,4},{12,5},{13,6},{14,7},{16,9},{17,10},{18,... | collective-permute-start | bytes 12296 | tf_op jit(solution)/shard_map/ppermute | solution.py:62
  75.7 7.9 %collective-permute-start.10 = (bf16[128,128]{1,0:T(8,128)(2,1)S(1)}, bf16[128,128]{1,0:T(8,128)(2,1)S(1)}, u32[]{:S(2)}, u32[]{:S(2)}) collective-permute-start(bf16[128,128]{1,0:T(8,128)(2,1)S(1)} %get-tuple-element.37), channel_id=1, source_target_pairs={{0,1},{1,2},{2,3},{3,4},{4,5},{5,6},{6,7},{8,9},{9,10},{10,11},{11... | collective-permute-start | bytes 98312 | tf_op jit(solution)/shard_map/ppermute | solution.py:62
  83.5 1.9 collective-permute-start.11
  85.4 0.0 collective-permute-done.12.refs_4_
  85.5 1.9 collective-permute-start.8
  87.4 0.0 collective-permute-done.13.refs_5_
  87.4 5.5 %collective-permute-start.9 = (bf16[128,128]{1,0:T(8,128)(2,1)S(1)}, bf16[128,128]{1,0:T(8,128)(2,1)S(1)}, u32[]{:S(2)}, u32[]{:S(2)}) collective-permute-start(bf16[128,128]{1,0:T(8,128)(2,1)S(1)} %get-tuple-element.36), channel_id=1, source_target_pairs={{8,0},{9,1},{10,2},{11,3},{12,4},{13,5},{14,6},{15,7},{16,8},{17,9... | collective-permute-start | bytes 98312 | tf_op jit(solution)/shard_map/ppermute | solution.py:62
  92.9 0.0 collective-permute-done.14.refs_6_
  92.9 1.9 collective-permute-start.15
  94.8 0.0 copy-done.1
  94.8 0.1 reverse_bitcast_fusion
  94.9 1.3 copy.9
  96.2 3.4 collective-permute-done.15.refs_7_
  99.6 0.0 collective-permute-done.10.refs_2_
  99.6 0.0 collective-permute-done.11.refs_3_
  99.6 0.0 collective-permute-done.8.refs_0_
  99.6 0.0 collective-permute-done.9.refs_1_
  99.6 0.0 copy-done.5
  99.6 3.4 %shard_map.86 = bf16[2,512,128]{2,1,0:T(8,128)(2,1)} custom-call(s32[2,27]{1,0:T(2,128)S(1)} %bitcast.18, bf16[2,512,128]{2,1,0:T(8,128)(2,1)S(1)} %get-tuple-element.33.scaled_ref, bf16[3,1152,128]{2,1,0:T(8,128)(2,1)S(1)} %bitcast.13, f32[2,512,128]{2,1,0:T(8,128)S(1)} %get-tuple-element.34.pre_grad_ref, ...), custom_call_target="tpu_custom_call" | custom-call | tf_op jit(solution)/shard_map/pallas_call | solution.py:195
  103.0 225.5 %all-reduce.2.cloned.1.call-done = f32[28,128,128]{2,1,0:T(8,128)} async-done(((f32[28,128,128]{2,1,0:T(8,128)}), f32[28,128,128]{2,1,0:T(8,128)}) %all-reduce.2.cloned.1.call-update) | async-done | bytes 1835024 | tf_op jit(solution)/shard_map/psum | solution.py:219
  328.5 2.9 slice.8
  331.4 1.2 slice_bitcast_fusion
Async XLA Ops:
  7.2 321.3 %all-reduce.2.cloned.1.call-start = ((), (), s32[]{:S(2)}) async-start(), calls=%async_computation | async-start | bytes 3670016 | tf_op jit(solution)/shard_map/psum | solution.py:219
  8.8 42.9 %collective-permute-start = (bf16[128,128]{1,0:T(8,128)(2,1)}, bf16[128,128]{1,0:T(8,128)(2,1)S(1)}, u32[]{:S(2)}, u32[]{:S(2)}) collective-permute-start(bf16[128,128]{1,0:T(8,128)(2,1)} %get-tuple-element.24), channel_id=1, source_target_pairs={{0,8},{1,9},{2,10},{3,11},{4,12},{5,13},{6,14},{7,15},{8,16},{9,17... | collective-permute-start | bytes 98312 | tf_op jit(solution)/shard_map/ppermute | solution.py:62
  12.0 39.8 %collective-permute-start.1 = (bf16[128,128]{1,0:T(8,128)(2,1)}, bf16[128,128]{1,0:T(8,128)(2,1)S(1)}, u32[]{:S(2)}, u32[]{:S(2)}) collective-permute-start(bf16[128,128]{1,0:T(8,128)(2,1)} %get-tuple-element.25), channel_id=1, source_target_pairs={{8,0},{9,1},{10,2},{11,3},{12,4},{13,5},{14,6},{15,7},{16,8},{17,9... | collective-permute-start | bytes 98312 | tf_op jit(solution)/shard_map/ppermute | solution.py:62
  16.2 35.5 %collective-permute-start.2 = (bf16[128,128]{1,0:T(8,128)(2,1)}, bf16[128,128]{1,0:T(8,128)(2,1)S(1)}, u32[]{:S(2)}, u32[]{:S(2)}) collective-permute-start(bf16[128,128]{1,0:T(8,128)(2,1)} %get-tuple-element.26), channel_id=1, source_target_pairs={{0,1},{1,2},{2,3},{3,4},{4,5},{5,6},{6,7},{8,9},{9,10},{10,11},{11... | collective-permute-start | bytes 98312 | tf_op jit(solution)/shard_map/ppermute | solution.py:62
  22.3 29.5 %collective-permute-start.3 = (bf16[128,128]{1,0:T(8,128)(2,1)}, bf16[128,128]{1,0:T(8,128)(2,1)S(1)}, u32[]{:S(2)}, u32[]{:S(2)}) collective-permute-start(bf16[128,128]{1,0:T(8,128)(2,1)} %get-tuple-element.27), channel_id=1, source_target_pairs={{1,0},{2,1},{3,2},{4,3},{5,4},{6,5},{7,6},{9,8},{10,9},{11,10},{12... | collective-permute-start | bytes 98312 | tf_op jit(solution)/shard_map/ppermute | solution.py:62
  24.2 7.2 %collective-permute-start.4 = (bf16[16,128]{1,0:T(8,128)(2,1)}, bf16[16,128]{1,0:T(8,128)(2,1)S(1)}, u32[]{:S(2)}, u32[]{:S(2)}) collective-permute-start(bf16[16,128]{1,0:T(8,128)(2,1)} %get-tuple-element.28), channel_id=1, source_target_pairs={{0,9},{1,10},{2,11},{3,12},{4,13},{5,14},{6,15},{8,17},{9,18},{10,... | collective-permute-start | bytes 12296 | tf_op jit(solution)/shard_map/ppermute | solution.py:62
  31.4 7.2 %collective-permute-start.5 = (bf16[16,128]{1,0:T(8,128)(2,1)}, bf16[16,128]{1,0:T(8,128)(2,1)S(1)}, u32[]{:S(2)}, u32[]{:S(2)}) collective-permute-start(bf16[16,128]{1,0:T(8,128)(2,1)} %get-tuple-element.29), channel_id=1, source_target_pairs={{1,8},{2,9},{3,10},{4,11},{5,12},{6,13},{7,14},{9,16},{10,17},{11,... | collective-permute-start | bytes 12296 | tf_op jit(solution)/shard_map/ppermute | solution.py:62
  38.7 5.1 %collective-permute-start.6 = (bf16[16,128]{1,0:T(8,128)(2,1)}, bf16[16,128]{1,0:T(8,128)(2,1)S(1)}, u32[]{:S(2)}, u32[]{:S(2)}) collective-permute-start(bf16[16,128]{1,0:T(8,128)(2,1)} %get-tuple-element.30), channel_id=1, source_target_pairs={{8,1},{9,2},{10,3},{11,4},{12,5},{13,6},{14,7},{16,9},{17,10},{18,... | collective-permute-start | bytes 12296 | tf_op jit(solution)/shard_map/ppermute | solution.py:62
  43.8 8.0 %collective-permute-start.7 = (bf16[16,128]{1,0:T(8,128)(2,1)}, bf16[16,128]{1,0:T(8,128)(2,1)S(1)}, u32[]{:S(2)}, u32[]{:S(2)}) collective-permute-start(bf16[16,128]{1,0:T(8,128)(2,1)} %get-tuple-element.31), channel_id=1, source_target_pairs={{9,0},{10,1},{11,2},{12,3},{13,4},{14,5},{15,6},{17,8},{18,9},{19,... | collective-permute-start | bytes 12296 | tf_op jit(solution)/shard_map/ppermute | solution.py:62
  51.8 1.2 copy-start
  53.0 0.9 copy-start.2
  53.9 0.9 copy-start.3
  54.9 0.7 copy-start.4
  55.5 0.7 copy-start.6
  56.2 38.6 %copy-start.1 = (bf16[27,128,128]{2,1,0:T(8,128)(2,1)S(1)}, bf16[27,128,128]{2,1,0:T(8,128)(2,1)}, u32[]{:S(2)}) copy-start(bf16[27,128,128]{2,1,0:T(8,128)(2,1)} %param.8) | copy-start | bytes 2654212
  61.9 37.7 %copy-start.5 = (s32[1,1,2,27]{3,2,1,0:T(2,128)S(1)}, s32[1,1,2,27]{3,2,1,0:T(2,128)}, u32[]{:S(2)}) copy-start(s32[1,1,2,27]{3,2,1,0:T(2,128)} %param.7) | copy-start | bytes 652
  61.9 23.5 %collective-permute-start.12 = (bf16[16,128]{1,0:T(8,128)(2,1)S(1)}, bf16[16,128]{1,0:T(8,128)(2,1)S(1)}, u32[]{:S(2)}, u32[]{:S(2)}) collective-permute-start(bf16[16,128]{1,0:T(8,128)(2,1)S(1)} %get-tuple-element.39), channel_id=1, source_target_pairs={{0,9},{1,10},{2,11},{3,12},{4,13},{5,14},{6,15},{8,17},{9,18},{10,... | collective-permute-start | bytes 12296 | tf_op jit(solution)/shard_map/ppermute | solution.py:62
  65.6 21.8 %collective-permute-start.13 = (bf16[16,128]{1,0:T(8,128)(2,1)S(1)}, bf16[16,128]{1,0:T(8,128)(2,1)S(1)}, u32[]{:S(2)}, u32[]{:S(2)}) collective-permute-start(bf16[16,128]{1,0:T(8,128)(2,1)S(1)} %get-tuple-element.40), channel_id=1, source_target_pairs={{1,8},{2,9},{3,10},{4,11},{5,12},{6,13},{7,14},{9,16},{10,17},{11,... | collective-permute-start | bytes 12296 | tf_op jit(solution)/shard_map/ppermute | solution.py:62
  70.5 22.4 %collective-permute-start.14 = (bf16[16,128]{1,0:T(8,128)(2,1)S(1)}, bf16[16,128]{1,0:T(8,128)(2,1)S(1)}, u32[]{:S(2)}, u32[]{:S(2)}) collective-permute-start(bf16[16,128]{1,0:T(8,128)(2,1)S(1)} %get-tuple-element.41), channel_id=1, source_target_pairs={{8,1},{9,2},{10,3},{11,4},{12,5},{13,6},{14,7},{16,9},{17,10},{18,... | collective-permute-start | bytes 12296 | tf_op jit(solution)/shard_map/ppermute | solution.py:62
  75.7 24.0 %collective-permute-start.10 = (bf16[128,128]{1,0:T(8,128)(2,1)S(1)}, bf16[128,128]{1,0:T(8,128)(2,1)S(1)}, u32[]{:S(2)}, u32[]{:S(2)}) collective-permute-start(bf16[128,128]{1,0:T(8,128)(2,1)S(1)} %get-tuple-element.37), channel_id=1, source_target_pairs={{0,1},{1,2},{2,3},{3,4},{4,5},{5,6},{6,7},{8,9},{9,10},{10,11},{11... | collective-permute-start | bytes 98312 | tf_op jit(solution)/shard_map/ppermute | solution.py:62
  83.5 16.1 %collective-permute-start.11 = (bf16[128,128]{1,0:T(8,128)(2,1)S(1)}, bf16[128,128]{1,0:T(8,128)(2,1)S(1)}, u32[]{:S(2)}, u32[]{:S(2)}) collective-permute-start(bf16[128,128]{1,0:T(8,128)(2,1)S(1)} %get-tuple-element.38), channel_id=1, source_target_pairs={{1,0},{2,1},{3,2},{4,3},{5,4},{6,5},{7,6},{9,8},{10,9},{11,10},{12... | collective-permute-start | bytes 98312 | tf_op jit(solution)/shard_map/ppermute | solution.py:62
  85.5 14.2 %collective-permute-start.8 = (bf16[128,128]{1,0:T(8,128)(2,1)S(1)}, bf16[128,128]{1,0:T(8,128)(2,1)S(1)}, u32[]{:S(2)}, u32[]{:S(2)}) collective-permute-start(bf16[128,128]{1,0:T(8,128)(2,1)S(1)} %get-tuple-element.35), channel_id=1, source_target_pairs={{0,8},{1,9},{2,10},{3,11},{4,12},{5,13},{6,14},{7,15},{8,16},{9,17... | collective-permute-start | bytes 98312 | tf_op jit(solution)/shard_map/ppermute | solution.py:62
  87.4 12.2 %collective-permute-start.9 = (bf16[128,128]{1,0:T(8,128)(2,1)S(1)}, bf16[128,128]{1,0:T(8,128)(2,1)S(1)}, u32[]{:S(2)}, u32[]{:S(2)}) collective-permute-start(bf16[128,128]{1,0:T(8,128)(2,1)S(1)} %get-tuple-element.36), channel_id=1, source_target_pairs={{8,0},{9,1},{10,2},{11,3},{12,4},{13,5},{14,6},{15,7},{16,8},{17,9... | collective-permute-start | bytes 98312 | tf_op jit(solution)/shard_map/ppermute | solution.py:62
  92.9 6.7 %collective-permute-start.15 = (bf16[16,128]{1,0:T(8,128)(2,1)S(1)}, bf16[16,128]{1,0:T(8,128)(2,1)S(1)}, u32[]{:S(2)}, u32[]{:S(2)}) collective-permute-start(bf16[16,128]{1,0:T(8,128)(2,1)S(1)} %get-tuple-element.42), channel_id=1, source_target_pairs={{9,0},{10,1},{11,2},{12,3},{13,4},{14,5},{15,6},{17,8},{18,9},{19,... | collective-permute-start | bytes 12296 | tf_op jit(solution)/shard_map/ppermute | solution.py:62
Sparse Core Ops, SparseCore 0:
  62.1 266.4 all-reduce.1

commit v2 on v1

v2 whole, which is shorter than its diff:
```python
import jax
import jax.numpy as jnp
from jax import lax
from jax.experimental import pallas as pl
from jax.experimental.pallas import tpu as pltpu
from jax.sharding import Mesh, PartitionSpec as P

C = 128
CAP = 2
SIDE = (-1, 0, 1)
EMPTY = 9 * CAP
HALF = 14
GAIN_ROW = 16
SPLIT = (4, 2, 4, 4, 2)
AXES = ("y", "zl", "x", "zh", "core")
VMEM = pltpu.VMEM
f32 = jnp.float32
bf16 = jnp.bfloat16


def rim(d):
    return {-1: (7, 1), 0: (0, 8), 1: (0, 1)}[d]


def place(d):
    return {-1: (0, 1), 0: (1, 8), 1: (9, 1)}[d]


def write_rims(value, out):
    x_low, x_high, y_low, y_high = out
    for ref, x in ((x_low, 0), (x_high, 7)):
        ref[...] = value[:, x].reshape(CAP * 64, C).astype(bf16)
    for ref, y in ((y_low, 0), (y_high, 7)):
        ref[...] = value[:, :, y].reshape(CAP * 64, C).astype(bf16)


RIMS = [jax.ShapeDtypeStruct((CAP * 64, C), bf16)] * 4


def load_kernel(x_hbm, dy_hbm, w_hbm, x_ref, dy_ref, w_ref, *refs):
    out, sems = refs[:4], refs[4]
    copies = [
        pltpu.make_async_copy(src, dst, sems.at[i])
        for i, (src, dst) in enumerate(((x_hbm, x_ref), (dy_hbm, dy_ref), (w_hbm, w_ref)))
    ]
    for copy in copies:
        copy.start()
    copies[0].wait()
    write_rims(x_ref[...].astype(f32).reshape(CAP, 8, 8, 8, C), out)
    copies[1].wait()
    copies[2].wait()


def load(x, dy, weights):
    here = [jax.ShapeDtypeStruct(v.shape, v.dtype) for v in (x, dy, weights)]
    return pl.pallas_call(
        load_kernel,
        out_shape=[*here, *RIMS],
        in_specs=[pl.BlockSpec(memory_space=pltpu.HBM)] * 3,
        out_specs=[pl.BlockSpec(memory_space=VMEM)] * 7,
        scratch_shapes=[pltpu.SemaphoreType.DMA((3,))],
        compiler_params=pltpu.CompilerParams(vmem_limit_bytes=16 * 2**20),
    )(x, dy, weights)


def adjoint_kernel(w_ref, out_ref):
    for k in range(27):
        at = C * (k % 9)
        out_ref[k // 9, at : at + C] = w_ref[26 - k].astype(f32).T.astype(bf16)


def adjoint_of(weights):
    return pl.pallas_call(
        adjoint_kernel,
        out_shape=jax.ShapeDtypeStruct((3, 9 * C, C), bf16),
        in_specs=[pl.BlockSpec(memory_space=VMEM)],
        out_specs=pl.BlockSpec(memory_space=VMEM),
        compiler_params=pltpu.CompilerParams(vmem_limit_bytes=8 * 2**20),
    )(weights)


def widen_kernel(before_ref, after_ref, low_ref, high_ref, low_out, high_out):
    before = before_ref[...].astype(f32).reshape(CAP, 1, 8, 8, C)
    after = after_ref[...].astype(f32).reshape(CAP, 1, 8, 8, C)
    for y, own, out in ((0, low_ref, low_out), (7, high_ref, high_out)):
        middle = own[...].astype(f32).reshape(CAP, 8, 8, C)
        wide = jnp.concatenate([before[:, :, y], middle, after[:, :, y]], axis=1)
        out[...] = wide.reshape(CAP * 80, C).astype(bf16)


def widen(before, after, low, high):
    return pl.pallas_call(
        widen_kernel,
        out_shape=[jax.ShapeDtypeStruct((CAP * 80, C), bf16)] * 2,
        in_specs=[pl.BlockSpec(memory_space=VMEM)] * 4,
        out_specs=[pl.BlockSpec(memory_space=VMEM)] * 2,
        compiler_params=pltpu.CompilerParams(vmem_limit_bytes=4 * 2**20),
    )(before, after, low, high)


def shift(value, dx, dy):
    ny = lax.axis_size("zh") * lax.axis_size("core")
    nx = lax.axis_size(AXES) // ny
    pairs = []
    for i in range(nx):
        for j in range(ny):
            if 0 <= i + dx < nx and 0 <= j + dy < ny:
                pairs.append((i * ny + j, (i + dx) * ny + j + dy))
    return lax.ppermute(value, AXES, pairs)


def fill_table(table, own, halo):
    from_xm, from_xp, from_ym, from_yp = halo
    table[4 * CAP : 5 * CAP] = own.astype(f32).reshape(CAP, 8, 64, C)
    table[EMPTY] = jnp.zeros((8, 64, C), f32)
    for ref, device, x in ((from_xm, 1, 7), (from_xp, 7, 0)):
        table[device * CAP : (device + 1) * CAP, x] = ref[...].astype(f32).reshape(CAP, 64, C)
    for ref, dy, y in ((from_ym, 0, 7), (from_yp, 2, 0)):
        wide = ref[...].astype(f32).reshape(CAP, 10, 8, C)
        for dx, at, x, count in ((0, 0, 7, 1), (1, 1, 0, 8), (2, 9, 0, 1)):
            device = 3 * dx + dy
            table[device * CAP : (device + 1) * CAP, x : x + count, 8 * y : 8 * y + 8] = wide[:, at : at + count]


def unfold(codes, table, planes, unfolded):
    height = lax.broadcasted_iota(jnp.int32, (1, 8, C), 1)
    for s in range(CAP):
        for a in SIDE:
            for b in SIDE:
                (xs, nx), (ys, ny) = rim(a), rim(b)
                (xd, _), (yd, _) = place(a), place(b)
                parts = []
                for c in SIDE:
                    code = codes[s, 9 * (a + 1) + 3 * (b + 1) + (c + 1)]
                    code = jnp.where(code < 0, EMPTY, code)
                    part = table[code, xs : xs + nx, 8 * ys : 8 * (ys + ny), :]
                    parts.append(part.reshape(nx * ny, 8, C))
                below, here, above = parts
                down = pltpu.roll(jnp.where(height == 7, below, here), 1, 1)
                up = pltpu.roll(jnp.where(height == 0, above, here), 7, 1)
                for i, part in enumerate((down, here, up)):
                    planes[i, xd : xd + nx, 8 * yd : 8 * (yd + ny), :] = part.reshape(nx, ny * 8, C)
        for b in SIDE:
            for c in SIDE:
                at = C * (3 * (b + 1) + (c + 1))
                unfolded[s, :, :, at : at + C] = planes[c + 1, :, 8 * (1 + b) : 8 * (1 + b) + 64, :].astype(bf16)


def split_gain(rows, at, here):
    total = rows[at : at + 8] + rows[at + 8 : at + 16]
    high = total.astype(bf16).astype(f32)
    pair = jnp.concatenate([high, total - high], axis=0)
    pair = jnp.where(here, pair, rows[at : at + 16])
    pieces = [rows[:at]] if at else []
    return jnp.concatenate([*pieces, pair, rows[at + 16 :]], axis=0)


def forward_kernel(codes, core, x_ref, dy_ref, w_ref, gain_ref, *refs):
    halo, refs = refs[:4], refs[4:]
    out_ref, pre_grad_ref, scaled_ref, keep_ref, send_ref = refs[:5]
    rim_refs, refs = refs[5:9], refs[9:]
    table, planes, unfolded, shifted, terms = refs
    fill_table(table, x_ref[...], halo)
    unfold(codes, table, planes, unfolded)
    gain = gain_ref[...]
    gain_sum = jnp.zeros((1, C), f32)
    rim_values = []
    for s in range(CAP):
        conv = jnp.zeros((512, C), f32)
        for a in range(3):
            conv = conv + jnp.dot(
                unfolded[s, a : a + 8].reshape(512, 9 * C), w_ref[a], preferred_element_type=f32
            )
        occupied = codes[s, 13] >= 0
        own = jnp.where(occupied, x_ref[s].astype(f32), 0.0)
        upstream = jnp.where(occupied, dy_ref[s].astype(f32), 0.0)
        pre_act = own + gain * conv
        sig = jax.nn.sigmoid(pre_act)
        out_ref[s] = (pre_act * sig).astype(bf16)
        pre_grad = upstream * sig * (1.0 + pre_act * (1.0 - sig))
        pre_grad_ref[s] = pre_grad
        scaled = (gain * pre_grad).astype(bf16)
        scaled_ref[s] = scaled
        rim_values.append(scaled.astype(f32).reshape(1, 8, 8, 8, C))
        gain_sum = gain_sum + jnp.sum(pre_grad * conv, axis=0, keepdims=True)
        for a in range(3):
            at = C * a
            shifted[s, a : a + 8, :, at : at + C] = scaled.reshape(8, 64, C)
            for x in range(10):
                if not a <= x < a + 8:
                    shifted[s, x, :, at : at + C] = jnp.zeros((64, C), bf16)
    write_rims(jnp.concatenate(rim_values, axis=0), rim_refs)
    rhs = shifted[...].reshape(CAP * 640, 3 * C)
    for bc in range(9):
        lhs = unfolded[:, :, :, C * bc : C * bc + C].reshape(CAP * 640, C)
        term = lax.dot_general(lhs, rhs, (((0,), (0,)), ((), ())), preferred_element_type=f32)
        for a in range(3):
            half, block = divmod(9 * a + bc, HALF)
            terms[half, block] = term[:, C * a : C * a + C]
    first = jnp.concatenate([gain_sum, jnp.zeros((7, C), f32)], axis=0)
    high = first.astype(bf16).astype(f32)
    terms[1, HALF - 1] = jnp.zeros((C, C), f32)
    terms[1, HALF - 1, GAIN_ROW : GAIN_ROW + 16] = jnp.concatenate([high, first - high], axis=0)
    keep_ref[...] = terms[core[0]].reshape(HALF * C, C)
    send_ref[...] = terms[1 - core[0]].reshape(HALF * C, C).astype(bf16)


def forward(codes, core, x, dy, weights, gain, halo):
    block = jax.ShapeDtypeStruct((CAP, 512, C), bf16)
    vmem = pl.BlockSpec(memory_space=VMEM)
    smem = pl.BlockSpec(memory_space=pltpu.SMEM)
    return pl.pallas_call(
        forward_kernel,
        out_shape=[
            block,
            jax.ShapeDtypeStruct((CAP, 512, C), f32),
            block,
            jax.ShapeDtypeStruct((HALF * C, C), f32),
            jax.ShapeDtypeStruct((HALF * C, C), bf16),
            *RIMS,
        ],
        in_specs=[smem] * 2 + [vmem] * 8,
        out_specs=[vmem] * 9,
        scratch_shapes=[
            VMEM((EMPTY + 1, 8, 64, C), f32),
            VMEM((3, 10, 80, C), f32),
            VMEM((CAP, 10, 64, 9 * C), bf16),
            VMEM((CAP, 10, 64, 3 * C), bf16),
            VMEM((2, HALF, C, C), f32),
        ],
        compiler_params=pltpu.CompilerParams(vmem_limit_bytes=40 * 2**20),
    )(codes, core, x, dy, weights, gain, *halo)


def backward_kernel(codes, scaled_ref, w_ref, pre_grad_ref, *refs):
    halo, (grad_ref, table, planes, unfolded) = refs[:4], refs[4:]
    fill_table(table, scaled_ref[...], halo)
    unfold(codes, table, planes, unfolded)
    for s in range(CAP):
        total = pre_grad_ref[s]
        for a in range(3):
            total = total + jnp.dot(
                unfolded[s, a : a + 8].reshape(512, 9 * C), w_ref[a], preferred_element_type=f32
            )
        grad_ref[s] = total.astype(bf16)


def backward(codes, scaled, weights, pre_grad, halo):
    vmem = pl.BlockSpec(memory_space=VMEM)
    return pl.pallas_call(
        backward_kernel,
        out_shape=jax.ShapeDtypeStruct((CAP, 512, C), bf16),
        in_specs=[pl.BlockSpec(memory_space=pltpu.SMEM)] + [vmem] * 7,
        out_specs=vmem,
        scratch_shapes=[
            VMEM((EMPTY + 1, 8, 64, C), f32),
            VMEM((3, 10, 80, C), f32),
            VMEM((CAP, 10, 64, 9 * C), bf16),
        ],
        compiler_params=pltpu.CompilerParams(vmem_limit_bytes=40 * 2**20),
    )(codes, scaled, weights, pre_grad, *halo)


def pair_kernel(core, keep_ref, arrived_ref, out_ref):
    total = keep_ref[...] + arrived_ref[...].astype(f32)
    total = split_gain(total, (HALF - 1) * C + GAIN_ROW, core[0] == 1)
    out_ref[...] = total.astype(bf16).reshape(out_ref.shape)


def sum_kernel(last, parts_ref, out_ref):
    total = jnp.sum(parts_ref[...].astype(f32), axis=0)
    rows = total.shape[0]
    total = split_gain(total, rows - C + GAIN_ROW, last[0] == 1)
    out_ref[...] = jnp.broadcast_to(total.astype(bf16)[None], out_ref.shape)


def finish_kernel(core, mine_ref, other_ref, weight_ref, gain_ref):
    mine = mine_ref[...].reshape(HALF * C, C).astype(f32)
    other = other_ref[...].reshape(HALF * C, C).astype(f32)
    first = core[0] == 0
    weight_ref[:HALF] = jnp.where(first, mine, other).reshape(HALF, C, C)
    second = jnp.where(first, other, mine)
    weight_ref[HALF:] = second[: (HALF - 1) * C].reshape(HALF - 1, C, C)
    at = (HALF - 1) * C + GAIN_ROW
    gain_ref[...] = second[at : at + 8] + second[at + 8 : at + 16]


def small(kernel, out_shape, scalar, *operands):
    vmem = pl.BlockSpec(memory_space=VMEM)
    return pl.pallas_call(
        kernel,
        out_shape=out_shape,
        in_specs=[pl.BlockSpec(memory_space=pltpu.SMEM)] + [vmem] * len(operands),
        out_specs=jax.tree.map(lambda _: vmem, out_shape),
        compiler_params=pltpu.CompilerParams(vmem_limit_bytes=40 * 2**20),
    )(scalar, *operands)


def trade(parts, axes):
    return lax.all_to_all(parts, axes, 0, 0, tiled=True)


def on_device(features, cotangent, neighbours, weights, channel_gain):
    together = lax.optimization_barrier
    plane, line = ("y", "x"), ("zl", "zh")
    n_plane, n_line = lax.axis_size(plane), lax.axis_size(line)
    rows = HALF * C // n_plane
    swap = [(0, 1), (1, 0)]
    core = lax.axis_index("core").astype(jnp.int32).reshape(1)
    last = core * (lax.axis_index(plane) == n_plane - 1).astype(jnp.int32)
    codes = neighbours[0, 0]

    x, dy, weights, x_low, x_high, y_low, y_high = load(features[0, 0], cotangent[0, 0], weights)
    before, after, adjoint = together((shift(x_high, 1, 0), shift(x_low, -1, 0), adjoint_of(weights)))
    low, high = widen(before, after, y_low, y_high)
    halo = (before, after, shift(high, 0, 1), shift(low, 0, -1))
    result, pre_grad, scaled, keep, send, x_low, x_high, y_low, y_high = forward(
        codes, core, x, dy, weights.reshape(3, 9 * C, C), channel_gain.reshape(1, C), halo
    )

    before, after, arrived = together(
        (shift(x_high, 1, 0), shift(x_low, -1, 0), lax.ppermute(send, "core", swap))
    )
    low, high = widen(before, after, y_low, y_high)
    parts = small(pair_kernel, jax.ShapeDtypeStruct((n_plane, rows, C), bf16), core, keep, arrived)
    below, above, parts = together((shift(high, 0, 1), shift(low, 0, -1), trade(parts, plane)))
    grad = backward(codes, scaled, adjoint, pre_grad, (before, after, below, above))
    parts = small(sum_kernel, jax.ShapeDtypeStruct((n_line, rows, C), bf16), last, parts)
    parts = small(sum_kernel, jax.ShapeDtypeStruct((n_plane, rows, C), bf16), last, trade(parts, line))
    mine = trade(parts, plane)
    other = lax.ppermute(mine, "core", swap)
    shapes = (jax.ShapeDtypeStruct((27, C, C), f32), jax.ShapeDtypeStruct((8, C), f32))
    weight_grad, gain_grad = small(finish_kernel, shapes, core, mine, other)
    return (result[None, None], grad[None, None], weight_grad, gain_grad[0])


def solution(mesh):
    physical = Mesh(mesh.devices.reshape(SPLIT), AXES)
    gx, gy = ("y", "zl", "x"), ("zh", "core")
    split = P(gx, gy, None, None, None)
    return jax.shard_map(
        on_device,
        mesh=physical,
        in_specs=(split, split, P(gx, gy, None, None), P(), P()),
        out_specs=(split, split, P(), P()),
        check_vma=False,
    )
```

time: 342 us -> 102 us (0.30)
  waiting for transfers between devices: 247 us -> 10.2 us
  blocking collectives: 0 us -> 30.4 us
  between operations: 14.3 us -> 0.83 us
  starting transfers between devices: 57.3 us -> 45.5 us
  local copies, waits for them, and re-layouts: 9.87 us -> 3.59 us
    psum x1 -> x0, waiting for transfers between devices: 225 us -> none  [on_device(): total = lax.psum(terms, ('gx', 'gy'))]
    all_to_all x0 -> x2, blocking collectives: none -> 30.4 us  [trade(): return lax.all_to_all(parts, axes, 0, 0, tiled=True)]
    ppermute x16 -> x10, starting transfers between devices: 57.2 us -> 36.5 us  [the longest x8 34.9 us: shift(): return lax.ppermute(value, AXES, pairs)]
    ppermute x16 -> x10, waiting for transfers between devices: 21.8 us -> 10.2 us  [the longest x8 10.2 us: shift(): return lax.ppermute(value, AXES, pairs)]
    all_to_all x0 -> x1, starting transfers between devices: none -> 9.02 us  [trade(): return lax.all_to_all(parts, axes, 0, 0, tiled=True)]
  transfers between devices with their start and end apart: 17 -> 11, of which waited for: 6 -> 4; matrix products, arithmetic and copies ran while one was open for 0% -> 0% of each run, Pallas kernels for 1% -> 4%
where the time goes in v2:
time: 102 us
  starting transfers between devices  45.5 us (45%)
  blocking collectives  30.4 us (30%)
  Pallas kernels  11 us (11%)
  waiting for transfers between devices  10.2 us (10%)
  local copies, waits for them, and re-layouts  3.59 us (4%)
    ppermute x8, starting transfers between devices, shift(): return lax.ppermute(value, AXES, pairs)  34.9 us
    all_to_all x2, blocking collectives, trade(): return lax.all_to_all(parts, axes, 0, 0, tiled=True)  30.4 us
    ppermute x8, waiting for transfers between devices, shift(): return lax.ppermute(value, AXES, pairs)  10.2 us
    all_to_all x1, starting transfers between devices, trade(): return lax.all_to_all(parts, axes, 0, 0, tiled=True)  9.02 us
    pallas_call x1, Pallas kernels, forward(): pl.pallas_call(forward_kernel, out_shape=[block, jax.ShapeDtypeStruct((CA...  4.58 us
    pallas_call x1, Pallas kernels, backward(): pl.pallas_call(backward_kernel, out_shape=jax.ShapeDtypeStruct((CAP, 512,...  3.37 us
    unnamed x10, local copies, waits for them, and re-layouts  3.08 us
    pallas_call x4, Pallas kernels, small(): pl.pallas_call(kernel, out_shape=out_shape, in_specs=[pl.BlockSpec(memory...  2.41 us
  transfers between devices with their start and end apart: 11, of which 4 were waited for; matrix products, arithmetic and copies ran while one was open for 0% of the time, Pallas kernels for 4%

profile of v2, /device:TPU:33, one launch (start us, length us, event | category | flops | bytes accessed | tf_op | source)
XLA Modules:
  0.0 101.5 jit_solution(11079049426617302618)
XLA Ops:
  0.6 0.0 copy-start.4
  0.6 0.0 copy-start.3
  0.7 0.0 copy-start
  0.7 1.2 %copy-done = bf16[27,128,128]{2,1,0:T(8,128)(2,1)S(1)} copy-done((bf16[27,128,128]{2,1,0:T(8,128)(2,1)S(1)}, bf16[27,128,128]{2,1,0:T(8,128)(2,1)}, u32[]{:S(2)}) %copy-start) | copy-done | bytes 884760
  1.8 0.0 copy-start.1
  1.8 0.9 copy-done.1
  2.8 0.0 copy-start.2
  2.8 0.9 copy-done.2
  3.7 0.3 shard_map.84
  4.0 3.1 %collective-permute-start = (bf16[128,128]{1,0:T(8,128)(2,1)S(1)}, bf16[128,128]{1,0:T(8,128)(2,1)S(1)}, u32[]{:S(2)}, u32[]{:S(2)}) collective-permute-start(bf16[128,128]{1,0:T(8,128)(2,1)S(1)} %get-tuple-element.38), channel_id=1, source_target_pairs={{0,8},{1,9},{2,10},{3,11},{4,12},{5,13},{6,14},{7,15},{8,16},{9,17... | collective-permute-start | bytes 98312 | tf_op jit(solution)/shard_map/ppermute | solution.py:109
  7.1 4.3 %collective-permute-start.1 = (bf16[128,128]{1,0:T(8,128)(2,1)S(1)}, bf16[128,128]{1,0:T(8,128)(2,1)S(1)}, u32[]{:S(2)}, u32[]{:S(2)}) collective-permute-start(bf16[128,128]{1,0:T(8,128)(2,1)S(1)} %get-tuple-element.39), channel_id=1, source_target_pairs={{8,0},{9,1},{10,2},{11,3},{12,4},{13,5},{14,6},{15,7},{16,8},{17,9... | collective-permute-start | bytes 98312 | tf_op jit(solution)/shard_map/ppermute | solution.py:109
  11.4 0.3 shard_map.85.w_ref
  11.7 0.0 collective-permute-done.before_ref.refs_0_
  11.7 0.7 collective-permute-done.1.after_ref.refs_1_
  12.4 6.6 %collective-permute-start.2 = (bf16[160,128]{1,0:T(8,128)(2,1)S(1)}, bf16[160,128]{1,0:T(8,128)(2,1)S(1)}, u32[]{:S(2)}, u32[]{:S(2)}) collective-permute-start(bf16[160,128]{1,0:T(8,128)(2,1)S(1)} %get-tuple-element.44), channel_id=1, source_target_pairs={{0,1},{1,2},{2,3},{3,4},{4,5},{5,6},{6,7},{8,9},{9,10},{10,11},{11... | collective-permute-start | bytes 122888 | tf_op jit(solution)/shard_map/ppermute | solution.py:109
  19.0 1.9 %collective-permute-start.3 = (bf16[160,128]{1,0:T(8,128)(2,1)S(1)}, bf16[160,128]{1,0:T(8,128)(2,1)S(1)}, u32[]{:S(2)}, u32[]{:S(2)}) collective-permute-start(bf16[160,128]{1,0:T(8,128)(2,1)S(1)} %get-tuple-element.45), channel_id=1, source_target_pairs={{1,0},{2,1},{3,2},{4,3},{5,4},{6,5},{7,6},{9,8},{10,9},{11,10},{12... | collective-permute-start | bytes 122888 | tf_op jit(solution)/shard_map/ppermute | solution.py:109
  21.0 0.0 collective-permute-done.2.refs_2_
  21.0 4.3 %collective-permute-done.3.refs_3_ = bf16[160,128]{1,0:T(8,128)(2,1)S(1)} collective-permute-done((bf16[160,128]{1,0:T(8,128)(2,1)S(1)}, bf16[160,128]{1,0:T(8,128)(2,1)S(1)}, u32[]{:S(2)}, u32[]{:S(2)}) %collective-permute-start.3) | collective-permute-done | bytes 40992 | tf_op jit(solution)/shard_map/ppermute | solution.py:109
  25.3 0.0 copy-done.4
  25.3 0.0 copy-done.3
  25.3 4.6 %shard_map.87 = (bf16[2,512,128]{2,1,0:T(8,128)(2,1)}, f32[2,512,128]{2,1,0:T(8,128)S(1)}, bf16[2,512,128]{2,1,0:T(8,128)(2,1)S(1)}, f32[1792,128]{1,0:T(8,128)S...) custom-call(s32[2,27]{1,0:T(2,128)S(1)} %bitcast.14, ...), custom_call_target="tpu_custom_call" | custom-call | tf_op jit(solution)/shard_map/pallas_call | solution.py:212
  29.9 0.1 collective-permute-start.6
  30.0 2.8 %collective-permute-start.4 = (bf16[128,128]{1,0:T(8,128)(2,1)S(1)}, bf16[128,128]{1,0:T(8,128)(2,1)S(1)}, u32[]{:S(2)}, u32[]{:S(2)}) collective-permute-start(bf16[128,128]{1,0:T(8,128)(2,1)S(1)} %get-tuple-element.50), channel_id=1, source_target_pairs={{0,8},{1,9},{2,10},{3,11},{4,12},{5,13},{6,14},{7,15},{8,16},{9,17... | collective-permute-start | bytes 98312 | tf_op jit(solution)/shard_map/ppermute | solution.py:109
  32.8 5.2 %collective-permute-start.5 = (bf16[128,128]{1,0:T(8,128)(2,1)S(1)}, bf16[128,128]{1,0:T(8,128)(2,1)S(1)}, u32[]{:S(2)}, u32[]{:S(2)}) collective-permute-start(bf16[128,128]{1,0:T(8,128)(2,1)S(1)} %get-tuple-element.51), channel_id=1, source_target_pairs={{8,0},{9,1},{10,2},{11,3},{12,4},{13,5},{14,6},{15,7},{16,8},{17,9... | collective-permute-start | bytes 98312 | tf_op jit(solution)/shard_map/ppermute | solution.py:109
  37.9 0.0 collective-permute-done.4.before_ref.refs_0_
  38.0 1.0 collective-permute-done.5.after_ref.refs_1_
  38.9 0.0 collective-permute-done.6.arrived_ref
  38.9 0.9 shard_map.89
  39.8 9.0 %all-to-all-start = ((bf16[16,112,128]{2,1,0:T(8,128)(2,1)}), bf16[16,112,128]{2,1,0:T(8,128)(2,1)S(1)}, u32[]{:S(2)}, u32[]{:S(2)}) async-start(bf16[16,112,128]{2,1,0:T(8,128)(2,1)} %shard_map.89), calls=%async_computation | async-start | bytes 917504 | tf_op jit(solution)/shard_map/all_to_all | solution.py:300
  48.9 9.1 %collective-permute-start.7 = (bf16[160,128]{1,0:T(8,128)(2,1)S(1)}, bf16[160,128]{1,0:T(8,128)(2,1)S(1)}, u32[]{:S(2)}, u32[]{:S(2)}) collective-permute-start(bf16[160,128]{1,0:T(8,128)(2,1)S(1)} %get-tuple-element.57), channel_id=1, source_target_pairs={{0,1},{1,2},{2,3},{3,4},{4,5},{5,6},{6,7},{8,9},{9,10},{10,11},{11... | collective-permute-start | bytes 122888 | tf_op jit(solution)/shard_map/ppermute | solution.py:109
  58.0 1.9 %collective-permute-start.8 = (bf16[160,128]{1,0:T(8,128)(2,1)S(1)}, bf16[160,128]{1,0:T(8,128)(2,1)S(1)}, u32[]{:S(2)}, u32[]{:S(2)}) collective-permute-start(bf16[160,128]{1,0:T(8,128)(2,1)S(1)} %get-tuple-element.58), channel_id=1, source_target_pairs={{1,0},{2,1},{3,2},{4,3},{5,4},{6,5},{7,6},{9,8},{10,9},{11,10},{12... | collective-permute-start | bytes 122888 | tf_op jit(solution)/shard_map/ppermute | solution.py:109
  60.0 0.0 collective-permute-done.7.refs_2_
  60.0 4.3 %collective-permute-done.8.refs_3_ = bf16[160,128]{1,0:T(8,128)(2,1)S(1)} collective-permute-done((bf16[160,128]{1,0:T(8,128)(2,1)S(1)}, bf16[160,128]{1,0:T(8,128)(2,1)S(1)}, u32[]{:S(2)}, u32[]{:S(2)}) %collective-permute-start.8) | collective-permute-done | bytes 40992 | tf_op jit(solution)/shard_map/ppermute | solution.py:109
  64.2 0.0 all-to-all-done.parts_ref
  64.2 0.1 shard_map.91
  64.3 12.8 %all_to_all.15.parts_ref = bf16[8,112,128]{2,1,0:T(8,128)(2,1)S(1)} all-to-all(bf16[8,112,128]{2,1,0:T(8,128)(2,1)S(1)} %shard_map.91), channel_id=1, replica_groups=mesh['y'=4,'zl'=2,'x'=4,'zh'=4,'core'=2] {'zl','zh'}, dimensions={0} | all-to-all | bytes 458752 | tf_op jit(solution)/shard_map/all_to_all | solution.py:300
  77.2 17.6 %all_to_all.16.mine_ref = bf16[16,112,128]{2,1,0:T(8,128)(2,1)S(1)} all-to-all(bf16[16,112,128]{2,1,0:T(8,128)(2,1)S(1)} %shard_map.92), channel_id=1, replica_groups=mesh['y'=4,'zl'=2,'x'=4,'zh'=4,'core'=2] {'y','x'}, dimensions={0} | all-to-all | bytes 917504 | tf_op jit(solution)/shard_map/all_to_all | solution.py:300
  94.8 1.5 %collective-permute-start.9 = (bf16[16,112,128]{2,1,0:T(8,128)(2,1)S(1)}, bf16[16,112,128]{2,1,0:T(8,128)(2,1)S(1)}, u32[]{:S(2)}, u32[]{:S(2)}) collective-permute-start(bf16[16,112,128]{2,1,0:T(8,128)(2,1)S(1)} %all_to_all.16.mine_ref), channel_id=1, source_target_pairs={{0,1},{1,0},{2,3},{3,2},{4,5},{5,4},{6,7},{7,6},{8,9},{9,8},{10,11... | collective-permute-start | bytes 1376264 | tf_op jit(solution)/shard_map/ppermute | solution.py:331
  96.2 3.4 %shard_map.90 = bf16[2,512,128]{2,1,0:T(8,128)(2,1)} custom-call(s32[2,27]{1,0:T(2,128)S(1)} %bitcast.15, bf16[2,512,128]{2,1,0:T(8,128)(2,1)S(1)} %get-tuple-element.47.scaled_ref, bf16[3,1152,128]{2,1,0:T(8,128)(2,1)S(1)} %shard_map.85.w_ref, f32[2,512,128]{2,1,0:T(8,128)S(1)} %get-tuple-element.49.pre_grad_ref, ...), custom_call_target="tpu_custom_call" | custom-call | tf_op jit(solution)/shard_map/pallas_call | solution.py:250
  99.6 0.0 collective-permute-done.9.other_ref
  99.6 1.4 %shard_map.93 = (f32[27,128,128]{2,1,0:T(8,128)}, f32[8,128]{1,0:T(8,128)S(1)}) custom-call(s32[1]{0:T(128)} %bitcast.1.core, bf16[16,112,128]{2,1,0:T(8,128)(2,1)S(1)} %all_to_all.16.mine_ref, bf16[16,112,128]{2,1,0:T(8,128)(2,1)S(1)} %collective-permute-done.9.other_ref), custom_call_target="tpu_custom_call" | custom-call | tf_op jit(solution)/shard_map/pallas_call | solution.py:290
  101.0 0.5 slice_bitcast_fusion
  (3 shorter events, 0.1 us)
Async XLA Ops:
  0.6 24.6 %copy-start.4 = (f32[128]{0:T(128)S(1)}, f32[128]{0:T(128)}, u32[]{:S(2)}) copy-start(f32[128]{0:T(128)} %param.9) | copy-start | bytes 1540
  0.6 24.6 %copy-start.3 = (s32[1,1,2,27]{3,2,1,0:T(2,128)S(1)}, s32[1,1,2,27]{3,2,1,0:T(2,128)}, u32[]{:S(2)}) copy-start(s32[1,1,2,27]{3,2,1,0:T(2,128)} %param.7) | copy-start | bytes 652
  0.7 1.2 %copy-start = (bf16[27,128,128]{2,1,0:T(8,128)(2,1)S(1)}, bf16[27,128,128]{2,1,0:T(8,128)(2,1)}, u32[]{:S(2)}) copy-start(bf16[27,128,128]{2,1,0:T(8,128)(2,1)} %w_hbm.1) | copy-start | bytes 2654212
  1.8 0.9 copy-start.1
  2.8 0.9 copy-start.2
  4.0 7.7 %collective-permute-start = (bf16[128,128]{1,0:T(8,128)(2,1)S(1)}, bf16[128,128]{1,0:T(8,128)(2,1)S(1)}, u32[]{:S(2)}, u32[]{:S(2)}) collective-permute-start(bf16[128,128]{1,0:T(8,128)(2,1)S(1)} %get-tuple-element.38), channel_id=1, source_target_pairs={{0,8},{1,9},{2,10},{3,11},{4,12},{5,13},{6,14},{7,15},{8,16},{9,17... | collective-permute-start | bytes 98312 | tf_op jit(solution)/shard_map/ppermute | solution.py:109
  7.1 5.3 %collective-permute-start.1 = (bf16[128,128]{1,0:T(8,128)(2,1)S(1)}, bf16[128,128]{1,0:T(8,128)(2,1)S(1)}, u32[]{:S(2)}, u32[]{:S(2)}) collective-permute-start(bf16[128,128]{1,0:T(8,128)(2,1)S(1)} %get-tuple-element.39), channel_id=1, source_target_pairs={{8,0},{9,1},{10,2},{11,3},{12,4},{13,5},{14,6},{15,7},{16,8},{17,9... | collective-permute-start | bytes 98312 | tf_op jit(solution)/shard_map/ppermute | solution.py:109
  12.4 8.5 %collective-permute-start.2 = (bf16[160,128]{1,0:T(8,128)(2,1)S(1)}, bf16[160,128]{1,0:T(8,128)(2,1)S(1)}, u32[]{:S(2)}, u32[]{:S(2)}) collective-permute-start(bf16[160,128]{1,0:T(8,128)(2,1)S(1)} %get-tuple-element.44), channel_id=1, source_target_pairs={{0,1},{1,2},{2,3},{3,4},{4,5},{5,6},{6,7},{8,9},{9,10},{10,11},{11... | collective-permute-start | bytes 122888 | tf_op jit(solution)/shard_map/ppermute | solution.py:109
  19.0 6.2 %collective-permute-start.3 = (bf16[160,128]{1,0:T(8,128)(2,1)S(1)}, bf16[160,128]{1,0:T(8,128)(2,1)S(1)}, u32[]{:S(2)}, u32[]{:S(2)}) collective-permute-start(bf16[160,128]{1,0:T(8,128)(2,1)S(1)} %get-tuple-element.45), channel_id=1, source_target_pairs={{1,0},{2,1},{3,2},{4,3},{5,4},{6,5},{7,6},{9,8},{10,9},{11,10},{12... | collective-permute-start | bytes 122888 | tf_op jit(solution)/shard_map/ppermute | solution.py:109
  29.9 9.1 %collective-permute-start.6 = (bf16[1792,128]{1,0:T(8,128)(2,1)S(1)}, bf16[1792,128]{1,0:T(8,128)(2,1)S(1)}, u32[]{:S(2)}, u32[]{:S(2)}) collective-permute-start(bf16[1792,128]{1,0:T(8,128)(2,1)S(1)} %get-tuple-element.52), channel_id=1, source_target_pairs={{0,1},{1,0},{2,3},{3,2},{4,5},{5,4},{6,7},{7,6},{8,9},{9,8},{10,11... | collective-permute-start | bytes 1376264 | tf_op jit(solution)/shard_map/ppermute | solution.py:322
  30.0 8.0 %collective-permute-start.4 = (bf16[128,128]{1,0:T(8,128)(2,1)S(1)}, bf16[128,128]{1,0:T(8,128)(2,1)S(1)}, u32[]{:S(2)}, u32[]{:S(2)}) collective-permute-start(bf16[128,128]{1,0:T(8,128)(2,1)S(1)} %get-tuple-element.50), channel_id=1, source_target_pairs={{0,8},{1,9},{2,10},{3,11},{4,12},{5,13},{6,14},{7,15},{8,16},{9,17... | collective-permute-start | bytes 98312 | tf_op jit(solution)/shard_map/ppermute | solution.py:109
  32.8 6.2 %collective-permute-start.5 = (bf16[128,128]{1,0:T(8,128)(2,1)S(1)}, bf16[128,128]{1,0:T(8,128)(2,1)S(1)}, u32[]{:S(2)}, u32[]{:S(2)}) collective-permute-start(bf16[128,128]{1,0:T(8,128)(2,1)S(1)} %get-tuple-element.51), channel_id=1, source_target_pairs={{8,0},{9,1},{10,2},{11,3},{12,4},{13,5},{14,6},{15,7},{16,8},{17,9... | collective-permute-start | bytes 98312 | tf_op jit(solution)/shard_map/ppermute | solution.py:109
  39.8 24.4 %all-to-all-start = ((bf16[16,112,128]{2,1,0:T(8,128)(2,1)}), bf16[16,112,128]{2,1,0:T(8,128)(2,1)S(1)}, u32[]{:S(2)}, u32[]{:S(2)}) async-start(bf16[16,112,128]{2,1,0:T(8,128)(2,1)} %shard_map.89), calls=%async_computation | async-start | bytes 917504 | tf_op jit(solution)/shard_map/all_to_all | solution.py:300
  48.9 11.1 %collective-permute-start.7 = (bf16[160,128]{1,0:T(8,128)(2,1)S(1)}, bf16[160,128]{1,0:T(8,128)(2,1)S(1)}, u32[]{:S(2)}, u32[]{:S(2)}) collective-permute-start(bf16[160,128]{1,0:T(8,128)(2,1)S(1)} %get-tuple-element.57), channel_id=1, source_target_pairs={{0,1},{1,2},{2,3},{3,4},{4,5},{5,6},{6,7},{8,9},{9,10},{10,11},{11... | collective-permute-start | bytes 122888 | tf_op jit(solution)/shard_map/ppermute | solution.py:109
  58.0 6.2 %collective-permute-start.8 = (bf16[160,128]{1,0:T(8,128)(2,1)S(1)}, bf16[160,128]{1,0:T(8,128)(2,1)S(1)}, u32[]{:S(2)}, u32[]{:S(2)}) collective-permute-start(bf16[160,128]{1,0:T(8,128)(2,1)S(1)} %get-tuple-element.58), channel_id=1, source_target_pairs={{1,0},{2,1},{3,2},{4,3},{5,4},{6,5},{7,6},{9,8},{10,9},{11,10},{12... | collective-permute-start | bytes 122888 | tf_op jit(solution)/shard_map/ppermute | solution.py:109
  94.8 4.8 %collective-permute-start.9 = (bf16[16,112,128]{2,1,0:T(8,128)(2,1)S(1)}, bf16[16,112,128]{2,1,0:T(8,128)(2,1)S(1)}, u32[]{:S(2)}, u32[]{:S(2)}) collective-permute-start(bf16[16,112,128]{2,1,0:T(8,128)(2,1)S(1)} %all_to_all.16.mine_ref), channel_id=1, source_target_pairs={{0,1},{1,0},{2,3},{3,2},{4,5},{5,4},{6,7},{7,6},{8,9},{9,8},{10,11... | collective-permute-start | bytes 1376264 | tf_op jit(solution)/shard_map/ppermute | solution.py:331

commit v3 on v2

v3 whole, which is shorter than its diff:
```python
import jax
import jax.numpy as jnp
from jax import lax
from jax.experimental import pallas as pl
from jax.experimental.pallas import tpu as pltpu
from jax.sharding import Mesh, PartitionSpec as P

C = 128
CAP = 2
SIDE = (-1, 0, 1)
EMPTY = 9 * CAP
HALF = 14
GAIN_ROW = 16
CORE, ODD, LAST = 0, 1, 2
SPLIT = (4, 2, 4, 4, 2)
AXES = ("y", "zl", "x", "zh", "core")
VMEM = pltpu.VMEM
f32 = jnp.float32
bf16 = jnp.bfloat16
BLOCK = jax.ShapeDtypeStruct((CAP, 512, C), bf16)


def rim(d):
    return {-1: (7, 1), 0: (0, 8), 1: (0, 1)}[d]


def place(d):
    return {-1: (0, 1), 0: (1, 8), 1: (9, 1)}[d]


def y_planes(value):
    value = value.astype(f32).reshape(CAP, 8, 8, 8, C)
    return [value[:, :, y].reshape(CAP * 64, C) for y in (0, 7)]


def rims_kernel(place, x_ref, near_ref, far_ref, x_out):
    x_out[...] = x_ref[...]
    low, high = y_planes(x_ref[...])
    first = place[CORE] == 0
    near_ref[...] = jnp.where(first, high, low).astype(bf16)
    far_ref[...] = jnp.where(first, low, high).astype(bf16)


def rims_of(place, x):
    plane = jax.ShapeDtypeStruct((CAP * 64, C), bf16)
    return small(rims_kernel, [plane, plane, BLOCK], 8, place, x)


def adjoint_kernel(w_ref, out_ref):
    for k in range(27):
        at = C * (k % 9)
        out_ref[k // 9, at : at + C] = w_ref[26 - k].astype(f32).T.astype(bf16)


def adjoint_of(weights):
    return small(adjoint_kernel, jax.ShapeDtypeStruct((3, 9 * C, C), bf16), 8, None, weights)


def fetch_kernel(value_ref, out_ref):
    out_ref[...] = value_ref[...]


def fetch(value):
    return small(fetch_kernel, BLOCK, 8, None, value)


def widen_kernel(place, near_ref, far_ref, x_ref, first_ref, second_ref):
    before, after = sides(place[CORE] == 0, near_ref, far_ref)
    wide = []
    for x in (0, 7):
        middle = x_ref[:, 64 * x : 64 * x + 64].astype(f32).reshape(CAP, 8, 8, C)
        ends = [v.reshape(CAP, 8, 8, C)[:, x : x + 1] for v in (before, after)]
        wide.append(jnp.concatenate([ends[0], middle, ends[1]], axis=1).reshape(CAP * 80, C))
    even = place[ODD] == 0
    first_ref[...] = jnp.where(even, wide[1], wide[0]).astype(bf16)
    second_ref[...] = jnp.where(even, wide[0], wide[1]).astype(bf16)


def widen(place, near, far, x):
    shapes = [jax.ShapeDtypeStruct((CAP * 80, C), bf16)] * 2
    return small(widen_kernel, shapes, 8, place, near, far, x)


def sides(first, one_ref, other_ref):
    one, other = one_ref[...].astype(f32), other_ref[...].astype(f32)
    return jnp.where(first, other, one), jnp.where(first, one, other)


def swap_far(value):
    n = lax.axis_size("zh")
    pairs = [(2 * i + 1, 2 * i + 2) for i in range(n - 1)]
    return lax.ppermute(value, ("zh", "core"), pairs + [(b, a) for a, b in pairs])


def swap_x(value, odd):
    axes = ("y", "zl", "x")
    pairs = [(i, i + 1) for i in range(odd, lax.axis_size(axes) - 1, 2)]
    return lax.ppermute(value, axes, pairs + [(b, a) for a, b in pairs])


def swap_core(value):
    return lax.ppermute(value, "core", [(0, 1), (1, 0)])


def fill_table(place, table, own, halo):
    near, far, first, second = halo
    table[4 * CAP : 5 * CAP] = own.astype(f32).reshape(CAP, 8, 64, C)
    table[EMPTY] = jnp.zeros((8, 64, C), f32)
    for value, device, y in zip(sides(place[CORE] == 0, near, far), (3, 5), (7, 0)):
        table[device * CAP : (device + 1) * CAP, :, 8 * y : 8 * y + 8] = value.reshape(CAP, 8, 8, C)
    for value, dx, x in zip(sides(place[ODD] == 0, first, second), (0, 2), (7, 0)):
        wide = value.reshape(CAP, 80, C)
        for dy, at, y, count in ((0, 0, 7, 1), (1, 1, 0, 8), (2, 9, 0, 1)):
            device = 3 * dx + dy
            table[device * CAP : (device + 1) * CAP, x, 8 * y : 8 * (y + count)] = wide[:, 8 * at : 8 * (at + count)]


def unfold(codes, table, planes, unfolded):
    height = lax.broadcasted_iota(jnp.int32, (1, 8, C), 1)
    for s in range(CAP):
        for a in SIDE:
            for b in SIDE:
                (xs, nx), (ys, ny) = rim(a), rim(b)
                (xd, _), (yd, _) = place(a), place(b)
                parts = []
                for c in SIDE:
                    code = codes[s, 9 * (a + 1) + 3 * (b + 1) + (c + 1)]
                    code = jnp.where(code < 0, EMPTY, code)
                    part = table[code, xs : xs + nx, 8 * ys : 8 * (ys + ny), :]
                    parts.append(part.reshape(nx * ny, 8, C))
                below, here, above = parts
                down = pltpu.roll(jnp.where(height == 7, below, here), 1, 1)
                up = pltpu.roll(jnp.where(height == 0, above, here), 7, 1)
                for i, part in enumerate((down, here, up)):
                    planes[i, xd : xd + nx, 8 * yd : 8 * (yd + ny), :] = part.reshape(nx, ny * 8, C)
        for b in SIDE:
            for c in SIDE:
                at = C * (3 * (b + 1) + (c + 1))
                unfolded[s, :, :, at : at + C] = planes[c + 1, :, 8 * (1 + b) : 8 * (1 + b) + 64, :].astype(bf16)


def split_gain(rows, at, here):
    total = rows[at : at + 8] + rows[at + 8 : at + 16]
    high = total.astype(bf16).astype(f32)
    pair = jnp.concatenate([high, total - high], axis=0)
    pair = jnp.where(here, pair, rows[at : at + 16])
    pieces = [rows[:at]] if at else []
    return jnp.concatenate([*pieces, pair, rows[at + 16 :]], axis=0)


def forward_kernel(codes, place, x_ref, dy_ref, w_ref, gain_ref, *refs):
    halo, refs = refs[:4], refs[4:]
    out_ref, pre_grad_ref, scaled_ref, keep_ref, send_ref, far_ref = refs[:6]
    table, planes, unfolded, shifted, terms, staged, sems = refs[6:]
    fill_table(place, table, x_ref[...], halo)
    unfold(codes, table, planes, unfolded)
    gain = gain_ref[...]
    gain_sum = jnp.zeros((1, C), f32)
    for s in range(CAP):
        conv = jnp.zeros((512, C), f32)
        for a in range(3):
            conv = conv + jnp.dot(
                unfolded[s, a : a + 8].reshape(512, 9 * C), w_ref[a], preferred_element_type=f32
            )
        occupied = codes[s, 13] >= 0
        upstream = jnp.where(occupied, dy_ref[s].astype(f32), 0.0)
        pre_act = jnp.where(occupied, x_ref[s].astype(f32), 0.0) + gain * conv
        sig = jax.nn.sigmoid(pre_act)
        staged[s] = (pre_act * sig).astype(bf16)
        pltpu.make_async_copy(staged.at[s], out_ref.at[s], sems.at[s]).start()
        pre_grad = upstream * sig * (1.0 + pre_act * (1.0 - sig))
        pre_grad_ref[s] = pre_grad
        scaled = (gain * pre_grad).astype(bf16)
        scaled_ref[s] = scaled
        gain_sum = gain_sum + jnp.sum(pre_grad * conv, axis=0, keepdims=True)
        for a in range(3):
            at = C * a
            shifted[s, a : a + 8, :, at : at + C] = scaled.reshape(8, 64, C)
            for x in range(10):
                if not a <= x < a + 8:
                    shifted[s, x, :, at : at + C] = jnp.zeros((64, C), bf16)
    core = place[CORE]
    low, high = y_planes(scaled_ref[...])
    far_ref[...] = jnp.where(core == 0, low, high).astype(bf16)
    send_ref[HALF * C :] = jnp.where(core == 0, high, low).astype(bf16)
    rhs = shifted[...].reshape(CAP * 640, 3 * C)
    for bc in range(9):
        lhs = unfolded[:, :, :, C * bc : C * bc + C].reshape(CAP * 640, C)
        term = lax.dot_general(lhs, rhs, (((0,), (0,)), ((), ())), preferred_element_type=f32)
        for a in range(3):
            half, block = divmod(9 * a + bc, HALF)
            terms[half, block] = term[:, C * a : C * a + C]
    first = jnp.concatenate([gain_sum, jnp.zeros((7, C), f32)], axis=0)
    high = first.astype(bf16).astype(f32)
    terms[1, HALF - 1] = jnp.zeros((C, C), f32)
    terms[1, HALF - 1, GAIN_ROW : GAIN_ROW + 16] = jnp.concatenate([high, first - high], axis=0)
    keep_ref[...] = terms[core].reshape(HALF * C, C)
    send_ref[: HALF * C] = terms[1 - core].reshape(HALF * C, C).astype(bf16)
    for s in range(CAP):
        pltpu.make_async_copy(staged.at[s], out_ref.at[s], sems.at[s]).wait()


def forward(codes, place, x, dy, weights, gain, halo):
    vmem = pl.BlockSpec(memory_space=VMEM)
    smem = pl.BlockSpec(memory_space=pltpu.SMEM)
    return pl.pallas_call(
        forward_kernel,
        out_shape=[
            BLOCK,
            jax.ShapeDtypeStruct((CAP, 512, C), f32),
            BLOCK,
            jax.ShapeDtypeStruct((HALF * C, C), f32),
            jax.ShapeDtypeStruct((HALF * C + CAP * 64, C), bf16),
            jax.ShapeDtypeStruct((CAP * 64, C), bf16),
        ],
        in_specs=[smem] * 2 + [vmem] * 8,
        out_specs=[pl.BlockSpec(memory_space=pltpu.HBM)] + [vmem] * 5,
        scratch_shapes=[
            VMEM((EMPTY + 1, 8, 64, C), f32),
            VMEM((3, 10, 80, C), f32),
            VMEM((CAP, 10, 64, 9 * C), bf16),
            VMEM((CAP, 10, 64, 3 * C), bf16),
            VMEM((2, HALF, C, C), f32),
            VMEM((CAP, 512, C), bf16),
            pltpu.SemaphoreType.DMA((CAP,)),
        ],
        compiler_params=pltpu.CompilerParams(vmem_limit_bytes=40 * 2**20),
    )(codes, place, x, dy, weights, gain, *halo)


def backward_kernel(codes, place, scaled_ref, w_ref, pre_grad_ref, *refs):
    halo, (grad_ref, table, planes, unfolded, staged, sems) = refs[:4], refs[4:]
    fill_table(place, table, scaled_ref[...], halo)
    unfold(codes, table, planes, unfolded)
    for s in range(CAP):
        total = pre_grad_ref[s]
        for a in range(3):
            total = total + jnp.dot(
                unfolded[s, a : a + 8].reshape(512, 9 * C), w_ref[a], preferred_element_type=f32
            )
        staged[s] = total.astype(bf16)
        pltpu.make_async_copy(staged.at[s], grad_ref.at[s], sems.at[s]).start()
    for s in range(CAP):
        pltpu.make_async_copy(staged.at[s], grad_ref.at[s], sems.at[s]).wait()


def backward(codes, place, scaled, weights, pre_grad, halo):
    vmem = pl.BlockSpec(memory_space=VMEM)
    return pl.pallas_call(
        backward_kernel,
        out_shape=BLOCK,
        in_specs=[pl.BlockSpec(memory_space=pltpu.SMEM)] * 2 + [vmem] * 7,
        out_specs=pl.BlockSpec(memory_space=pltpu.HBM),
        scratch_shapes=[
            VMEM((EMPTY + 1, 8, 64, C), f32),
            VMEM((3, 10, 80, C), f32),
            VMEM((CAP, 10, 64, 9 * C), bf16),
            VMEM((CAP, 512, C), bf16),
            pltpu.SemaphoreType.DMA((CAP,)),
        ],
        compiler_params=pltpu.CompilerParams(vmem_limit_bytes=40 * 2**20),
    )(codes, place, scaled, weights, pre_grad, *halo)


def pair_kernel(place, keep_ref, arrived_ref, out_ref, near_ref):
    total = keep_ref[...] + arrived_ref[: HALF * C].astype(f32)
    total = split_gain(total, (HALF - 1) * C + GAIN_ROW, place[CORE] == 1)
    out_ref[...] = total.astype(bf16).reshape(out_ref.shape)
    near_ref[...] = arrived_ref[HALF * C :]


def sum_kernel(place, parts_ref, out_ref):
    total = jnp.sum(parts_ref[...].astype(f32), axis=0)
    rows = total.shape[0]
    total = split_gain(total, rows - C + GAIN_ROW, place[LAST] == 1)
    out_ref[...] = jnp.broadcast_to(total.astype(bf16)[None], out_ref.shape)


def write_half(second, rows_ref, weight_ref, staged, sem):
    staged[...] = rows_ref[...].reshape(HALF, C, C).astype(f32)

    @pl.when(second)
    def _():
        copy = pltpu.make_async_copy(staged.at[: HALF - 1], weight_ref.at[HALF:], sem)
        copy.start()
        copy.wait()

    @pl.when(jnp.logical_not(second))
    def _():
        copy = pltpu.make_async_copy(staged, weight_ref.at[:HALF], sem)
        copy.start()
        copy.wait()


def mine_kernel(place, mine_ref, weight_ref, staged, sem):
    write_half(place[CORE] == 1, mine_ref, weight_ref, staged, sem)


def other_kernel(place, mine_ref, other_ref, _, weight_ref, gain_hbm, staged, sem, gain_ref, gain_sem):
    at = (HALF - 1) * C + GAIN_ROW
    mine, other = (ref[...].reshape(HALF * C, C)[at : at + 16].astype(f32) for ref in (mine_ref, other_ref))
    pair = jnp.where(place[CORE] == 1, mine, other)
    gain_ref[...] = pair[:1] + pair[8:9]
    copy = pltpu.make_async_copy(gain_ref, gain_hbm, gain_sem)
    copy.start()
    write_half(place[CORE] == 0, other_ref, weight_ref, staged, sem)
    copy.wait()


def finish(place, mine, other):
    smem, vmem, hbm = (pl.BlockSpec(memory_space=m) for m in (pltpu.SMEM, VMEM, pltpu.HBM))
    weight_grad = jax.ShapeDtypeStruct((27, C, C), f32)
    scratch = [VMEM((HALF, C, C), f32), pltpu.SemaphoreType.DMA]
    params = pltpu.CompilerParams(vmem_limit_bytes=8 * 2**20)
    partial = pl.pallas_call(
        mine_kernel,
        out_shape=weight_grad,
        in_specs=[smem, vmem],
        out_specs=hbm,
        scratch_shapes=scratch,
        compiler_params=params,
    )(place, mine)
    return pl.pallas_call(
        other_kernel,
        out_shape=[weight_grad, jax.ShapeDtypeStruct((1, C), f32)],
        in_specs=[smem, vmem, vmem, hbm],
        out_specs=[hbm, hbm],
        scratch_shapes=[*scratch, VMEM((1, C), f32), pltpu.SemaphoreType.DMA],
        input_output_aliases={3: 0},
        compiler_params=params,
    )(place, mine, other, partial)


def small(kernel, out_shape, megabytes, scalars, *operands):
    vmem = pl.BlockSpec(memory_space=VMEM)
    smem = [] if scalars is None else [scalars]
    return pl.pallas_call(
        kernel,
        out_shape=out_shape,
        in_specs=[pl.BlockSpec(memory_space=pltpu.SMEM)] * len(smem) + [vmem] * len(operands),
        out_specs=jax.tree.map(lambda _: vmem, out_shape),
        compiler_params=pltpu.CompilerParams(vmem_limit_bytes=megabytes * 2**20),
    )(*smem, *operands)


def trade(parts, axes):
    return lax.all_to_all(parts, axes, 0, 0, tiled=True)


def on_device(features, cotangent, neighbours, weights, channel_gain):
    together = lax.optimization_barrier
    plane, line = ("y", "x"), ("zl", "zh")
    n_plane, n_line = lax.axis_size(plane), lax.axis_size(line)
    rows = HALF * C // n_plane
    core = lax.axis_index("core")
    last = core * (lax.axis_index(plane) == n_plane - 1)
    place = jnp.stack([core, lax.axis_index("x") % 2, last]).astype(jnp.int32)
    codes = neighbours[0, 0]
    near, far, x = rims_of(place, features[0, 0])
    near, far, adjoint = together((swap_core(near), swap_far(far), adjoint_of(weights)))
    first, second = widen(place, near, far, x)
    first, second, dy = together((swap_x(first, 0), swap_x(second, 1), fetch(cotangent[0, 0])))
    halo = (near, far, first, second)
    result, pre_grad, scaled, keep, send, far = forward(
        codes, place, x, dy, weights.reshape(3, 9 * C, C), channel_gain.reshape(1, C), halo
    )

    shapes = [jax.ShapeDtypeStruct((n_plane, rows, C), bf16), jax.ShapeDtypeStruct((CAP * 64, C), bf16)]
    parts, near = small(pair_kernel, shapes, 8, place, keep, swap_core(send))
    far, parts = together((swap_far(far), trade(parts, plane)))
    first, second = widen(place, near, far, scaled)
    parts = small(sum_kernel, jax.ShapeDtypeStruct((n_line, rows, C), bf16), 8, place, parts)
    first, second, parts = together((swap_x(first, 0), swap_x(second, 1), trade(parts, line)))
    parts = small(sum_kernel, jax.ShapeDtypeStruct((n_plane, rows, C), bf16), 8, place, parts)
    grad = backward(codes, place, scaled, adjoint, pre_grad, (near, far, first, second))
    grad, mine = together((grad, trade(parts, plane)))
    weight_grad, gain_grad = finish(place, mine, swap_core(mine))
    return (result[None, None], grad[None, None], weight_grad, gain_grad.reshape(C))


def solution(mesh):
    physical = Mesh(mesh.devices.reshape(SPLIT), AXES)
    gx, gy = ("y", "zl", "x"), ("zh", "core")
    split = P(gx, gy, None, None, None)
    return jax.shard_map(
        on_device,
        mesh=physical,
        in_specs=(split, split, P(gx, gy, None, None), P(), P()),
        out_specs=(split, split, P(), P()),
        check_vma=False,
    )
```

time: 102 us -> 84.4 us (0.83)
  blocking collectives: 30.4 us -> 0 us
  waiting for transfers between devices: 10.2 us -> 19.1 us
  Pallas kernels: 11 us -> 17.1 us
  local copies, waits for them, and re-layouts: 3.59 us -> 2.13 us
    all_to_all x2 -> x0, blocking collectives: 30.4 us -> none  [trade(): return lax.all_to_all(parts, axes, 0, 0, tiled=True)]
    ppermute x10 -> x9, starting transfers between devices: 36.5 us -> 23.5 us  [the longest x2 11 us: swap_far(): lax.ppermute(value, ('zh', 'core'), pairs + [(b, a) for a, b in pairs])]
    all_to_all x1 -> x3, starting transfers between devices: 9.02 us -> 21 us  [trade(): return lax.all_to_all(parts, axes, 0, 0, tiled=True)]
    all_to_all x1 -> x3, waiting for transfers between devices: 0.01 us -> 7.32 us  [trade(): return lax.all_to_all(parts, axes, 0, 0, tiled=True)]
    pallas_call x4 -> x8, Pallas kernels: 2.41 us -> 6.06 us  [small(): pl.pallas_call(kernel, out_shape=out_shape, in_specs=[pl.BlockSpec(memory...]
    pallas_call x6 -> x4, Pallas kernels: 8.55 us -> 11.1 us  [the longest x1 4.67 us: forward(): pl.pallas_call(forward_kernel, out_shape=[BLOCK, jax.ShapeDtypeStruct((CA...]
    ppermute x10 -> x9, waiting for transfers between devices: 10.2 us -> 11.8 us  [the longest x4 7.93 us: swap_x(): return lax.ppermute(value, axes, pairs + [(b, a) for a, b in pairs])]
    unnamed x10 -> x12, local copies, waits for them, and re-layouts: 3.08 us -> 2.13 us
  transfers between devices with their start and end apart: 11 -> 12, of which waited for: 4 -> 8; matrix products, arithmetic and copies ran while one was open for 0% -> 0% of each run, Pallas kernels for 4% -> 7%
where the time goes in v3:
time: 84.4 us; the launch traced here: 83.9 us
  starting transfers between devices  44.6 us (53%)
  waiting for transfers between devices  19.1 us (23%)
  Pallas kernels  17.1 us (20%)
  local copies, waits for them, and re-layouts  2.13 us (3%)
    all_to_all x3, starting transfers between devices, trade(): return lax.all_to_all(parts, axes, 0, 0, tiled=True)  21 us
    ppermute x2, starting transfers between devices, swap_far(): lax.ppermute(value, ('zh', 'core'), pairs + [(b, a) for a, b in pairs])  11 us
    ppermute x4, waiting for transfers between devices, swap_x(): return lax.ppermute(value, axes, pairs + [(b, a) for a, b in pairs])  7.93 us
    ppermute x4, starting transfers between devices, swap_x(): return lax.ppermute(value, axes, pairs + [(b, a) for a, b in pairs])  7.4 us
    all_to_all x3, waiting for transfers between devices, trade(): return lax.all_to_all(parts, axes, 0, 0, tiled=True)  7.32 us
    pallas_call x8, Pallas kernels, small(): pl.pallas_call(kernel, out_shape=out_shape, in_specs=[pl.BlockSpec(memory...  6.06 us
    ppermute x3, starting transfers between devices, swap_core(): return lax.ppermute(value, 'core', [(0, 1), (1, 0)])  5.1 us
    pallas_call x1, Pallas kernels, forward(): pl.pallas_call(forward_kernel, out_shape=[BLOCK, jax.ShapeDtypeStruct((CA...  4.67 us
  transfers between devices with their start and end apart: 12, of which 8 were waited for; matrix products, arithmetic and copies ran while one was open for 0% of the time, Pallas kernels for 7%

profile of v3, /device:TPU:33, one launch (start us, length us, event | category | flops | bytes accessed | tf_op | source)
XLA Modules:
  0.0 83.9 jit_solution(2074396273694275999)
XLA Ops:
  0.6 0.0 copy-start.5
  0.6 0.0 copy-start.4
  0.7 0.1 pad_add_fusion.place
  0.7 0.0 copy-start.2
  0.7 0.9 %copy-done.2 = bf16[1,1,2,512,128]{4,3,2,1,0:T(8,128)(2,1)S(1)} copy-done((bf16[1,1,2,512,128]{4,3,2,1,0:T(8,128)(2,1)S(1)}, bf16[1,1,2,512,128]{4,3,2,1,0:T(8,128)(2,1)}, u32[]{:S(2)}) %copy-start.2) | copy-done | bytes 262168
  1.7 0.0 copy-start.3
  1.7 0.6 shard_map.84
  2.3 0.8 collective-permute-start
  3.0 4.8 %collective-permute-start.1 = (bf16[128,128]{1,0:T(8,128)(2,1)S(1)}, bf16[128,128]{1,0:T(8,128)(2,1)S(1)}, u32[]{:S(2)}, u32[]{:S(2)}) collective-permute-start(bf16[128,128]{1,0:T(8,128)(2,1)S(1)} %get-tuple-element.36), channel_id=1, source_target_pairs={{1,2},{3,4},{5,6},{2,1},{4,3},{6,5},{9,10},{11,12},{13,14},{10,9},... | collective-permute-start | bytes 98312 | tf_op jit(solution)/shard_map/ppermute | solution.py:92
  7.8 0.0 copy-start
  7.9 1.2 %copy-done = bf16[27,128,128]{2,1,0:T(8,128)(2,1)S(1)} copy-done((bf16[27,128,128]{2,1,0:T(8,128)(2,1)S(1)}, bf16[27,128,128]{2,1,0:T(8,128)(2,1)}, u32[]{:S(2)}) %copy-start) | copy-done | bytes 884760
  9.0 0.0 copy-start.1
  9.0 0.3 shard_map.85.w_ref
  9.3 0.0 collective-permute-done.near_ref.refs_0_
  9.3 0.1 collective-permute-done.1.far_ref.refs_1_
  9.4 0.6 shard_map.86
  10.0 1.3 %collective-permute-start.2 = (bf16[160,128]{1,0:T(8,128)(2,1)S(1)}, bf16[160,128]{1,0:T(8,128)(2,1)S(1)}, u32[]{:S(2)}, u32[]{:S(2)}) collective-permute-start(bf16[160,128]{1,0:T(8,128)(2,1)S(1)} %get-tuple-element.39), channel_id=1, source_target_pairs={{0,8},{16,24},{32,40},{48,56},{64,72},{80,88},{96,104},{112,120},{... | collective-permute-start | bytes 122888 | tf_op jit(solution)/shard_map/ppermute | solution.py:98
  11.3 3.3 %collective-permute-start.3 = (bf16[160,128]{1,0:T(8,128)(2,1)S(1)}, bf16[160,128]{1,0:T(8,128)(2,1)S(1)}, u32[]{:S(2)}, u32[]{:S(2)}) collective-permute-start(bf16[160,128]{1,0:T(8,128)(2,1)S(1)} %get-tuple-element.40), channel_id=1, source_target_pairs={{8,16},{24,32},{40,48},{56,64},{72,80},{88,96},{104,112},{120,128}... | collective-permute-start | bytes 122888 | tf_op jit(solution)/shard_map/ppermute | solution.py:98
  14.6 0.0 copy-done.3
  14.6 0.0 collective-permute-done.2.refs_2_
  14.6 3.5 %collective-permute-done.3.refs_3_ = bf16[160,128]{1,0:T(8,128)(2,1)S(1)} collective-permute-done((bf16[160,128]{1,0:T(8,128)(2,1)S(1)}, bf16[160,128]{1,0:T(8,128)(2,1)S(1)}, u32[]{:S(2)}, u32[]{:S(2)}) %collective-permute-start.3) | collective-permute-done | bytes 40992 | tf_op jit(solution)/shard_map/ppermute | solution.py:98
  18.1 0.0 copy-done.5
  18.1 0.0 copy-done.4
  18.1 0.0 copy-done.1
  18.1 4.7 %shard_map.88 = (bf16[2,512,128]{2,1,0:T(8,128)(2,1)}, f32[2,512,128]{2,1,0:T(8,128)S(1)}, bf16[2,512,128]{2,1,0:T(8,128)(2,1)S(1)}, f32[1792,128]{1,0:T(8,128)S...) custom-call(s32[2,27]{1,0:T(2,128)S(1)} %bitcast.14, s32[3]{0:T(128)S(1)} %pad_add_fusion.place, ...), custom_call_target="tpu_custom_call" | custom-call | tf_op jit(solution)/shard_map/pallas_call | solution.py:206
  22.8 0.1 collective-permute-start.4
  22.9 1.9 %collective-permute-done.4.arrived_ref = bf16[1920,128]{1,0:T(8,128)(2,1)S(1)} collective-permute-done((bf16[1920,128]{1,0:T(8,128)(2,1)S(1)}, bf16[1920,128]{1,0:T(8,128)(2,1)S(1)}, u32[]{:S(2)}, u32[]{:S(2)}) %collective-permute-start.4) | collective-permute-done | bytes 491552 | tf_op jit(solution)/shard_map/ppermute | solution.py:102
  24.8 1.4 %shard_map.89 = (bf16[16,112,128]{2,1,0:T(8,128)(2,1)}, bf16[128,128]{1,0:T(8,128)(2,1)S(1)}) custom-call(s32[3]{0:T(128)S(1)} %pad_add_fusion.place, f32[1792,128]{1,0:T(8,128)S(1)} %get-tuple-element.48.keep_ref, bf16[1920,128]{1,0:T(8,128)(2,1)S(1)} %collective-permute-done.4.arrived_ref), custom_call_target="tpu_custom_call" | custom-call | tf_op jit(solution)/shard_map/pallas_call | solution.py:337
  26.2 6.7 %all-to-all-start = ((bf16[16,112,128]{2,1,0:T(8,128)(2,1)}), bf16[16,112,128]{2,1,0:T(8,128)(2,1)S(1)}, u32[]{:S(2)}, u32[]{:S(2)}) async-start(bf16[16,112,128]{2,1,0:T(8,128)(2,1)} %get-tuple-element.52), calls=%async_computation | async-start | bytes 917504 | tf_op jit(solution)/shard_map/all_to_all | solution.py:347
  32.9 6.3 %collective-permute-start.5 = (bf16[128,128]{1,0:T(8,128)(2,1)S(1)}, bf16[128,128]{1,0:T(8,128)(2,1)S(1)}, u32[]{:S(2)}, u32[]{:S(2)}) collective-permute-start(bf16[128,128]{1,0:T(8,128)(2,1)S(1)} %get-tuple-element.51), channel_id=1, source_target_pairs={{1,2},{3,4},{5,6},{2,1},{4,3},{6,5},{9,10},{11,12},{13,14},{10,9},... | collective-permute-start | bytes 98312 | tf_op jit(solution)/shard_map/ppermute | solution.py:92
  39.2 1.9 %collective-permute-done.5.far_ref.refs_1_ = bf16[128,128]{1,0:T(8,128)(2,1)S(1)} collective-permute-done((bf16[128,128]{1,0:T(8,128)(2,1)S(1)}, bf16[128,128]{1,0:T(8,128)(2,1)S(1)}, u32[]{:S(2)}, u32[]{:S(2)}) %collective-permute-start.5) | collective-permute-done | bytes 32800 | tf_op jit(solution)/shard_map/ppermute | solution.py:92
  41.1 2.1 %all-to-all-done.parts_ref = bf16[16,112,128]{2,1,0:T(8,128)(2,1)S(1)} async-done(((bf16[16,112,128]{2,1,0:T(8,128)(2,1)}), bf16[16,112,128]{2,1,0:T(8,128)(2,1)S(1)}, u32[]{:S(2)}, u32[]{:S(2)}) %all-to-all-start) | async-done | bytes 458784 | tf_op jit(solution)/shard_map/all_to_all | solution.py:347
  43.1 1.3 %shard_map.91 = bf16[8,112,128]{2,1,0:T(8,128)(2,1)} custom-call(s32[3]{0:T(128)S(1)} %pad_add_fusion.place, bf16[16,112,128]{2,1,0:T(8,128)(2,1)S(1)} %all-to-all-done.parts_ref), custom_call_target="tpu_custom_call" | custom-call | tf_op jit(solution)/shard_map/pallas_call | solution.py:337
  44.4 9.3 %all-to-all-start.1 = ((bf16[8,112,128]{2,1,0:T(8,128)(2,1)}), bf16[8,112,128]{2,1,0:T(8,128)(2,1)S(1)}, u32[]{:S(2)}, u32[]{:S(2)}) async-start(bf16[8,112,128]{2,1,0:T(8,128)(2,1)} %shard_map.91), calls=%async_computation.1 | async-start | bytes 458752 | tf_op jit(solution)/shard_map/all_to_all | solution.py:347
  53.7 0.6 shard_map.90
  54.3 0.4 collective-permute-start.6
  54.7 2.5 %collective-permute-start.7 = (bf16[160,128]{1,0:T(8,128)(2,1)S(1)}, bf16[160,128]{1,0:T(8,128)(2,1)S(1)}, u32[]{:S(2)}, u32[]{:S(2)}) collective-permute-start(bf16[160,128]{1,0:T(8,128)(2,1)S(1)} %get-tuple-element.55), channel_id=1, source_target_pairs={{8,16},{24,32},{40,48},{56,64},{72,80},{88,96},{104,112},{120,128}... | collective-permute-start | bytes 122888 | tf_op jit(solution)/shard_map/ppermute | solution.py:98
  57.2 0.1 collective-permute-done.6.refs_2_
  57.2 4.3 %collective-permute-done.7.refs_3_ = bf16[160,128]{1,0:T(8,128)(2,1)S(1)} collective-permute-done((bf16[160,128]{1,0:T(8,128)(2,1)S(1)}, bf16[160,128]{1,0:T(8,128)(2,1)S(1)}, u32[]{:S(2)}, u32[]{:S(2)}) %collective-permute-start.7) | collective-permute-done | bytes 40992 | tf_op jit(solution)/shard_map/ppermute | solution.py:98
  61.6 0.0 all-to-all-done.1.parts_ref
  61.6 1.4 %shard_map.93 = bf16[16,112,128]{2,1,0:T(8,128)(2,1)} custom-call(s32[3]{0:T(128)S(1)} %pad_add_fusion.place, bf16[8,112,128]{2,1,0:T(8,128)(2,1)S(1)} %all-to-all-done.1.parts_ref), custom_call_target="tpu_custom_call" | custom-call | tf_op jit(solution)/shard_map/pallas_call | solution.py:337
  62.9 5.0 %all-to-all-start.2 = ((bf16[16,112,128]{2,1,0:T(8,128)(2,1)}), bf16[16,112,128]{2,1,0:T(8,128)(2,1)S(1)}, u32[]{:S(2)}, u32[]{:S(2)}) async-start(bf16[16,112,128]{2,1,0:T(8,128)(2,1)} %shard_map.93), calls=%async_computation.2 | async-start | bytes 917504 | tf_op jit(solution)/shard_map/all_to_all | solution.py:347
  68.0 3.4 %shard_map.92 = bf16[2,512,128]{2,1,0:T(8,128)(2,1)} custom-call(s32[2,27]{1,0:T(2,128)S(1)} %bitcast.15, s32[3]{0:T(128)S(1)} %pad_add_fusion.place, bf16[2,512,128]{2,1,0:T(8,128)(2,1)S(1)} %get-tuple-element.45.x_ref.scaled_ref, bf16[3,1152,128]{2,1,0:T(8,128)(2,1)S(1)} %shard_map.85.w_ref, f32[2,512,128]{2,1,0:T(8,128)S(1)} %get-tuple-element.47.pre_grad_ref, ...), custom_call_target="tpu_custom_call" | custom-call | tf_op jit(solution)/shard_map/pallas_call | solution.py:249
  71.3 5.2 %all-to-all-done.2.mine_ref = bf16[16,112,128]{2,1,0:T(8,128)(2,1)S(1)} async-done(((bf16[16,112,128]{2,1,0:T(8,128)(2,1)}), bf16[16,112,128]{2,1,0:T(8,128)(2,1)S(1)}, u32[]{:S(2)}, u32[]{:S(2)}) %all-to-all-start.2) | async-done | bytes 458784 | tf_op jit(solution)/shard_map/all_to_all | solution.py:347
  76.5 4.2 %collective-permute-start.8 = (bf16[16,112,128]{2,1,0:T(8,128)(2,1)S(1)}, bf16[16,112,128]{2,1,0:T(8,128)(2,1)S(1)}, u32[]{:S(2)}, u32[]{:S(2)}) collective-permute-start(bf16[16,112,128]{2,1,0:T(8,128)(2,1)S(1)} %all-to-all-done.2.mine_ref), channel_id=1, source_target_pairs={{0,1},{1,0},{2,3},{3,2},{4,5},{5,4},{6,7},{7,6},{8,9},{9,8},{10,11... | collective-permute-start | bytes 1376264 | tf_op jit(solution)/shard_map/ppermute | solution.py:102
  80.8 1.5 %shard_map.94._ = f32[27,128,128]{2,1,0:T(8,128)} custom-call(s32[3]{0:T(128)S(1)} %pad_add_fusion.place, bf16[16,112,128]{2,1,0:T(8,128)(2,1)S(1)} %all-to-all-done.2.mine_ref), custom_call_target="tpu_custom_call" | custom-call | tf_op jit(solution)/shard_map/pallas_call | solution.py:315
  82.3 0.0 collective-permute-done.8.other_ref
  82.3 1.5 %shard_map.95 = (f32[27,128,128]{2,1,0:T(8,128)}, f32[1,128]{1,0:T(1,128)}) custom-call(s32[3]{0:T(128)S(1)} %pad_add_fusion.place, bf16[16,112,128]{2,1,0:T(8,128)(2,1)S(1)} %all-to-all-done.2.mine_ref, bf16[16,112,128]{2,1,0:T(8,128)(2,1)S(1)} %collective-permute-done.8.other_ref, f32[27,128,128]{2,1,0:T(8,128)} %shard_map.94._), custom_call_target="tpu_custom_call", output_to_operand_aliasing={{0}: (3, {})} | custom-call | tf_op jit(solution)/shard_map/pallas_call | solution.py:323
  (1 shorter events, 0.0 us)
Async XLA Ops:
  0.6 17.5 %copy-start.5 = (f32[128]{0:T(128)S(1)}, f32[128]{0:T(128)}, u32[]{:S(2)}) copy-start(f32[128]{0:T(128)} %param.9) | copy-start | bytes 1540
  0.6 17.5 %copy-start.4 = (s32[1,1,2,27]{3,2,1,0:T(2,128)S(1)}, s32[1,1,2,27]{3,2,1,0:T(2,128)}, u32[]{:S(2)}) copy-start(s32[1,1,2,27]{3,2,1,0:T(2,128)} %param.7) | copy-start | bytes 652
  0.7 1.0 %copy-start.2 = (bf16[1,1,2,512,128]{4,3,2,1,0:T(8,128)(2,1)S(1)}, bf16[1,1,2,512,128]{4,3,2,1,0:T(8,128)(2,1)}, u32[]{:S(2)}) copy-start(bf16[1,1,2,512,128]{4,3,2,1,0:T(8,128)(2,1)} %param.5) | copy-start | bytes 786436
  1.7 12.9 %copy-start.3 = (bf16[1,1,2,512,128]{4,3,2,1,0:T(8,128)(2,1)S(1)}, bf16[1,1,2,512,128]{4,3,2,1,0:T(8,128)(2,1)}, u32[]{:S(2)}) copy-start(bf16[1,1,2,512,128]{4,3,2,1,0:T(8,128)(2,1)} %param.6) | copy-start | bytes 786436
  2.3 7.1 %collective-permute-start = (bf16[128,128]{1,0:T(8,128)(2,1)S(1)}, bf16[128,128]{1,0:T(8,128)(2,1)S(1)}, u32[]{:S(2)}, u32[]{:S(2)}) collective-permute-start(bf16[128,128]{1,0:T(8,128)(2,1)S(1)} %get-tuple-element.35), channel_id=1, source_target_pairs={{0,1},{1,0},{2,3},{3,2},{4,5},{5,4},{6,7},{7,6},{8,9},{9,8},{10,11... | collective-permute-start | bytes 98312 | tf_op jit(solution)/shard_map/ppermute | solution.py:102
  3.0 6.4 %collective-permute-start.1 = (bf16[128,128]{1,0:T(8,128)(2,1)S(1)}, bf16[128,128]{1,0:T(8,128)(2,1)S(1)}, u32[]{:S(2)}, u32[]{:S(2)}) collective-permute-start(bf16[128,128]{1,0:T(8,128)(2,1)S(1)} %get-tuple-element.36), channel_id=1, source_target_pairs={{1,2},{3,4},{5,6},{2,1},{4,3},{6,5},{9,10},{11,12},{13,14},{10,9},... | collective-permute-start | bytes 98312 | tf_op jit(solution)/shard_map/ppermute | solution.py:92
  7.8 1.2 %copy-start = (bf16[27,128,128]{2,1,0:T(8,128)(2,1)S(1)}, bf16[27,128,128]{2,1,0:T(8,128)(2,1)}, u32[]{:S(2)}) copy-start(bf16[27,128,128]{2,1,0:T(8,128)(2,1)} %w_ref.1) | copy-start | bytes 2654212
  9.0 9.1 %copy-start.1 = (bf16[27,128,128]{2,1,0:T(8,128)(2,1)S(1)}, bf16[27,128,128]{2,1,0:T(8,128)(2,1)}, u32[]{:S(2)}) copy-start(bf16[27,128,128]{2,1,0:T(8,128)(2,1)} %w_ref.1) | copy-start | bytes 2654212
  10.0 4.6 %collective-permute-start.2 = (bf16[160,128]{1,0:T(8,128)(2,1)S(1)}, bf16[160,128]{1,0:T(8,128)(2,1)S(1)}, u32[]{:S(2)}, u32[]{:S(2)}) collective-permute-start(bf16[160,128]{1,0:T(8,128)(2,1)S(1)} %get-tuple-element.39), channel_id=1, source_target_pairs={{0,8},{16,24},{32,40},{48,56},{64,72},{80,88},{96,104},{112,120},{... | collective-permute-start | bytes 122888 | tf_op jit(solution)/shard_map/ppermute | solution.py:98
  11.3 6.8 %collective-permute-start.3 = (bf16[160,128]{1,0:T(8,128)(2,1)S(1)}, bf16[160,128]{1,0:T(8,128)(2,1)S(1)}, u32[]{:S(2)}, u32[]{:S(2)}) collective-permute-start(bf16[160,128]{1,0:T(8,128)(2,1)S(1)} %get-tuple-element.40), channel_id=1, source_target_pairs={{8,16},{24,32},{40,48},{56,64},{72,80},{88,96},{104,112},{120,128}... | collective-permute-start | bytes 122888 | tf_op jit(solution)/shard_map/ppermute | solution.py:98
  22.8 2.0 %collective-permute-start.4 = (bf16[1920,128]{1,0:T(8,128)(2,1)S(1)}, bf16[1920,128]{1,0:T(8,128)(2,1)S(1)}, u32[]{:S(2)}, u32[]{:S(2)}) collective-permute-start(bf16[1920,128]{1,0:T(8,128)(2,1)S(1)} %get-tuple-element.49), channel_id=1, source_target_pairs={{0,1},{1,0},{2,3},{3,2},{4,5},{5,4},{6,7},{7,6},{8,9},{9,8},{10,11... | collective-permute-start | bytes 1474568 | tf_op jit(solution)/shard_map/ppermute | solution.py:102
  26.2 16.9 %all-to-all-start = ((bf16[16,112,128]{2,1,0:T(8,128)(2,1)}), bf16[16,112,128]{2,1,0:T(8,128)(2,1)S(1)}, u32[]{:S(2)}, u32[]{:S(2)}) async-start(bf16[16,112,128]{2,1,0:T(8,128)(2,1)} %get-tuple-element.52), calls=%async_computation | async-start | bytes 917504 | tf_op jit(solution)/shard_map/all_to_all | solution.py:347
  32.9 8.1 %collective-permute-start.5 = (bf16[128,128]{1,0:T(8,128)(2,1)S(1)}, bf16[128,128]{1,0:T(8,128)(2,1)S(1)}, u32[]{:S(2)}, u32[]{:S(2)}) collective-permute-start(bf16[128,128]{1,0:T(8,128)(2,1)S(1)} %get-tuple-element.51), channel_id=1, source_target_pairs={{1,2},{3,4},{5,6},{2,1},{4,3},{6,5},{9,10},{11,12},{13,14},{10,9},... | collective-permute-start | bytes 98312 | tf_op jit(solution)/shard_map/ppermute | solution.py:92
  44.4 17.1 %all-to-all-start.1 = ((bf16[8,112,128]{2,1,0:T(8,128)(2,1)}), bf16[8,112,128]{2,1,0:T(8,128)(2,1)S(1)}, u32[]{:S(2)}, u32[]{:S(2)}) async-start(bf16[8,112,128]{2,1,0:T(8,128)(2,1)} %shard_map.91), calls=%async_computation.1 | async-start | bytes 458752 | tf_op jit(solution)/shard_map/all_to_all | solution.py:347
  54.3 2.9 %collective-permute-start.6 = (bf16[160,128]{1,0:T(8,128)(2,1)S(1)}, bf16[160,128]{1,0:T(8,128)(2,1)S(1)}, u32[]{:S(2)}, u32[]{:S(2)}) collective-permute-start(bf16[160,128]{1,0:T(8,128)(2,1)S(1)} %get-tuple-element.54), channel_id=1, source_target_pairs={{0,8},{16,24},{32,40},{48,56},{64,72},{80,88},{96,104},{112,120},{... | collective-permute-start | bytes 122888 | tf_op jit(solution)/shard_map/ppermute | solution.py:98
  54.7 6.9 %collective-permute-start.7 = (bf16[160,128]{1,0:T(8,128)(2,1)S(1)}, bf16[160,128]{1,0:T(8,128)(2,1)S(1)}, u32[]{:S(2)}, u32[]{:S(2)}) collective-permute-start(bf16[160,128]{1,0:T(8,128)(2,1)S(1)} %get-tuple-element.55), channel_id=1, source_target_pairs={{8,16},{24,32},{40,48},{56,64},{72,80},{88,96},{104,112},{120,128}... | collective-permute-start | bytes 122888 | tf_op jit(solution)/shard_map/ppermute | solution.py:98
  62.9 13.6 %all-to-all-start.2 = ((bf16[16,112,128]{2,1,0:T(8,128)(2,1)}), bf16[16,112,128]{2,1,0:T(8,128)(2,1)S(1)}, u32[]{:S(2)}, u32[]{:S(2)}) async-start(bf16[16,112,128]{2,1,0:T(8,128)(2,1)} %shard_map.93), calls=%async_computation.2 | async-start | bytes 917504 | tf_op jit(solution)/shard_map/all_to_all | solution.py:347
  76.5 5.8 %collective-permute-start.8 = (bf16[16,112,128]{2,1,0:T(8,128)(2,1)S(1)}, bf16[16,112,128]{2,1,0:T(8,128)(2,1)S(1)}, u32[]{:S(2)}, u32[]{:S(2)}) collective-permute-start(bf16[16,112,128]{2,1,0:T(8,128)(2,1)S(1)} %all-to-all-done.2.mine_ref), channel_id=1, source_target_pairs={{0,1},{1,0},{2,3},{3,2},{4,5},{5,4},{6,7},{7,6},{8,9},{9,8},{10,11... | collective-permute-start | bytes 1376264 | tf_op jit(solution)/shard_map/ppermute | solution.py:102

commit v4 on v3

--- a/solution.py
+++ b/solution.py
@@ -11,6 +11,7 @@
 EMPTY = 9 * CAP
 HALF = 14
 GAIN_ROW = 16
+PIECES = 2
 CORE, ODD, LAST = 0, 1, 2
 SPLIT = (4, 2, 4, 4, 2)
 AXES = ("y", "zl", "x", "zh", "core")
@@ -24,7 +25,7 @@
     return {-1: (7, 1), 0: (0, 8), 1: (0, 1)}[d]
 
 
-def place(d):
+def span(d):
     return {-1: (0, 1), 0: (1, 8), 1: (9, 1)}[d]
 
 
@@ -46,14 +47,21 @@
     return small(rims_kernel, [plane, plane, BLOCK], 8, place, x)
 
 
-def adjoint_kernel(w_ref, out_ref):
+def matrices_kernel(w_ref, adjoint_ref, ends_ref, adjoint_ends_ref):
     for k in range(27):
-        at = C * (k % 9)
-        out_ref[k // 9, at : at + C] = w_ref[26 - k].astype(f32).T.astype(bf16)
-
-
-def adjoint_of(weights):
-    return small(adjoint_kernel, jax.ShapeDtypeStruct((3, 9 * C, C), bf16), 8, None, weights)
+        a, at = k // 9, C * (k % 9)
+        matrix = w_ref[26 - k].astype(f32).T.astype(bf16)
+        adjoint_ref[a, at : at + C] = matrix
+        if a != 1:
+            column = 0 if a == 0 else C
+            adjoint_ends_ref[at : at + C, column : column + C] = matrix
+            ends_ref[at : at + C, column : column + C] = w_ref[k]
+
+
+def matrices_of(weights):
+    ends = jax.ShapeDtypeStruct((9 * C, 2 * C), bf16)
+    shapes = [jax.ShapeDtypeStruct((3, 9 * C, C), bf16), ends, ends]
+    return small(matrices_kernel, shapes, 8, None, weights)
 
 
 def fetch_kernel(value_ref, out_ref):
@@ -102,12 +110,16 @@
     return lax.ppermute(value, "core", [(0, 1), (1, 0)])
 
 
-def fill_table(place, table, own, halo):
-    near, far, first, second = halo
+def fill_own(place, table, own, near, far):
     table[4 * CAP : 5 * CAP] = own.astype(f32).reshape(CAP, 8, 64, C)
     table[EMPTY] = jnp.zeros((8, 64, C), f32)
     for value, device, y in zip(sides(place[CORE] == 0, near, far), (3, 5), (7, 0)):
         table[device * CAP : (device + 1) * CAP, :, 8 * y : 8 * y + 8] = value.reshape(CAP, 8, 8, C)
+
+
+def fill_table(place, table, own, halo):
+    near, far, first, second = halo
+    fill_own(place, table, own, near, far)
     for value, dx, x in zip(sides(place[ODD] == 0, first, second), (0, 2), (7, 0)):
         wide = value.reshape(CAP, 80, C)
         for dy, at, y, count in ((0, 0, 7, 1), (1, 1, 0, 8), (2, 9, 0, 1)):
@@ -115,13 +127,18 @@
             table[device * CAP : (device + 1) * CAP, x, 8 * y : 8 * (y + count)] = wide[:, 8 * at : 8 * (at + count)]
 
 
-def unfold(codes, table, planes, unfolded):
+ALL = {-1: 0, 0: 1, 1: 9}
+MIDDLE = {0: 0}
+RIM = {-1: 0, 1: 1}
+
+
+def unfold(codes, table, planes, unfolded, places):
     height = lax.broadcasted_iota(jnp.int32, (1, 8, C), 1)
     for s in range(CAP):
-        for a in SIDE:
+        for a, xd in places.items():
             for b in SIDE:
                 (xs, nx), (ys, ny) = rim(a), rim(b)
-                (xd, _), (yd, _) = place(a), place(b)
+                yd, _ = span(b)
                 parts = []
                 for c in SIDE:
                     code = codes[s, 9 * (a + 1) + 3 * (b + 1) + (c + 1)]
@@ -148,20 +165,50 @@
     return jnp.concatenate([*pieces, pair, rows[at + 16 :]], axis=0)
 
 
-def forward_kernel(codes, place, x_ref, dy_ref, w_ref, gain_ref, *refs):
+def middle_kernel(codes, place, x_ref, w_ref, ends_ref, near_ref, far_ref, conv_ref, middle_ref, table, planes):
+    fill_own(place, table, x_ref[...], near_ref, far_ref)
+    unfold(codes, table, planes, middle_ref, MIDDLE)
+    for s in range(CAP):
+        ends = dot_rows(middle_ref[s], ends_ref[...])
+        conv_ref[s] = dot_rows(middle_ref[s], w_ref[1])
+        conv_ref[s, 64:] += ends[:448, :C]
+        conv_ref[s, :448] += ends[64:, C:]
+
+
+def middle(codes, place, x, weights, ends, near, far, keep):
+    vmem = pl.BlockSpec(memory_space=VMEM)
+    smem = pl.BlockSpec(memory_space=pltpu.SMEM)
+    conv = jax.ShapeDtypeStruct((CAP, 512, C), f32)
+    scratch = [VMEM((EMPTY + 1, 8, 64, C), f32), VMEM((3, 8, 80, C), f32)]
+    shape = (CAP, 8, 64, 9 * C)
+    return pl.pallas_call(
+        middle_kernel,
+        out_shape=[conv, jax.ShapeDtypeStruct(shape, bf16)] if keep else [conv],
+        in_specs=[smem] * 2 + [vmem] * 5,
+        out_specs=[vmem] * (2 if keep else 1),
+        scratch_shapes=scratch if keep else [VMEM(shape, bf16), *scratch],
+        compiler_params=pltpu.CompilerParams(vmem_limit_bytes=24 * 2**20),
+    )(codes, place, x, weights, ends, near, far)
+
+
+def dot_rows(planes, matrix):
+    rows = planes.shape[0] * planes.shape[1]
+    return jnp.dot(planes.reshape(rows, planes.shape[2]), matrix, preferred_element_type=f32)
+
+
+def forward_kernel(codes, place, x_ref, dy_ref, w_ref, gain_ref, conv_ref, middle_ref, *refs):
     halo, refs = refs[:4], refs[4:]
     out_ref, pre_grad_ref, scaled_ref, keep_ref, send_ref, far_ref = refs[:6]
-    table, planes, unfolded, shifted, terms, staged, sems = refs[6:]
+    table, planes, rim_planes, conv_all, shifted, shifted_rim, terms, staged, sems = refs[6:]
     fill_table(place, table, x_ref[...], halo)
-    unfold(codes, table, planes, unfolded)
+    unfold(codes, table, planes, rim_planes, RIM)
+    conv_all[...] = conv_ref[...]
+    conv_all[:, :64] += dot_rows(rim_planes[:, 0], w_ref[0]).reshape(CAP, 64, C)
+    conv_all[:, 448:] += dot_rows(rim_planes[:, 1], w_ref[2]).reshape(CAP, 64, C)
     gain = gain_ref[...]
     gain_sum = jnp.zeros((1, C), f32)
     for s in range(CAP):
-        conv = jnp.zeros((512, C), f32)
-        for a in range(3):
-            conv = conv + jnp.dot(
-                unfolded[s, a : a + 8].reshape(512, 9 * C), w_ref[a], preferred_element_type=f32
-            )
+        conv = conv_all[s]
         occupied = codes[s, 13] >= 0
         upstream = jnp.where(occupied, dy_ref[s].astype(f32), 0.0)
         pre_act = jnp.where(occupied, x_ref[s].astype(f32), 0.0) + gain * conv
@@ -173,20 +220,27 @@
         scaled = (gain * pre_grad).astype(bf16)
         scaled_ref[s] = scaled
         gain_sum = gain_sum + jnp.sum(pre_grad * conv, axis=0, keepdims=True)
-        for a in range(3):
-            at = C * a
-            shifted[s, a : a + 8, :, at : at + C] = scaled.reshape(8, 64, C)
-            for x in range(10):
-                if not a <= x < a + 8:
-                    shifted[s, x, :, at : at + C] = jnp.zeros((64, C), bf16)
+        scaled = scaled.reshape(8, 64, C)
+        zero = jnp.zeros((64, C), bf16)
+        shifted[s, :7, :, :C] = scaled[1:]
+        shifted[s, 7, :, :C] = zero
+        shifted[s, :, :, C : 2 * C] = scaled
+        shifted[s, 0, :, 2 * C :] = zero
+        shifted[s, 1:, :, 2 * C :] = scaled[:7]
+        shifted_rim[s] = jnp.zeros((2, 64, 3 * C), bf16)
+        shifted_rim[s, 0, :, :C] = scaled[0]
+        shifted_rim[s, 1, :, 2 * C :] = scaled[7]
     core = place[CORE]
     low, high = y_planes(scaled_ref[...])
     far_ref[...] = jnp.where(core == 0, low, high).astype(bf16)
     send_ref[HALF * C :] = jnp.where(core == 0, high, low).astype(bf16)
-    rhs = shifted[...].reshape(CAP * 640, 3 * C)
+    pairs = ((middle_ref, shifted, CAP * 512), (rim_planes, shifted_rim, CAP * 128))
     for bc in range(9):
-        lhs = unfolded[:, :, :, C * bc : C * bc + C].reshape(CAP * 640, C)
-        term = lax.dot_general(lhs, rhs, (((0,), (0,)), ((), ())), preferred_element_type=f32)
+        term = jnp.zeros((C, 3 * C), f32)
+        for source, target, rows in pairs:
+            lhs = source[:, :, :, C * bc : C * bc + C].reshape(rows, C)
+            rhs = target[...].reshape(rows, 3 * C)
+            term = term + lax.dot_general(lhs, rhs, (((0,), (0,)), ((), ())), preferred_element_type=f32)
         for a in range(3):
             half, block = divmod(9 * a + bc, HALF)
             terms[half, block] = term[:, C * a : C * a + C]
@@ -200,7 +254,7 @@
         pltpu.make_async_copy(staged.at[s], out_ref.at[s], sems.at[s]).wait()
 
 
-def forward(codes, place, x, dy, weights, gain, halo):
+def forward(codes, place, x, dy, weights, gain, conv, unfolded, halo):
     vmem = pl.BlockSpec(memory_space=VMEM)
     smem = pl.BlockSpec(memory_space=pltpu.SMEM)
     return pl.pallas_call(
@@ -213,104 +267,133 @@
             jax.ShapeDtypeStruct((HALF * C + CAP * 64, C), bf16),
             jax.ShapeDtypeStruct((CAP * 64, C), bf16),
         ],
-        in_specs=[smem] * 2 + [vmem] * 8,
+        in_specs=[smem] * 2 + [vmem] * 10,
         out_specs=[pl.BlockSpec(memory_space=pltpu.HBM)] + [vmem] * 5,
         scratch_shapes=[
             VMEM((EMPTY + 1, 8, 64, C), f32),
-            VMEM((3, 10, 80, C), f32),
-            VMEM((CAP, 10, 64, 9 * C), bf16),
-            VMEM((CAP, 10, 64, 3 * C), bf16),
+            VMEM((3, 2, 80, C), f32),
+            VMEM((CAP, 2, 64, 9 * C), bf16),
+            VMEM((CAP, 512, C), f32),
+            VMEM((CAP, 8, 64, 3 * C), bf16),
+            VMEM((CAP, 2, 64, 3 * C), bf16),
             VMEM((2, HALF, C, C), f32),
             VMEM((CAP, 512, C), bf16),
             pltpu.SemaphoreType.DMA((CAP,)),
         ],
-        compiler_params=pltpu.CompilerParams(vmem_limit_bytes=40 * 2**20),
-    )(codes, place, x, dy, weights, gain, *halo)
-
-
-def backward_kernel(codes, place, scaled_ref, w_ref, pre_grad_ref, *refs):
-    halo, (grad_ref, table, planes, unfolded, staged, sems) = refs[:4], refs[4:]
+        compiler_params=pltpu.CompilerParams(vmem_limit_bytes=32 * 2**20),
+    )(codes, place, x, dy, weights, gain, conv, unfolded, *halo)
+
+
+def backward_kernel(codes, place, scaled_ref, w_ref, pre_grad_ref, conv_ref, *refs):
+    halo, (grad_ref, table, planes, rim_planes, staged, total, sems) = refs[:4], refs[4:]
     fill_table(place, table, scaled_ref[...], halo)
-    unfold(codes, table, planes, unfolded)
-    for s in range(CAP):
-        total = pre_grad_ref[s]
-        for a in range(3):
-            total = total + jnp.dot(
-                unfolded[s, a : a + 8].reshape(512, 9 * C), w_ref[a], preferred_element_type=f32
-            )
-        staged[s] = total.astype(bf16)
-        pltpu.make_async_copy(staged.at[s], grad_ref.at[s], sems.at[s]).start()
-    for s in range(CAP):
-        pltpu.make_async_copy(staged.at[s], grad_ref.at[s], sems.at[s]).wait()
-
-
-def backward(codes, place, scaled, weights, pre_grad, halo):
+    unfold(codes, table, planes, rim_planes, RIM)
+    total[...] = pre_grad_ref[...] + conv_ref[...]
+    total[:, :64] += dot_rows(rim_planes[:, 0], w_ref[0]).reshape(CAP, 64, C)
+    total[:, 448:] += dot_rows(rim_planes[:, 1], w_ref[2]).reshape(CAP, 64, C)
+    staged[...] = total[...].astype(bf16)
+    copy = pltpu.make_async_copy(staged, grad_ref, sems)
+    copy.start()
+    copy.wait()
+
+
+def backward(codes, place, scaled, weights, pre_grad, conv, halo):
     vmem = pl.BlockSpec(memory_space=VMEM)
     return pl.pallas_call(
         backward_kernel,
         out_shape=BLOCK,
-        in_specs=[pl.BlockSpec(memory_space=pltpu.SMEM)] * 2 + [vmem] * 7,
+        in_specs=[pl.BlockSpec(memory_space=pltpu.SMEM)] * 2 + [vmem] * 8,
         out_specs=pl.BlockSpec(memory_space=pltpu.HBM),
         scratch_shapes=[
             VMEM((EMPTY + 1, 8, 64, C), f32),
-            VMEM((3, 10, 80, C), f32),
-            VMEM((CAP, 10, 64, 9 * C), bf16),
+            VMEM((3, 2, 80, C), f32),
+            VMEM((CAP, 2, 64, 9 * C), bf16),
             VMEM((CAP, 512, C), bf16),
-            pltpu.SemaphoreType.DMA((CAP,)),
+            VMEM((CAP, 512, C), f32),
+            pltpu.SemaphoreType.DMA,
         ],
-        compiler_params=pltpu.CompilerParams(vmem_limit_bytes=40 * 2**20),
-    )(codes, place, scaled, weights, pre_grad, *halo)
-
-
-def pair_kernel(place, keep_ref, arrived_ref, out_ref, near_ref):
-    total = keep_ref[...] + arrived_ref[: HALF * C].astype(f32)
-    total = split_gain(total, (HALF - 1) * C + GAIN_ROW, place[CORE] == 1)
-    out_ref[...] = total.astype(bf16).reshape(out_ref.shape)
+        compiler_params=pltpu.CompilerParams(vmem_limit_bytes=32 * 2**20),
+    )(codes, place, scaled, weights, pre_grad, conv, *halo)
+
+
+def pair_kernel(place, keep_ref, arrived_ref, out_hbm, near_ref, staged, sems):
     near_ref[...] = arrived_ref[HALF * C :]
+    chunks, rows, _ = staged.shape
+    copies = []
+    for i in range(0, chunks, chunks // PIECES):
+        piece = slice(i, i + chunks // PIECES)
+        flat = slice(i * rows, (i + chunks // PIECES) * rows)
+        total = keep_ref[flat] + arrived_ref[flat].astype(f32)
+        at = (HALF - 1) * C + GAIN_ROW - flat.start
+        if flat.stop == HALF * C:
+            total = split_gain(total, at, place[CORE] == 1)
+        staged[piece] = total.astype(bf16).reshape(chunks // PIECES, rows, C)
+        copies.append(pltpu.make_async_copy(staged.at[piece], out_hbm.at[piece], sems.at[len(copies)]))
+        copies[-1].start()
+    for copy in copies:
+        copy.wait()
+
+
+def pair_sum(place, keep, arrived, chunks):
+    smem, vmem, hbm = (pl.BlockSpec(memory_space=m) for m in (pltpu.SMEM, VMEM, pltpu.HBM))
+    shape = (chunks, HALF * C // chunks, C)
+    return pl.pallas_call(
+        pair_kernel,
+        out_shape=[jax.ShapeDtypeStruct(shape, bf16), jax.ShapeDtypeStruct((CAP * 64, C), bf16)],
+        in_specs=[smem, vmem, vmem],
+        out_specs=[hbm, vmem],
+        scratch_shapes=[VMEM(shape, bf16), pltpu.SemaphoreType.DMA((PIECES,))],
+        compiler_params=pltpu.CompilerParams(vmem_limit_bytes=8 * 2**20),
+    )(place, keep, arrived)
 
 
 def sum_kernel(place, parts_ref, out_ref):
     total = jnp.sum(parts_ref[...].astype(f32), axis=0)
-    rows = total.shape[0]
-    total = split_gain(total, rows - C + GAIN_ROW, place[LAST] == 1)
+    total = split_gain(total, total.shape[0] - C + GAIN_ROW, place[LAST] == 1)
     out_ref[...] = jnp.broadcast_to(total.astype(bf16)[None], out_ref.shape)
 
 
-def write_half(second, rows_ref, weight_ref, staged, sem):
-    staged[...] = rows_ref[...].reshape(HALF, C, C).astype(f32)
-
-    @pl.when(second)
-    def _():
-        copy = pltpu.make_async_copy(staged.at[: HALF - 1], weight_ref.at[HALF:], sem)
-        copy.start()
-        copy.wait()
-
-    @pl.when(jnp.logical_not(second))
-    def _():
-        copy = pltpu.make_async_copy(staged, weight_ref.at[:HALF], sem)
-        copy.start()
-        copy.wait()
-
-
-def mine_kernel(place, mine_ref, weight_ref, staged, sem):
-    write_half(place[CORE] == 1, mine_ref, weight_ref, staged, sem)
-
-
-def other_kernel(place, mine_ref, other_ref, _, weight_ref, gain_hbm, staged, sem, gain_ref, gain_sem):
+def sum_of(place, parts, count):
+    return small(sum_kernel, jax.ShapeDtypeStruct((count, *parts.shape[1:]), bf16), 8, place, parts)
+
+
+def write_half(second, rows_ref, weight_ref, staged, sems):
+    rows = rows_ref[...].reshape(HALF, C, C)
+
+    def copies(at, stop, i):
+        here = slice(at, min(stop, HALF - 1))
+        behind = pltpu.make_async_copy(staged.at[here], weight_ref.at[HALF + at : HALF + here.stop], sems.at[i])
+        return behind, pltpu.make_async_copy(staged.at[at:stop], weight_ref.at[at:stop], sems.at[i])
+
+    pieces = [copies(0, 7, 0), copies(7, HALF, 1)]
+    for i, (behind, ahead) in enumerate(pieces):
+        staged[7 * i : 7 * i + 7] = rows[7 * i : 7 * i + 7].astype(f32)
+        pl.when(second)(behind.start)
+        pl.when(jnp.logical_not(second))(ahead.start)
+    for behind, ahead in pieces:
+        pl.when(second)(behind.wait)
+        pl.when(jnp.logical_not(second))(ahead.wait)
+
+
+def mine_kernel(place, mine_ref, weight_ref, staged, sems):
+    write_half(place[CORE] == 1, mine_ref, weight_ref, staged, sems)
+
+
+def other_kernel(place, mine_ref, other_ref, _, weight_ref, gain_hbm, staged, sems, gain_ref, gain_sem):
     at = (HALF - 1) * C + GAIN_ROW
     mine, other = (ref[...].reshape(HALF * C, C)[at : at + 16].astype(f32) for ref in (mine_ref, other_ref))
     pair = jnp.where(place[CORE] == 1, mine, other)
     gain_ref[...] = pair[:1] + pair[8:9]
     copy = pltpu.make_async_copy(gain_ref, gain_hbm, gain_sem)
     copy.start()
-    write_half(place[CORE] == 0, other_ref, weight_ref, staged, sem)
+    write_half(place[CORE] == 0, other_ref, weight_ref, staged, sems)
     copy.wait()
 
 
 def finish(place, mine, other):
     smem, vmem, hbm = (pl.BlockSpec(memory_space=m) for m in (pltpu.SMEM, VMEM, pltpu.HBM))
     weight_grad = jax.ShapeDtypeStruct((27, C, C), f32)
-    scratch = [VMEM((HALF, C, C), f32), pltpu.SemaphoreType.DMA]
+    scratch = [VMEM((HALF, C, C), f32), pltpu.SemaphoreType.DMA((2,))]
     params = pltpu.CompilerParams(vmem_limit_bytes=8 * 2**20)
     partial = pl.pallas_call(
         mine_kernel,
@@ -351,28 +434,32 @@
     together = lax.optimization_barrier
     plane, line = ("y", "x"), ("zl", "zh")
     n_plane, n_line = lax.axis_size(plane), lax.axis_size(line)
-    rows = HALF * C // n_plane
     core = lax.axis_index("core")
     last = core * (lax.axis_index(plane) == n_plane - 1)
     place = jnp.stack([core, lax.axis_index("x") % 2, last]).astype(jnp.int32)
     codes = neighbours[0, 0]
     near, far, x = rims_of(place, features[0, 0])
-    near, far, adjoint = together((swap_core(near), swap_far(far), adjoint_of(weights)))
+    near, far, (adjoint, ends, adjoint_ends), dy = together(
+        (swap_core(near), swap_far(far), matrices_of(weights), fetch(cotangent[0, 0]))
+    )
     first, second = widen(place, near, far, x)
-    first, second, dy = together((swap_x(first, 0), swap_x(second, 1), fetch(cotangent[0, 0])))
+    matrices = weights.reshape(3, 9 * C, C)
+    conv, unfolded = middle(codes, place, x, matrices, ends, near, far, True)
+    first, second, conv, unfolded = together((swap_x(first, 0), swap_x(second, 1), conv, unfolded))
     halo = (near, far, first, second)
     result, pre_grad, scaled, keep, send, far = forward(
-        codes, place, x, dy, weights.reshape(3, 9 * C, C), channel_gain.reshape(1, C), halo
+        codes, place, x, dy, matrices, channel_gain.reshape(1, C), conv, unfolded, halo
     )
 
-    shapes = [jax.ShapeDtypeStruct((n_plane, rows, C), bf16), jax.ShapeDtypeStruct((CAP * 64, C), bf16)]
-    parts, near = small(pair_kernel, shapes, 8, place, keep, swap_core(send))
+    parts, near = pair_sum(place, keep, swap_core(send), n_plane)
     far, parts = together((swap_far(far), trade(parts, plane)))
     first, second = widen(place, near, far, scaled)
-    parts = small(sum_kernel, jax.ShapeDtypeStruct((n_line, rows, C), bf16), 8, place, parts)
-    first, second, parts = together((swap_x(first, 0), swap_x(second, 1), trade(parts, line)))
-    parts = small(sum_kernel, jax.ShapeDtypeStruct((n_plane, rows, C), bf16), 8, place, parts)
-    grad = backward(codes, place, scaled, adjoint, pre_grad, (near, far, first, second))
+    parts = sum_of(place, parts, n_line)
+    (conv,) = middle(codes, place, scaled, adjoint, adjoint_ends, near, far, False)
+    first, conv, parts = together((swap_x(first, 0), conv, trade(parts, line)))
+    parts = sum_of(place, parts, n_plane)
+    second = swap_x(second, 1)
+    grad = backward(codes, place, scaled, adjoint, pre_grad, conv, (near, far, first, second))
     grad, mine = together((grad, trade(parts, plane)))
     weight_grad, gain_grad = finish(place, mine, swap_core(mine))
     return (result[None, None], grad[None, None], weight_grad, gain_grad.reshape(C))

time: 84.4 us -> 82.8 us (0.981)
  the two profiles are of different devices: /device:TPU:33 before, /device:TPU:39 now
where the time goes in v4:
time: 82.8 us; the launch traced here: 82.2 us
  starting transfers between devices  45.8 us (55%)
  Pallas kernels  18 us (22%)
  waiting for transfers between devices  14.4 us (17%)
  local copies, waits for them, and re-layouts  3.07 us (4%)
  between operations  0.86 us (1%)
    all_to_all x3, starting transfers between devices, trade(): return lax.all_to_all(parts, axes, 0, 0, tiled=True)  21 us
    ppermute x2, starting transfers between devices, swap_far(): lax.ppermute(value, ('zh', 'core'), pairs + [(b, a) for a, b in pairs])  10.6 us
    ppermute x4, starting transfers between devices, swap_x(): return lax.ppermute(value, axes, pairs + [(b, a) for a, b in pairs])  8.01 us
    ppermute x4, waiting for transfers between devices, swap_x(): return lax.ppermute(value, axes, pairs + [(b, a) for a, b in pairs])  6.96 us
    ppermute x3, starting transfers between devices, swap_core(): return lax.ppermute(value, 'core', [(0, 1), (1, 0)])  6.26 us
    pallas_call x7, Pallas kernels, small(): pl.pallas_call(kernel, out_shape=out_shape, in_specs=[pl.BlockSpec(memory...  4.72 us
    pallas_call x2, Pallas kernels, middle(): pl.pallas_call(middle_kernel, out_shape=[conv, jax.ShapeDtypeStruct(shape...  4.17 us
    all_to_all x3, waiting for transfers between devices, trade(): return lax.all_to_all(parts, axes, 0, 0, tiled=True)  3.69 us
  transfers between devices with their start and end apart: 12, of which 5 were waited for; matrix products, arithmetic and copies ran while one was open for 0% of the time, Pallas kernels for 10%

profile of v4, /device:TPU:39, one launch (start us, length us, event | category | flops | bytes accessed | tf_op | source)
XLA Modules:
  0.0 82.2 jit_solution(4983930650545400663)
XLA Ops:
  0.6 0.0 copy-start.4
  0.7 0.1 pad_add_fusion.place
  0.7 0.0 copy-start.2
  0.7 0.9 %copy-done.2 = bf16[1,1,2,512,128]{4,3,2,1,0:T(8,128)(2,1)S(1)} copy-done((bf16[1,1,2,512,128]{4,3,2,1,0:T(8,128)(2,1)S(1)}, bf16[1,1,2,512,128]{4,3,2,1,0:T(8,128)(2,1)}, u32[]{:S(2)}) %copy-start.2) | copy-done | bytes 262168
  1.7 0.6 shard_map.84
  2.3 0.8 collective-permute-start
  3.0 4.8 %collective-permute-start.1 = (bf16[128,128]{1,0:T(8,128)(2,1)S(1)}, bf16[128,128]{1,0:T(8,128)(2,1)S(1)}, u32[]{:S(2)}, u32[]{:S(2)}) collective-permute-start(bf16[128,128]{1,0:T(8,128)(2,1)S(1)} %get-tuple-element.45), channel_id=1, source_target_pairs={{1,2},{3,4},{5,6},{2,1},{4,3},{6,5},{9,10},{11,12},{13,14},{10,9},... | collective-permute-start | bytes 98312 | tf_op jit(solution)/shard_map/ppermute | solution.py:100
  7.8 0.0 copy-start.3
  7.8 0.9 %copy-done.3 = bf16[1,1,2,512,128]{4,3,2,1,0:T(8,128)(2,1)S(1)} copy-done((bf16[1,1,2,512,128]{4,3,2,1,0:T(8,128)(2,1)S(1)}, bf16[1,1,2,512,128]{4,3,2,1,0:T(8,128)(2,1)}, u32[]{:S(2)}) %copy-start.3) | copy-done | bytes 262168
  8.8 0.0 copy-start.5
  8.8 0.0 copy-start
  8.8 1.2 %copy-done = bf16[27,128,128]{2,1,0:T(8,128)(2,1)S(1)} copy-done((bf16[27,128,128]{2,1,0:T(8,128)(2,1)S(1)}, bf16[27,128,128]{2,1,0:T(8,128)(2,1)}, u32[]{:S(2)}) %copy-start) | copy-done | bytes 884760
  10.0 0.0 copy-start.1
  10.0 0.4 shard_map.85
  10.4 0.0 collective-permute-done.near_ref.refs_0_
  10.4 0.0 collective-permute-done.1.far_ref.refs_1_
  10.4 0.6 shard_map.87
  10.9 0.6 collective-permute-start.2
  11.6 3.3 %collective-permute-start.3 = (bf16[160,128]{1,0:T(8,128)(2,1)S(1)}, bf16[160,128]{1,0:T(8,128)(2,1)S(1)}, u32[]{:S(2)}, u32[]{:S(2)}) collective-permute-start(bf16[160,128]{1,0:T(8,128)(2,1)S(1)} %get-tuple-element.53), channel_id=1, source_target_pairs={{8,16},{24,32},{40,48},{56,64},{72,80},{88,96},{104,112},{120,128}... | collective-permute-start | bytes 122888 | tf_op jit(solution)/shard_map/ppermute | solution.py:106
  14.9 0.0 copy-done.4
  14.9 0.0 copy-done.1
  14.9 2.1 %shard_map.88 = (f32[2,512,128]{2,1,0:T(8,128)S(1)}, bf16[2,8,64,1152]{3,2,1,0:T(8,128)(2,1)S(1)}) custom-call(s32[2,27]{1,0:T(2,128)S(1)} %bitcast.15, s32[3]{0:T(128)S(1)} %pad_add_fusion.place, bf16[2,512,128]{2,1,0:T(8,128)(2,1)S(1)} %get-tuple-element.43.x_ref, bf16[3,1152,128]{2,1,0:T(8,128)(2,1)S(1)} %bitcast.11, ...), custom_call_target="tpu_custom_call" | custom-call | tf_op jit(solution)/shard_map/pallas_call | solution.py:184
  17.0 0.0 collective-permute-done.2.refs_2_
  17.0 2.3 %collective-permute-done.3.refs_3_ = bf16[160,128]{1,0:T(8,128)(2,1)S(1)} collective-permute-done((bf16[160,128]{1,0:T(8,128)(2,1)S(1)}, bf16[160,128]{1,0:T(8,128)(2,1)S(1)}, u32[]{:S(2)}, u32[]{:S(2)}) %collective-permute-start.3) | collective-permute-done | bytes 40992 | tf_op jit(solution)/shard_map/ppermute | solution.py:106
  19.3 0.0 copy-done.5
  19.3 3.1 %shard_map.89 = (bf16[2,512,128]{2,1,0:T(8,128)(2,1)}, f32[2,512,128]{2,1,0:T(8,128)S(1)}, bf16[2,512,128]{2,1,0:T(8,128)(2,1)S(1)}, f32[1792,128]{1,0:T(8,128)S...) custom-call(s32[2,27]{1,0:T(2,128)S(1)} %bitcast.16, s32[3]{0:T(128)S(1)} %pad_add_fusion.place, ...), custom_call_target="tpu_custom_call" | custom-call | tf_op jit(solution)/shard_map/pallas_call | solution.py:260
  22.4 0.1 collective-permute-start.4
  22.5 1.9 %collective-permute-done.4.arrived_ref = bf16[1920,128]{1,0:T(8,128)(2,1)S(1)} collective-permute-done((bf16[1920,128]{1,0:T(8,128)(2,1)S(1)}, bf16[1920,128]{1,0:T(8,128)(2,1)S(1)}, u32[]{:S(2)}, u32[]{:S(2)}) %collective-permute-start.4) | collective-permute-done | bytes 491552 | tf_op jit(solution)/shard_map/ppermute | solution.py:110
  24.4 1.4 %shard_map.90 = (bf16[16,112,128]{2,1,0:T(8,128)(2,1)}, bf16[128,128]{1,0:T(8,128)(2,1)S(1)}) custom-call(s32[3]{0:T(128)S(1)} %pad_add_fusion.place, f32[1792,128]{1,0:T(8,128)S(1)} %get-tuple-element.65.keep_ref, bf16[1920,128]{1,0:T(8,128)(2,1)S(1)} %collective-permute-done.4.arrived_ref), custom_call_target="tpu_custom_call" | custom-call | tf_op jit(solution)/shard_map/pallas_call | solution.py:340
  25.7 6.6 %all-to-all-start = ((bf16[16,112,128]{2,1,0:T(8,128)(2,1)}), bf16[16,112,128]{2,1,0:T(8,128)(2,1)S(1)}, u32[]{:S(2)}, u32[]{:S(2)}) async-start(bf16[16,112,128]{2,1,0:T(8,128)(2,1)} %get-tuple-element.69), calls=%async_computation | async-start | bytes 917504 | tf_op jit(solution)/shard_map/all_to_all | solution.py:430
  32.3 5.8 %collective-permute-start.5 = (bf16[128,128]{1,0:T(8,128)(2,1)S(1)}, bf16[128,128]{1,0:T(8,128)(2,1)S(1)}, u32[]{:S(2)}, u32[]{:S(2)}) collective-permute-start(bf16[128,128]{1,0:T(8,128)(2,1)S(1)} %get-tuple-element.68), channel_id=1, source_target_pairs={{1,2},{3,4},{5,6},{2,1},{4,3},{6,5},{9,10},{11,12},{13,14},{10,9},... | collective-permute-start | bytes 98312 | tf_op jit(solution)/shard_map/ppermute | solution.py:100
  38.1 1.9 %collective-permute-done.5.far_ref.refs_1_ = bf16[128,128]{1,0:T(8,128)(2,1)S(1)} collective-permute-done((bf16[128,128]{1,0:T(8,128)(2,1)S(1)}, bf16[128,128]{1,0:T(8,128)(2,1)S(1)}, u32[]{:S(2)}, u32[]{:S(2)}) %collective-permute-start.5) | collective-permute-done | bytes 32800 | tf_op jit(solution)/shard_map/ppermute | solution.py:100
  40.0 0.0 all-to-all-done.parts_ref
  40.0 1.3 %shard_map.93 = bf16[8,112,128]{2,1,0:T(8,128)(2,1)} custom-call(s32[3]{0:T(128)S(1)} %pad_add_fusion.place, bf16[16,112,128]{2,1,0:T(8,128)(2,1)S(1)} %all-to-all-done.parts_ref), custom_call_target="tpu_custom_call" | custom-call | tf_op jit(solution)/shard_map/pallas_call | solution.py:420
  41.3 8.7 %all-to-all-start.1 = ((bf16[8,112,128]{2,1,0:T(8,128)(2,1)}), bf16[8,112,128]{2,1,0:T(8,128)(2,1)S(1)}, u32[]{:S(2)}, u32[]{:S(2)}) async-start(bf16[8,112,128]{2,1,0:T(8,128)(2,1)} %shard_map.93), calls=%async_computation.1 | async-start | bytes 458752 | tf_op jit(solution)/shard_map/all_to_all | solution.py:430
  50.0 0.6 shard_map.91
  50.6 0.8 %collective-permute-start.6 = (bf16[160,128]{1,0:T(8,128)(2,1)S(1)}, bf16[160,128]{1,0:T(8,128)(2,1)S(1)}, u32[]{:S(2)}, u32[]{:S(2)}) collective-permute-start(bf16[160,128]{1,0:T(8,128)(2,1)S(1)} %get-tuple-element.71), channel_id=1, source_target_pairs={{0,8},{16,24},{32,40},{48,56},{64,72},{80,88},{96,104},{112,120},{... | collective-permute-start | bytes 122888 | tf_op jit(solution)/shard_map/ppermute | solution.py:106
  51.4 2.1 %shard_map.92.conv_ref = f32[2,512,128]{2,1,0:T(8,128)S(1)} custom-call(s32[2,27]{1,0:T(2,128)S(1)} %bitcast.17, s32[3]{0:T(128)S(1)} %pad_add_fusion.place, bf16[2,512,128]{2,1,0:T(8,128)(2,1)S(1)} %get-tuple-element.62.x_ref.scaled_ref, bf16[3,1152,128]{2,1,0:T(8,128)(2,1)S(1)} %get-tuple-element.63.w_ref, ...), custom_call_target="tpu_custom_call" | custom-call | tf_op jit(solution)/shard_map/pallas_call | solution.py:184
  53.5 0.0 collective-permute-done.6.refs_2_
  53.5 3.7 %all-to-all-done.1.parts_ref = bf16[8,112,128]{2,1,0:T(8,128)(2,1)S(1)} async-done(((bf16[8,112,128]{2,1,0:T(8,128)(2,1)}), bf16[8,112,128]{2,1,0:T(8,128)(2,1)S(1)}, u32[]{:S(2)}, u32[]{:S(2)}) %all-to-all-start.1) | async-done | bytes 229408 | tf_op jit(solution)/shard_map/all_to_all | solution.py:430
  57.2 1.3 %shard_map.95 = bf16[16,112,128]{2,1,0:T(8,128)(2,1)} custom-call(s32[3]{0:T(128)S(1)} %pad_add_fusion.place, bf16[8,112,128]{2,1,0:T(8,128)(2,1)S(1)} %all-to-all-done.1.parts_ref), custom_call_target="tpu_custom_call" | custom-call | tf_op jit(solution)/shard_map/pallas_call | solution.py:420
  58.6 5.6 %all-to-all-start.2 = ((bf16[16,112,128]{2,1,0:T(8,128)(2,1)}), bf16[16,112,128]{2,1,0:T(8,128)(2,1)S(1)}, u32[]{:S(2)}, u32[]{:S(2)}) async-start(bf16[16,112,128]{2,1,0:T(8,128)(2,1)} %shard_map.95), calls=%async_computation.2 | async-start | bytes 917504 | tf_op jit(solution)/shard_map/all_to_all | solution.py:430
  64.2 3.2 %collective-permute-start.7 = (bf16[160,128]{1,0:T(8,128)(2,1)S(1)}, bf16[160,128]{1,0:T(8,128)(2,1)S(1)}, u32[]{:S(2)}, u32[]{:S(2)}) collective-permute-start(bf16[160,128]{1,0:T(8,128)(2,1)S(1)} %get-tuple-element.76), channel_id=1, source_target_pairs={{8,16},{24,32},{40,48},{56,64},{72,80},{88,96},{104,112},{120,128}... | collective-permute-start | bytes 122888 | tf_op jit(solution)/shard_map/ppermute | solution.py:106
  67.5 4.6 %collective-permute-done.7.refs_3_ = bf16[160,128]{1,0:T(8,128)(2,1)S(1)} collective-permute-done((bf16[160,128]{1,0:T(8,128)(2,1)S(1)}, bf16[160,128]{1,0:T(8,128)(2,1)S(1)}, u32[]{:S(2)}, u32[]{:S(2)}) %collective-permute-start.7) | collective-permute-done | bytes 40992 | tf_op jit(solution)/shard_map/ppermute | solution.py:106
  72.1 1.6 %shard_map.94 = bf16[2,512,128]{2,1,0:T(8,128)(2,1)} custom-call(s32[2,27]{1,0:T(2,128)S(1)} %bitcast.18, s32[3]{0:T(128)S(1)} %pad_add_fusion.place, bf16[2,512,128]{2,1,0:T(8,128)(2,1)S(1)} %get-tuple-element.62.x_ref.scaled_ref, bf16[3,1152,128]{2,1,0:T(8,128)(2,1)S(1)} %get-tuple-element.63.w_ref, f32[2,512,128]{2,1,0:T(8,128)S(1)} %get-tuple-element.64.pre_grad_ref, ...), custom_call_target="tpu_custom_call" | custom-call | tf_op jit(solution)/shard_map/pallas_call | solution.py:302
  73.8 0.0 all-to-all-done.2.mine_ref
  73.8 5.4 %collective-permute-start.8 = (bf16[16,112,128]{2,1,0:T(8,128)(2,1)S(1)}, bf16[16,112,128]{2,1,0:T(8,128)(2,1)S(1)}, u32[]{:S(2)}, u32[]{:S(2)}) collective-permute-start(bf16[16,112,128]{2,1,0:T(8,128)(2,1)S(1)} %all-to-all-done.2.mine_ref), channel_id=1, source_target_pairs={{0,1},{1,0},{2,3},{3,2},{4,5},{5,4},{6,7},{7,6},{8,9},{9,8},{10,11... | collective-permute-start | bytes 1376264 | tf_op jit(solution)/shard_map/ppermute | solution.py:110
  79.2 1.5 %shard_map.96._ = f32[27,128,128]{2,1,0:T(8,128)} custom-call(s32[3]{0:T(128)S(1)} %pad_add_fusion.place, bf16[16,112,128]{2,1,0:T(8,128)(2,1)S(1)} %all-to-all-done.2.mine_ref), custom_call_target="tpu_custom_call" | custom-call | tf_op jit(solution)/shard_map/pallas_call | solution.py:398
  80.7 0.0 collective-permute-done.8.other_ref
  80.7 1.5 %shard_map.97 = (f32[27,128,128]{2,1,0:T(8,128)}, f32[1,128]{1,0:T(1,128)}) custom-call(s32[3]{0:T(128)S(1)} %pad_add_fusion.place, bf16[16,112,128]{2,1,0:T(8,128)(2,1)S(1)} %all-to-all-done.2.mine_ref, bf16[16,112,128]{2,1,0:T(8,128)(2,1)S(1)} %collective-permute-done.8.other_ref, f32[27,128,128]{2,1,0:T(8,128)} %shard_map.96._), custom_call_target="tpu_custom_call", output_to_operand_aliasing={{0}: (3, {})} | custom-call | tf_op jit(solution)/shard_map/pallas_call | solution.py:406
  (1 shorter events, 0.0 us)
Async XLA Ops:
  0.6 14.3 %copy-start.4 = (s32[1,1,2,27]{3,2,1,0:T(2,128)S(1)}, s32[1,1,2,27]{3,2,1,0:T(2,128)}, u32[]{:S(2)}) copy-start(s32[1,1,2,27]{3,2,1,0:T(2,128)} %param.7) | copy-start | bytes 652
  0.7 1.0 %copy-start.2 = (bf16[1,1,2,512,128]{4,3,2,1,0:T(8,128)(2,1)S(1)}, bf16[1,1,2,512,128]{4,3,2,1,0:T(8,128)(2,1)}, u32[]{:S(2)}) copy-start(bf16[1,1,2,512,128]{4,3,2,1,0:T(8,128)(2,1)} %param.5) | copy-start | bytes 786436
  2.3 8.1 %collective-permute-start = (bf16[128,128]{1,0:T(8,128)(2,1)S(1)}, bf16[128,128]{1,0:T(8,128)(2,1)S(1)}, u32[]{:S(2)}, u32[]{:S(2)}) collective-permute-start(bf16[128,128]{1,0:T(8,128)(2,1)S(1)} %get-tuple-element.44), channel_id=1, source_target_pairs={{0,1},{1,0},{2,3},{3,2},{4,5},{5,4},{6,7},{7,6},{8,9},{9,8},{10,11... | collective-permute-start | bytes 98312 | tf_op jit(solution)/shard_map/ppermute | solution.py:110
  3.0 7.3 %collective-permute-start.1 = (bf16[128,128]{1,0:T(8,128)(2,1)S(1)}, bf16[128,128]{1,0:T(8,128)(2,1)S(1)}, u32[]{:S(2)}, u32[]{:S(2)}) collective-permute-start(bf16[128,128]{1,0:T(8,128)(2,1)S(1)} %get-tuple-element.45), channel_id=1, source_target_pairs={{1,2},{3,4},{5,6},{2,1},{4,3},{6,5},{9,10},{11,12},{13,14},{10,9},... | collective-permute-start | bytes 98312 | tf_op jit(solution)/shard_map/ppermute | solution.py:100
  7.8 1.0 %copy-start.3 = (bf16[1,1,2,512,128]{4,3,2,1,0:T(8,128)(2,1)S(1)}, bf16[1,1,2,512,128]{4,3,2,1,0:T(8,128)(2,1)}, u32[]{:S(2)}) copy-start(bf16[1,1,2,512,128]{4,3,2,1,0:T(8,128)(2,1)} %param.6) | copy-start | bytes 786436
  8.8 10.5 %copy-start.5 = (f32[128]{0:T(128)S(1)}, f32[128]{0:T(128)}, u32[]{:S(2)}) copy-start(f32[128]{0:T(128)} %param.9) | copy-start | bytes 1540
  8.8 1.2 %copy-start = (bf16[27,128,128]{2,1,0:T(8,128)(2,1)S(1)}, bf16[27,128,128]{2,1,0:T(8,128)(2,1)}, u32[]{:S(2)}) copy-start(bf16[27,128,128]{2,1,0:T(8,128)(2,1)} %w_ref.1) | copy-start | bytes 2654212
  10.0 4.9 %copy-start.1 = (bf16[27,128,128]{2,1,0:T(8,128)(2,1)S(1)}, bf16[27,128,128]{2,1,0:T(8,128)(2,1)}, u32[]{:S(2)}) copy-start(bf16[27,128,128]{2,1,0:T(8,128)(2,1)} %w_ref.1) | copy-start | bytes 2654212
  10.9 6.1 %collective-permute-start.2 = (bf16[160,128]{1,0:T(8,128)(2,1)S(1)}, bf16[160,128]{1,0:T(8,128)(2,1)S(1)}, u32[]{:S(2)}, u32[]{:S(2)}) collective-permute-start(bf16[160,128]{1,0:T(8,128)(2,1)S(1)} %get-tuple-element.52), channel_id=1, source_target_pairs={{0,8},{16,24},{32,40},{48,56},{64,72},{80,88},{96,104},{112,120},{... | collective-permute-start | bytes 122888 | tf_op jit(solution)/shard_map/ppermute | solution.py:106
  11.6 7.7 %collective-permute-start.3 = (bf16[160,128]{1,0:T(8,128)(2,1)S(1)}, bf16[160,128]{1,0:T(8,128)(2,1)S(1)}, u32[]{:S(2)}, u32[]{:S(2)}) collective-permute-start(bf16[160,128]{1,0:T(8,128)(2,1)S(1)} %get-tuple-element.53), channel_id=1, source_target_pairs={{8,16},{24,32},{40,48},{56,64},{72,80},{88,96},{104,112},{120,128}... | collective-permute-start | bytes 122888 | tf_op jit(solution)/shard_map/ppermute | solution.py:106
  22.4 2.0 %collective-permute-start.4 = (bf16[1920,128]{1,0:T(8,128)(2,1)S(1)}, bf16[1920,128]{1,0:T(8,128)(2,1)S(1)}, u32[]{:S(2)}, u32[]{:S(2)}) collective-permute-start(bf16[1920,128]{1,0:T(8,128)(2,1)S(1)} %get-tuple-element.66), channel_id=1, source_target_pairs={{0,1},{1,0},{2,3},{3,2},{4,5},{5,4},{6,7},{7,6},{8,9},{9,8},{10,11... | collective-permute-start | bytes 1474568 | tf_op jit(solution)/shard_map/ppermute | solution.py:110
  25.7 14.3 %all-to-all-start = ((bf16[16,112,128]{2,1,0:T(8,128)(2,1)}), bf16[16,112,128]{2,1,0:T(8,128)(2,1)S(1)}, u32[]{:S(2)}, u32[]{:S(2)}) async-start(bf16[16,112,128]{2,1,0:T(8,128)(2,1)} %get-tuple-element.69), calls=%async_computation | async-start | bytes 917504 | tf_op jit(solution)/shard_map/all_to_all | solution.py:430
  32.3 7.7 %collective-permute-start.5 = (bf16[128,128]{1,0:T(8,128)(2,1)S(1)}, bf16[128,128]{1,0:T(8,128)(2,1)S(1)}, u32[]{:S(2)}, u32[]{:S(2)}) collective-permute-start(bf16[128,128]{1,0:T(8,128)(2,1)S(1)} %get-tuple-element.68), channel_id=1, source_target_pairs={{1,2},{3,4},{5,6},{2,1},{4,3},{6,5},{9,10},{11,12},{13,14},{10,9},... | collective-permute-start | bytes 98312 | tf_op jit(solution)/shard_map/ppermute | solution.py:100
  41.3 15.9 %all-to-all-start.1 = ((bf16[8,112,128]{2,1,0:T(8,128)(2,1)}), bf16[8,112,128]{2,1,0:T(8,128)(2,1)S(1)}, u32[]{:S(2)}, u32[]{:S(2)}) async-start(bf16[8,112,128]{2,1,0:T(8,128)(2,1)} %shard_map.93), calls=%async_computation.1 | async-start | bytes 458752 | tf_op jit(solution)/shard_map/all_to_all | solution.py:430
  50.6 2.9 %collective-permute-start.6 = (bf16[160,128]{1,0:T(8,128)(2,1)S(1)}, bf16[160,128]{1,0:T(8,128)(2,1)S(1)}, u32[]{:S(2)}, u32[]{:S(2)}) collective-permute-start(bf16[160,128]{1,0:T(8,128)(2,1)S(1)} %get-tuple-element.71), channel_id=1, source_target_pairs={{0,8},{16,24},{32,40},{48,56},{64,72},{80,88},{96,104},{112,120},{... | collective-permute-start | bytes 122888 | tf_op jit(solution)/shard_map/ppermute | solution.py:106
  58.6 15.2 %all-to-all-start.2 = ((bf16[16,112,128]{2,1,0:T(8,128)(2,1)}), bf16[16,112,128]{2,1,0:T(8,128)(2,1)S(1)}, u32[]{:S(2)}, u32[]{:S(2)}) async-start(bf16[16,112,128]{2,1,0:T(8,128)(2,1)} %shard_map.95), calls=%async_computation.2 | async-start | bytes 917504 | tf_op jit(solution)/shard_map/all_to_all | solution.py:430
  64.2 7.9 %collective-permute-start.7 = (bf16[160,128]{1,0:T(8,128)(2,1)S(1)}, bf16[160,128]{1,0:T(8,128)(2,1)S(1)}, u32[]{:S(2)}, u32[]{:S(2)}) collective-permute-start(bf16[160,128]{1,0:T(8,128)(2,1)S(1)} %get-tuple-element.76), channel_id=1, source_target_pairs={{8,16},{24,32},{40,48},{56,64},{72,80},{88,96},{104,112},{120,128}... | collective-permute-start | bytes 122888 | tf_op jit(solution)/shard_map/ppermute | solution.py:106
  73.8 6.9 %collective-permute-start.8 = (bf16[16,112,128]{2,1,0:T(8,128)(2,1)S(1)}, bf16[16,112,128]{2,1,0:T(8,128)(2,1)S(1)}, u32[]{:S(2)}, u32[]{:S(2)}) collective-permute-start(bf16[16,112,128]{2,1,0:T(8,128)(2,1)S(1)} %all-to-all-done.2.mine_ref), channel_id=1, source_target_pairs={{0,1},{1,0},{2,3},{3,2},{4,5},{5,4},{6,7},{7,6},{8,9},{9,8},{10,11... | collective-permute-start | bytes 1376264 | tf_op jit(solution)/shard_map/ppermute | solution.py:110

commit v5 on v4

--- a/solution.py
+++ b/solution.py
@@ -47,9 +47,11 @@
     return small(rims_kernel, [plane, plane, BLOCK], 8, place, x)
 
 
-def matrices_kernel(w_ref, adjoint_ref, ends_ref, adjoint_ends_ref):
+def prepare_kernel(w_ref, codes_ref, w_out, codes_out, adjoint_ref, ends_ref, adjoint_ends_ref):
+    codes_out[...] = codes_ref[...]
     for k in range(27):
         a, at = k // 9, C * (k % 9)
+        w_out[a, at : at + C] = w_ref[k]
         matrix = w_ref[26 - k].astype(f32).T.astype(bf16)
         adjoint_ref[a, at : at + C] = matrix
         if a != 1:
@@ -58,10 +60,11 @@
             ends_ref[at : at + C, column : column + C] = w_ref[k]
 
 
-def matrices_of(weights):
+def prepare(weights, codes):
     ends = jax.ShapeDtypeStruct((9 * C, 2 * C), bf16)
-    shapes = [jax.ShapeDtypeStruct((3, 9 * C, C), bf16), ends, ends]
-    return small(matrices_kernel, shapes, 8, None, weights)
+    matrices = jax.ShapeDtypeStruct((3, 9 * C, C), bf16)
+    shapes = [matrices, jax.ShapeDtypeStruct(codes.shape, codes.dtype), matrices, ends, ends]
+    return small(prepare_kernel, shapes, 8, None, weights, codes)
 
 
 def fetch_kernel(value_ref, out_ref):
@@ -110,16 +113,18 @@
     return lax.ppermute(value, "core", [(0, 1), (1, 0)])
 
 
-def fill_own(place, table, own, near, far):
-    table[4 * CAP : 5 * CAP] = own.astype(f32).reshape(CAP, 8, 64, C)
-    table[EMPTY] = jnp.zeros((8, 64, C), f32)
+def fill_own(place, table, own, near, far, planes):
+    own = own.astype(f32).reshape(CAP, 8, 64, C)
+    for x in planes:
+        table[4 * CAP : 5 * CAP, x] = own[:, x]
+        table[EMPTY, x] = jnp.zeros((64, C), f32)
     for value, device, y in zip(sides(place[CORE] == 0, near, far), (3, 5), (7, 0)):
         table[device * CAP : (device + 1) * CAP, :, 8 * y : 8 * y + 8] = value.reshape(CAP, 8, 8, C)
 
 
 def fill_table(place, table, own, halo):
     near, far, first, second = halo
-    fill_own(place, table, own, near, far)
+    fill_own(place, table, own, near, far, (0, 7))
     for value, dx, x in zip(sides(place[ODD] == 0, first, second), (0, 2), (7, 0)):
         wide = value.reshape(CAP, 80, C)
         for dy, at, y, count in ((0, 0, 7, 1), (1, 1, 0, 8), (2, 9, 0, 1)):
@@ -166,7 +171,7 @@
 
 
 def middle_kernel(codes, place, x_ref, w_ref, ends_ref, near_ref, far_ref, conv_ref, middle_ref, table, planes):
-    fill_own(place, table, x_ref[...], near_ref, far_ref)
+    fill_own(place, table, x_ref[...], near_ref, far_ref, range(8))
     unfold(codes, table, planes, middle_ref, MIDDLE)
     for s in range(CAP):
         ends = dot_rows(middle_ref[s], ends_ref[...])
@@ -199,7 +204,7 @@
 def forward_kernel(codes, place, x_ref, dy_ref, w_ref, gain_ref, conv_ref, middle_ref, *refs):
     halo, refs = refs[:4], refs[4:]
     out_ref, pre_grad_ref, scaled_ref, keep_ref, send_ref, far_ref = refs[:6]
-    table, planes, rim_planes, conv_all, shifted, shifted_rim, terms, staged, sems = refs[6:]
+    table, planes, rim_planes, conv_all, shifted, shifted_rim, staged, sems = refs[6:]
     fill_table(place, table, x_ref[...], halo)
     unfold(codes, table, planes, rim_planes, RIM)
     conv_all[...] = conv_ref[...]
@@ -234,7 +239,21 @@
     low, high = y_planes(scaled_ref[...])
     far_ref[...] = jnp.where(core == 0, low, high).astype(bf16)
     send_ref[HALF * C :] = jnp.where(core == 0, high, low).astype(bf16)
-    pairs = ((middle_ref, shifted, CAP * 512), (rim_planes, shifted_rim, CAP * 128))
+    for own in (0, 1):
+        pl.when(core == own)(
+            lambda own=own: weight_terms(
+                own, gain_sum, ((middle_ref, shifted, CAP * 512), (rim_planes, shifted_rim, CAP * 128)), keep_ref, send_ref
+            )
+        )
+    for s in range(CAP):
+        pltpu.make_async_copy(staged.at[s], out_ref.at[s], sems.at[s]).wait()
+
+
+def weight_terms(own, gain_sum, pairs, keep_ref, send_ref):
+    def put(half, at, value):
+        ref = keep_ref if half == own else send_ref
+        ref[at : at + value.shape[0]] = value.astype(ref.dtype)
+
     for bc in range(9):
         term = jnp.zeros((C, 3 * C), f32)
         for source, target, rows in pairs:
@@ -243,15 +262,11 @@
             term = term + lax.dot_general(lhs, rhs, (((0,), (0,)), ((), ())), preferred_element_type=f32)
         for a in range(3):
             half, block = divmod(9 * a + bc, HALF)
-            terms[half, block] = term[:, C * a : C * a + C]
+            put(half, C * block, term[:, C * a : C * a + C])
     first = jnp.concatenate([gain_sum, jnp.zeros((7, C), f32)], axis=0)
     high = first.astype(bf16).astype(f32)
-    terms[1, HALF - 1] = jnp.zeros((C, C), f32)
-    terms[1, HALF - 1, GAIN_ROW : GAIN_ROW + 16] = jnp.concatenate([high, first - high], axis=0)
-    keep_ref[...] = terms[core].reshape(HALF * C, C)
-    send_ref[: HALF * C] = terms[1 - core].reshape(HALF * C, C).astype(bf16)
-    for s in range(CAP):
-        pltpu.make_async_copy(staged.at[s], out_ref.at[s], sems.at[s]).wait()
+    rows = [jnp.zeros((GAIN_ROW, C), f32), high, first - high, jnp.zeros((C - GAIN_ROW - 16, C), f32)]
+    put(1, C * (HALF - 1), jnp.concatenate(rows, axis=0))
 
 
 def forward(codes, place, x, dy, weights, gain, conv, unfolded, halo):
@@ -276,7 +291,6 @@
             VMEM((CAP, 512, C), f32),
             VMEM((CAP, 8, 64, 3 * C), bf16),
             VMEM((CAP, 2, 64, 3 * C), bf16),
-            VMEM((2, HALF, C, C), f32),
             VMEM((CAP, 512, C), bf16),
             pltpu.SemaphoreType.DMA((CAP,)),
         ],
@@ -357,61 +371,46 @@
     return small(sum_kernel, jax.ShapeDtypeStruct((count, *parts.shape[1:]), bf16), 8, place, parts)
 
 
-def write_half(second, rows_ref, weight_ref, staged, sems):
-    rows = rows_ref[...].reshape(HALF, C, C)
-
-    def copies(at, stop, i):
-        here = slice(at, min(stop, HALF - 1))
-        behind = pltpu.make_async_copy(staged.at[here], weight_ref.at[HALF + at : HALF + here.stop], sems.at[i])
-        return behind, pltpu.make_async_copy(staged.at[at:stop], weight_ref.at[at:stop], sems.at[i])
-
-    pieces = [copies(0, 7, 0), copies(7, HALF, 1)]
-    for i, (behind, ahead) in enumerate(pieces):
-        staged[7 * i : 7 * i + 7] = rows[7 * i : 7 * i + 7].astype(f32)
-        pl.when(second)(behind.start)
-        pl.when(jnp.logical_not(second))(ahead.start)
-    for behind, ahead in pieces:
-        pl.when(second)(behind.wait)
-        pl.when(jnp.logical_not(second))(ahead.wait)
-
-
-def mine_kernel(place, mine_ref, weight_ref, staged, sems):
-    write_half(place[CORE] == 1, mine_ref, weight_ref, staged, sems)
-
-
-def other_kernel(place, mine_ref, other_ref, _, weight_ref, gain_hbm, staged, sems, gain_ref, gain_sem):
+def finish_kernel(place, mine_ref, other_ref, weight_hbm, gain_hbm, staged, sems, gain_ref, gain_sem):
     at = (HALF - 1) * C + GAIN_ROW
-    mine, other = (ref[...].reshape(HALF * C, C)[at : at + 16].astype(f32) for ref in (mine_ref, other_ref))
-    pair = jnp.where(place[CORE] == 1, mine, other)
-    gain_ref[...] = pair[:1] + pair[8:9]
-    copy = pltpu.make_async_copy(gain_ref, gain_hbm, gain_sem)
-    copy.start()
-    write_half(place[CORE] == 0, other_ref, weight_ref, staged, sems)
-    copy.wait()
+    gain_copy = pltpu.make_async_copy(gain_ref, gain_hbm, gain_sem)
+    pieces = ((0, 0, 7), (0, 7, 14), (1, 0, 7), (1, 7, 13))
+    copies = []
+    for i, (half, start, stop) in enumerate(pieces):
+        here = slice(HALF * half + start, HALF * half + stop)
+        copies.append(pltpu.make_async_copy(staged.at[here], weight_hbm.at[here], sems.at[i]))
+
+    def write(halves):
+        pair = halves[1][...].reshape(HALF * C, C)[at : at + 16].astype(f32)
+        gain_ref[...] = pair[:1] + pair[8:9]
+        gain_copy.start()
+        for copy, (half, start, stop) in zip(copies, pieces):
+            rows = halves[half][...].reshape(HALF, C, C)[start:stop]
+            staged[HALF * half + start : HALF * half + stop] = rows.astype(f32)
+            copy.start()
+
+    pl.when(place[CORE] == 0)(lambda: write((mine_ref, other_ref)))
+    pl.when(place[CORE] == 1)(lambda: write((other_ref, mine_ref)))
+    gain_copy.wait()
+    for copy in copies:
+        copy.wait()
 
 
 def finish(place, mine, other):
     smem, vmem, hbm = (pl.BlockSpec(memory_space=m) for m in (pltpu.SMEM, VMEM, pltpu.HBM))
-    weight_grad = jax.ShapeDtypeStruct((27, C, C), f32)
-    scratch = [VMEM((HALF, C, C), f32), pltpu.SemaphoreType.DMA((2,))]
-    params = pltpu.CompilerParams(vmem_limit_bytes=8 * 2**20)
-    partial = pl.pallas_call(
-        mine_kernel,
-        out_shape=weight_grad,
-        in_specs=[smem, vmem],
-        out_specs=hbm,
-        scratch_shapes=scratch,
-        compiler_params=params,
-    )(place, mine)
-    return pl.pallas_call(
-        other_kernel,
-        out_shape=[weight_grad, jax.ShapeDtypeStruct((1, C), f32)],
-        in_specs=[smem, vmem, vmem, hbm],
+    return pl.pallas_call(
+        finish_kernel,
+        out_shape=[jax.ShapeDtypeStruct((27, C, C), f32), jax.ShapeDtypeStruct((1, C), f32)],
+        in_specs=[smem, vmem, vmem],
         out_specs=[hbm, hbm],
-        scratch_shapes=[*scratch, VMEM((1, C), f32), pltpu.SemaphoreType.DMA],
-        input_output_aliases={3: 0},
-        compiler_params=params,
-    )(place, mine, other, partial)
+        scratch_shapes=[
+            VMEM((27, C, C), f32),
+            pltpu.SemaphoreType.DMA((4,)),
+            VMEM((1, C), f32),
+            pltpu.SemaphoreType.DMA,
+        ],
+        compiler_params=pltpu.CompilerParams(vmem_limit_bytes=8 * 2**20),
+    )(place, mine, other)
 
 
 def small(kernel, out_shape, megabytes, scalars, *operands):
@@ -437,15 +436,15 @@
     core = lax.axis_index("core")
     last = core * (lax.axis_index(plane) == n_plane - 1)
     place = jnp.stack([core, lax.axis_index("x") % 2, last]).astype(jnp.int32)
-    codes = neighbours[0, 0]
     near, far, x = rims_of(place, features[0, 0])
-    near, far, (adjoint, ends, adjoint_ends), dy = together(
-        (swap_core(near), swap_far(far), matrices_of(weights), fetch(cotangent[0, 0]))
+    near, far, (matrices, codes, adjoint, ends, adjoint_ends) = together(
+        (swap_core(near), swap_far(far), prepare(weights, neighbours[0, 0]))
     )
     first, second = widen(place, near, far, x)
-    matrices = weights.reshape(3, 9 * C, C)
     conv, unfolded = middle(codes, place, x, matrices, ends, near, far, True)
-    first, second, conv, unfolded = together((swap_x(first, 0), swap_x(second, 1), conv, unfolded))
+    first, second, dy, conv, unfolded = together(
+        (swap_x(first, 0), swap_x(second, 1), fetch(cotangent[0, 0]), conv, unfolded)
+    )
     halo = (near, far, first, second)
     result, pre_grad, scaled, keep, send, far = forward(
         codes, place, x, dy, matrices, channel_gain.reshape(1, C), conv, unfolded, halo
@@ -458,10 +457,10 @@
     (conv,) = middle(codes, place, scaled, adjoint, adjoint_ends, near, far, False)
     first, conv, parts = together((swap_x(first, 0), conv, trade(parts, line)))
     parts = sum_of(place, parts, n_plane)
-    second = swap_x(second, 1)
+    second, mine = together((swap_x(second, 1), trade(parts, plane)))
     grad = backward(codes, place, scaled, adjoint, pre_grad, conv, (near, far, first, second))
-    grad, mine = together((grad, trade(parts, plane)))
-    weight_grad, gain_grad = finish(place, mine, swap_core(mine))
+    grad, other = together((grad, swap_core(mine)))
+    weight_grad, gain_grad = finish(place, mine, other)
     return (result[None, None], grad[None, None], weight_grad, gain_grad.reshape(C))
 
 

time: 82.8 us -> 82.1 us (level)
  the two profiles are of different devices: /device:TPU:39 before, /device:TPU:33 now
where the time goes in v5:
time: 82.1 us; the launch traced here: 81.4 us
  starting transfers between devices  44.5 us (54%)
  Pallas kernels  17 us (21%)
  waiting for transfers between devices  15.2 us (19%)
  local copies, waits for them, and re-layouts  3.74 us (5%)
  between operations  0.84 us (1%)
    all_to_all x3, starting transfers between devices, trade(): return lax.all_to_all(parts, axes, 0, 0, tiled=True)  18.8 us
    ppermute x2, starting transfers between devices, swap_far(): lax.ppermute(value, ('zh', 'core'), pairs + [(b, a) for a, b in pairs])  10.3 us
    ppermute x4, starting transfers between devices, swap_x(): return lax.ppermute(value, axes, pairs + [(b, a) for a, b in pairs])  9.47 us
    all_to_all x3, waiting for transfers between devices, trade(): return lax.all_to_all(parts, axes, 0, 0, tiled=True)  8.29 us
    ppermute x3, starting transfers between devices, swap_core(): return lax.ppermute(value, 'core', [(0, 1), (1, 0)])  5.89 us
    pallas_call x7, Pallas kernels, small(): pl.pallas_call(kernel, out_shape=out_shape, in_specs=[pl.BlockSpec(memory...  4.8 us
    pallas_call x2, Pallas kernels, middle(): pl.pallas_call(middle_kernel, out_shape=[conv, jax.ShapeDtypeStruct(shape...  4.24 us
    unnamed x10, local copies, waits for them, and re-layouts  3.74 us
  transfers between devices with their start and end apart: 12, of which 8 were waited for; matrix products, arithmetic and copies ran while one was open for 0% of the time, Pallas kernels for 8%

profile of v5, /device:TPU:33, one launch (start us, length us, event | category | flops | bytes accessed | tf_op | source)
XLA Modules:
  0.0 81.4 jit_solution(298668419614368766)
XLA Ops:
  0.6 0.0 copy-start.4
  0.7 0.1 pad_add_fusion.place
  0.7 0.0 copy-start.1
  0.7 0.9 %copy-done.1 = bf16[1,1,2,512,128]{4,3,2,1,0:T(8,128)(2,1)S(1)} copy-done((bf16[1,1,2,512,128]{4,3,2,1,0:T(8,128)(2,1)S(1)}, bf16[1,1,2,512,128]{4,3,2,1,0:T(8,128)(2,1)}, u32[]{:S(2)}) %copy-start.1) | copy-done | bytes 262168
  1.7 0.6 shard_map.84
  2.3 0.8 collective-permute-start
  3.0 4.8 %collective-permute-start.1 = (bf16[128,128]{1,0:T(8,128)(2,1)S(1)}, bf16[128,128]{1,0:T(8,128)(2,1)S(1)}, u32[]{:S(2)}, u32[]{:S(2)}) collective-permute-start(bf16[128,128]{1,0:T(8,128)(2,1)S(1)} %get-tuple-element.50), channel_id=1, source_target_pairs={{1,2},{3,4},{5,6},{2,1},{4,3},{6,5},{9,10},{11,12},{13,14},{10,9},... | collective-permute-start | bytes 98312 | tf_op jit(solution)/shard_map/ppermute | solution.py:103
  7.8 0.0 copy-start
  7.8 1.2 %copy-done = bf16[27,128,128]{2,1,0:T(8,128)(2,1)S(1)} copy-done((bf16[27,128,128]{2,1,0:T(8,128)(2,1)S(1)}, bf16[27,128,128]{2,1,0:T(8,128)(2,1)}, u32[]{:S(2)}) %copy-start) | copy-done | bytes 884760
  9.0 0.0 copy-start.3
  9.0 0.7 copy-done.3
  9.7 0.4 shard_map.85
  10.1 0.0 collective-permute-done.near_ref.refs_0_
  10.1 0.0 collective-permute-done.1.far_ref.refs_1_
  10.2 0.6 shard_map.86
  10.7 1.3 %collective-permute-start.2 = (bf16[160,128]{1,0:T(8,128)(2,1)S(1)}, bf16[160,128]{1,0:T(8,128)(2,1)S(1)}, u32[]{:S(2)}, u32[]{:S(2)}) collective-permute-start(bf16[160,128]{1,0:T(8,128)(2,1)S(1)} %get-tuple-element.60), channel_id=1, source_target_pairs={{0,8},{16,24},{32,40},{48,56},{64,72},{80,88},{96,104},{112,120},{... | collective-permute-start | bytes 122888 | tf_op jit(solution)/shard_map/ppermute | solution.py:109
  12.0 3.3 %collective-permute-start.3 = (bf16[160,128]{1,0:T(8,128)(2,1)S(1)}, bf16[160,128]{1,0:T(8,128)(2,1)S(1)}, u32[]{:S(2)}, u32[]{:S(2)}) collective-permute-start(bf16[160,128]{1,0:T(8,128)(2,1)S(1)} %get-tuple-element.61), channel_id=1, source_target_pairs={{8,16},{24,32},{40,48},{56,64},{72,80},{88,96},{104,112},{120,128}... | collective-permute-start | bytes 122888 | tf_op jit(solution)/shard_map/ppermute | solution.py:109
  15.3 0.0 copy-start.2
  15.3 0.9 %copy-done.2 = bf16[1,1,2,512,128]{4,3,2,1,0:T(8,128)(2,1)S(1)} copy-done((bf16[1,1,2,512,128]{4,3,2,1,0:T(8,128)(2,1)S(1)}, bf16[1,1,2,512,128]{4,3,2,1,0:T(8,128)(2,1)}, u32[]{:S(2)}) %copy-start.2) | copy-done | bytes 262168
  16.3 2.2 %shard_map.88 = (f32[2,512,128]{2,1,0:T(8,128)S(1)}, bf16[2,8,64,1152]{3,2,1,0:T(8,128)(2,1)S(1)}) custom-call(s32[2,27]{1,0:T(2,128)S(1)} %get-tuple-element.56.codes, s32[3]{0:T(128)S(1)} %pad_add_fusion.place, bf16[2,512,128]{2,1,0:T(8,128)(2,1)S(1)} %get-tuple-element.57.x_ref, bf16[3,1152,128]{2,1,0:T(8,128)(2,1)S(1)} %get-tuple-element.62.w_ref, ...), custom_call_target="tpu_custom_call" | custom-call | tf_op jit(solution)/shard_map/pallas_call | solution.py:189
  18.4 0.0 collective-permute-done.2.refs_2_
  18.4 0.4 collective-permute-done.3.refs_3_
  18.9 0.0 copy-done.4
  18.9 3.1 %shard_map.89 = (bf16[2,512,128]{2,1,0:T(8,128)(2,1)}, f32[2,512,128]{2,1,0:T(8,128)S(1)}, bf16[2,512,128]{2,1,0:T(8,128)(2,1)S(1)}, f32[1792,128]{1,0:T(8,128)S...) custom-call(s32[2,27]{1,0:T(2,128)S(1)} %get-tuple-element.56.codes, s32[3]{0:T(128)S(1)} %pad_add_fusion.place, ...), custom_call_target="tpu_custom_call" | custom-call | tf_op jit(solution)/shard_map/pallas_call | solution.py:275
  22.0 0.1 collective-permute-start.4
  22.1 1.9 %collective-permute-done.4.arrived_ref = bf16[1920,128]{1,0:T(8,128)(2,1)S(1)} collective-permute-done((bf16[1920,128]{1,0:T(8,128)(2,1)S(1)}, bf16[1920,128]{1,0:T(8,128)(2,1)S(1)}, u32[]{:S(2)}, u32[]{:S(2)}) %collective-permute-start.4) | collective-permute-done | bytes 491552 | tf_op jit(solution)/shard_map/ppermute | solution.py:113
  24.0 1.4 %shard_map.90 = (bf16[16,112,128]{2,1,0:T(8,128)(2,1)}, bf16[128,128]{1,0:T(8,128)(2,1)S(1)}) custom-call(s32[3]{0:T(128)S(1)} %pad_add_fusion.place, f32[1792,128]{1,0:T(8,128)S(1)} %get-tuple-element.75.keep_ref, bf16[1920,128]{1,0:T(8,128)(2,1)S(1)} %collective-permute-done.4.arrived_ref), custom_call_target="tpu_custom_call" | custom-call | tf_op jit(solution)/shard_map/pallas_call | solution.py:354
  25.3 6.7 %all-to-all-start = ((bf16[16,112,128]{2,1,0:T(8,128)(2,1)}), bf16[16,112,128]{2,1,0:T(8,128)(2,1)S(1)}, u32[]{:S(2)}, u32[]{:S(2)}) async-start(bf16[16,112,128]{2,1,0:T(8,128)(2,1)} %get-tuple-element.79), calls=%async_computation | async-start | bytes 917504 | tf_op jit(solution)/shard_map/all_to_all | solution.py:429
  32.1 5.5 %collective-permute-start.5 = (bf16[128,128]{1,0:T(8,128)(2,1)S(1)}, bf16[128,128]{1,0:T(8,128)(2,1)S(1)}, u32[]{:S(2)}, u32[]{:S(2)}) collective-permute-start(bf16[128,128]{1,0:T(8,128)(2,1)S(1)} %get-tuple-element.78), channel_id=1, source_target_pairs={{1,2},{3,4},{5,6},{2,1},{4,3},{6,5},{9,10},{11,12},{13,14},{10,9},... | collective-permute-start | bytes 98312 | tf_op jit(solution)/shard_map/ppermute | solution.py:103
  37.6 1.9 %collective-permute-done.5.far_ref.refs_1_ = bf16[128,128]{1,0:T(8,128)(2,1)S(1)} collective-permute-done((bf16[128,128]{1,0:T(8,128)(2,1)S(1)}, bf16[128,128]{1,0:T(8,128)(2,1)S(1)}, u32[]{:S(2)}, u32[]{:S(2)}) %collective-permute-start.5) | collective-permute-done | bytes 32800 | tf_op jit(solution)/shard_map/ppermute | solution.py:103
  39.5 2.8 %all-to-all-done.parts_ref = bf16[16,112,128]{2,1,0:T(8,128)(2,1)S(1)} async-done(((bf16[16,112,128]{2,1,0:T(8,128)(2,1)}), bf16[16,112,128]{2,1,0:T(8,128)(2,1)S(1)}, u32[]{:S(2)}, u32[]{:S(2)}) %all-to-all-start) | async-done | bytes 458784 | tf_op jit(solution)/shard_map/all_to_all | solution.py:429
  42.3 1.3 %shard_map.93 = bf16[8,112,128]{2,1,0:T(8,128)(2,1)} custom-call(s32[3]{0:T(128)S(1)} %pad_add_fusion.place, bf16[16,112,128]{2,1,0:T(8,128)(2,1)S(1)} %all-to-all-done.parts_ref), custom_call_target="tpu_custom_call" | custom-call | tf_op jit(solution)/shard_map/pallas_call | solution.py:419
  43.6 8.5 %all-to-all-start.1 = ((bf16[8,112,128]{2,1,0:T(8,128)(2,1)}), bf16[8,112,128]{2,1,0:T(8,128)(2,1)S(1)}, u32[]{:S(2)}, u32[]{:S(2)}) async-start(bf16[8,112,128]{2,1,0:T(8,128)(2,1)} %shard_map.93), calls=%async_computation.1 | async-start | bytes 458752 | tf_op jit(solution)/shard_map/all_to_all | solution.py:429
  52.1 0.6 shard_map.91
  52.7 0.4 collective-permute-start.6
  53.1 2.1 %shard_map.92.conv_ref = f32[2,512,128]{2,1,0:T(8,128)S(1)} custom-call(s32[2,27]{1,0:T(2,128)S(1)} %get-tuple-element.56.codes, s32[3]{0:T(128)S(1)} %pad_add_fusion.place, bf16[2,512,128]{2,1,0:T(8,128)(2,1)S(1)} %get-tuple-element.72.x_ref.scaled_ref, bf16[3,1152,128]{2,1,0:T(8,128)(2,1)S(1)} %get-tuple-element.73.w_ref, ...), custom_call_target="tpu_custom_call" | custom-call | tf_op jit(solution)/shard_map/pallas_call | solution.py:189
  55.2 0.5 collective-permute-done.6.refs_2_
  55.6 3.7 %all-to-all-done.1.parts_ref = bf16[8,112,128]{2,1,0:T(8,128)(2,1)S(1)} async-done(((bf16[8,112,128]{2,1,0:T(8,128)(2,1)}), bf16[8,112,128]{2,1,0:T(8,128)(2,1)S(1)}, u32[]{:S(2)}, u32[]{:S(2)}) %all-to-all-start.1) | async-done | bytes 229408 | tf_op jit(solution)/shard_map/all_to_all | solution.py:429
  59.3 1.3 %shard_map.94 = bf16[16,112,128]{2,1,0:T(8,128)(2,1)} custom-call(s32[3]{0:T(128)S(1)} %pad_add_fusion.place, bf16[8,112,128]{2,1,0:T(8,128)(2,1)S(1)} %all-to-all-done.1.parts_ref), custom_call_target="tpu_custom_call" | custom-call | tf_op jit(solution)/shard_map/pallas_call | solution.py:419
  60.7 3.6 %all-to-all-start.2 = ((bf16[16,112,128]{2,1,0:T(8,128)(2,1)}), bf16[16,112,128]{2,1,0:T(8,128)(2,1)S(1)}, u32[]{:S(2)}, u32[]{:S(2)}) async-start(bf16[16,112,128]{2,1,0:T(8,128)(2,1)} %shard_map.94), calls=%async_computation.2 | async-start | bytes 917504 | tf_op jit(solution)/shard_map/all_to_all | solution.py:429
  64.2 4.5 %collective-permute-start.7 = (bf16[160,128]{1,0:T(8,128)(2,1)S(1)}, bf16[160,128]{1,0:T(8,128)(2,1)S(1)}, u32[]{:S(2)}, u32[]{:S(2)}) collective-permute-start(bf16[160,128]{1,0:T(8,128)(2,1)S(1)} %get-tuple-element.86), channel_id=1, source_target_pairs={{8,16},{24,32},{40,48},{56,64},{72,80},{88,96},{104,112},{120,128}... | collective-permute-start | bytes 122888 | tf_op jit(solution)/shard_map/ppermute | solution.py:109
  68.8 2.3 %collective-permute-done.7.refs_3_ = bf16[160,128]{1,0:T(8,128)(2,1)S(1)} collective-permute-done((bf16[160,128]{1,0:T(8,128)(2,1)S(1)}, bf16[160,128]{1,0:T(8,128)(2,1)S(1)}, u32[]{:S(2)}, u32[]{:S(2)}) %collective-permute-start.7) | collective-permute-done | bytes 40992 | tf_op jit(solution)/shard_map/ppermute | solution.py:109
  71.1 1.8 %all-to-all-done.2.mine_ref = bf16[16,112,128]{2,1,0:T(8,128)(2,1)S(1)} async-done(((bf16[16,112,128]{2,1,0:T(8,128)(2,1)}), bf16[16,112,128]{2,1,0:T(8,128)(2,1)S(1)}, u32[]{:S(2)}, u32[]{:S(2)}) %all-to-all-start.2) | async-done | bytes 458784 | tf_op jit(solution)/shard_map/all_to_all | solution.py:429
  72.9 5.0 %collective-permute-start.8 = (bf16[16,112,128]{2,1,0:T(8,128)(2,1)S(1)}, bf16[16,112,128]{2,1,0:T(8,128)(2,1)S(1)}, u32[]{:S(2)}, u32[]{:S(2)}) collective-permute-start(bf16[16,112,128]{2,1,0:T(8,128)(2,1)S(1)} %all-to-all-done.2.mine_ref), channel_id=1, source_target_pairs={{0,1},{1,0},{2,3},{3,2},{4,5},{5,4},{6,7},{7,6},{8,9},{9,8},{10,11... | collective-permute-start | bytes 1376264 | tf_op jit(solution)/shard_map/ppermute | solution.py:113
  77.9 1.6 %shard_map.95 = bf16[2,512,128]{2,1,0:T(8,128)(2,1)} custom-call(s32[2,27]{1,0:T(2,128)S(1)} %get-tuple-element.56.codes, s32[3]{0:T(128)S(1)} %pad_add_fusion.place, bf16[2,512,128]{2,1,0:T(8,128)(2,1)S(1)} %get-tuple-element.72.x_ref.scaled_ref, bf16[3,1152,128]{2,1,0:T(8,128)(2,1)S(1)} %get-tuple-element.73.w_ref, ...), custom_call_target="tpu_custom_call" | custom-call | tf_op jit(solution)/shard_map/pallas_call | solution.py:316
  79.6 0.0 collective-permute-done.8.other_ref
  79.6 1.8 %shard_map.96 = (f32[27,128,128]{2,1,0:T(8,128)}, f32[1,128]{1,0:T(1,128)}) custom-call(s32[3]{0:T(128)S(1)} %pad_add_fusion.place, bf16[16,112,128]{2,1,0:T(8,128)(2,1)S(1)} %all-to-all-done.2.mine_ref, bf16[16,112,128]{2,1,0:T(8,128)(2,1)S(1)} %collective-permute-done.8.other_ref), custom_call_target="tpu_custom_call" | custom-call | tf_op jit(solution)/shard_map/pallas_call | solution.py:401
  (1 shorter events, 0.0 us)
Async XLA Ops:
  0.6 18.2 %copy-start.4 = (f32[128]{0:T(128)S(1)}, f32[128]{0:T(128)}, u32[]{:S(2)}) copy-start(f32[128]{0:T(128)} %param.9) | copy-start | bytes 1540
  0.7 1.0 %copy-start.1 = (bf16[1,1,2,512,128]{4,3,2,1,0:T(8,128)(2,1)S(1)}, bf16[1,1,2,512,128]{4,3,2,1,0:T(8,128)(2,1)}, u32[]{:S(2)}) copy-start(bf16[1,1,2,512,128]{4,3,2,1,0:T(8,128)(2,1)} %param.5) | copy-start | bytes 786436
  2.3 7.9 %collective-permute-start = (bf16[128,128]{1,0:T(8,128)(2,1)S(1)}, bf16[128,128]{1,0:T(8,128)(2,1)S(1)}, u32[]{:S(2)}, u32[]{:S(2)}) collective-permute-start(bf16[128,128]{1,0:T(8,128)(2,1)S(1)} %get-tuple-element.49), channel_id=1, source_target_pairs={{0,1},{1,0},{2,3},{3,2},{4,5},{5,4},{6,7},{7,6},{8,9},{9,8},{10,11... | collective-permute-start | bytes 98312 | tf_op jit(solution)/shard_map/ppermute | solution.py:113
  3.0 7.1 %collective-permute-start.1 = (bf16[128,128]{1,0:T(8,128)(2,1)S(1)}, bf16[128,128]{1,0:T(8,128)(2,1)S(1)}, u32[]{:S(2)}, u32[]{:S(2)}) collective-permute-start(bf16[128,128]{1,0:T(8,128)(2,1)S(1)} %get-tuple-element.50), channel_id=1, source_target_pairs={{1,2},{3,4},{5,6},{2,1},{4,3},{6,5},{9,10},{11,12},{13,14},{10,9},... | collective-permute-start | bytes 98312 | tf_op jit(solution)/shard_map/ppermute | solution.py:103
  7.8 1.2 %copy-start = (bf16[27,128,128]{2,1,0:T(8,128)(2,1)S(1)}, bf16[27,128,128]{2,1,0:T(8,128)(2,1)}, u32[]{:S(2)}) copy-start(bf16[27,128,128]{2,1,0:T(8,128)(2,1)} %w_ref.1) | copy-start | bytes 2654212
  9.0 0.7 copy-start.3
  10.7 7.7 %collective-permute-start.2 = (bf16[160,128]{1,0:T(8,128)(2,1)S(1)}, bf16[160,128]{1,0:T(8,128)(2,1)S(1)}, u32[]{:S(2)}, u32[]{:S(2)}) collective-permute-start(bf16[160,128]{1,0:T(8,128)(2,1)S(1)} %get-tuple-element.60), channel_id=1, source_target_pairs={{0,8},{16,24},{32,40},{48,56},{64,72},{80,88},{96,104},{112,120},{... | collective-permute-start | bytes 122888 | tf_op jit(solution)/shard_map/ppermute | solution.py:109
  12.0 6.8 %collective-permute-start.3 = (bf16[160,128]{1,0:T(8,128)(2,1)S(1)}, bf16[160,128]{1,0:T(8,128)(2,1)S(1)}, u32[]{:S(2)}, u32[]{:S(2)}) collective-permute-start(bf16[160,128]{1,0:T(8,128)(2,1)S(1)} %get-tuple-element.61), channel_id=1, source_target_pairs={{8,16},{24,32},{40,48},{56,64},{72,80},{88,96},{104,112},{120,128}... | collective-permute-start | bytes 122888 | tf_op jit(solution)/shard_map/ppermute | solution.py:109
  15.3 1.0 %copy-start.2 = (bf16[1,1,2,512,128]{4,3,2,1,0:T(8,128)(2,1)S(1)}, bf16[1,1,2,512,128]{4,3,2,1,0:T(8,128)(2,1)}, u32[]{:S(2)}) copy-start(bf16[1,1,2,512,128]{4,3,2,1,0:T(8,128)(2,1)} %param.6) | copy-start | bytes 786436
  22.0 2.0 %collective-permute-start.4 = (bf16[1920,128]{1,0:T(8,128)(2,1)S(1)}, bf16[1920,128]{1,0:T(8,128)(2,1)S(1)}, u32[]{:S(2)}, u32[]{:S(2)}) collective-permute-start(bf16[1920,128]{1,0:T(8,128)(2,1)S(1)} %get-tuple-element.76), channel_id=1, source_target_pairs={{0,1},{1,0},{2,3},{3,2},{4,5},{5,4},{6,7},{7,6},{8,9},{9,8},{10,11... | collective-permute-start | bytes 1474568 | tf_op jit(solution)/shard_map/ppermute | solution.py:113
  25.3 17.0 %all-to-all-start = ((bf16[16,112,128]{2,1,0:T(8,128)(2,1)}), bf16[16,112,128]{2,1,0:T(8,128)(2,1)S(1)}, u32[]{:S(2)}, u32[]{:S(2)}) async-start(bf16[16,112,128]{2,1,0:T(8,128)(2,1)} %get-tuple-element.79), calls=%async_computation | async-start | bytes 917504 | tf_op jit(solution)/shard_map/all_to_all | solution.py:429
  32.1 7.4 %collective-permute-start.5 = (bf16[128,128]{1,0:T(8,128)(2,1)S(1)}, bf16[128,128]{1,0:T(8,128)(2,1)S(1)}, u32[]{:S(2)}, u32[]{:S(2)}) collective-permute-start(bf16[128,128]{1,0:T(8,128)(2,1)S(1)} %get-tuple-element.78), channel_id=1, source_target_pairs={{1,2},{3,4},{5,6},{2,1},{4,3},{6,5},{9,10},{11,12},{13,14},{10,9},... | collective-permute-start | bytes 98312 | tf_op jit(solution)/shard_map/ppermute | solution.py:103
  43.6 15.7 %all-to-all-start.1 = ((bf16[8,112,128]{2,1,0:T(8,128)(2,1)}), bf16[8,112,128]{2,1,0:T(8,128)(2,1)S(1)}, u32[]{:S(2)}, u32[]{:S(2)}) async-start(bf16[8,112,128]{2,1,0:T(8,128)(2,1)} %shard_map.93), calls=%async_computation.1 | async-start | bytes 458752 | tf_op jit(solution)/shard_map/all_to_all | solution.py:429
  52.7 2.9 %collective-permute-start.6 = (bf16[160,128]{1,0:T(8,128)(2,1)S(1)}, bf16[160,128]{1,0:T(8,128)(2,1)S(1)}, u32[]{:S(2)}, u32[]{:S(2)}) collective-permute-start(bf16[160,128]{1,0:T(8,128)(2,1)S(1)} %get-tuple-element.81), channel_id=1, source_target_pairs={{0,8},{16,24},{32,40},{48,56},{64,72},{80,88},{96,104},{112,120},{... | collective-permute-start | bytes 122888 | tf_op jit(solution)/shard_map/ppermute | solution.py:109
  60.7 12.2 %all-to-all-start.2 = ((bf16[16,112,128]{2,1,0:T(8,128)(2,1)}), bf16[16,112,128]{2,1,0:T(8,128)(2,1)S(1)}, u32[]{:S(2)}, u32[]{:S(2)}) async-start(bf16[16,112,128]{2,1,0:T(8,128)(2,1)} %shard_map.94), calls=%async_computation.2 | async-start | bytes 917504 | tf_op jit(solution)/shard_map/all_to_all | solution.py:429
  64.2 6.9 %collective-permute-start.7 = (bf16[160,128]{1,0:T(8,128)(2,1)S(1)}, bf16[160,128]{1,0:T(8,128)(2,1)S(1)}, u32[]{:S(2)}, u32[]{:S(2)}) collective-permute-start(bf16[160,128]{1,0:T(8,128)(2,1)S(1)} %get-tuple-element.86), channel_id=1, source_target_pairs={{8,16},{24,32},{40,48},{56,64},{72,80},{88,96},{104,112},{120,128}... | collective-permute-start | bytes 122888 | tf_op jit(solution)/shard_map/ppermute | solution.py:109
  72.9 6.7 %collective-permute-start.8 = (bf16[16,112,128]{2,1,0:T(8,128)(2,1)S(1)}, bf16[16,112,128]{2,1,0:T(8,128)(2,1)S(1)}, u32[]{:S(2)}, u32[]{:S(2)}) collective-permute-start(bf16[16,112,128]{2,1,0:T(8,128)(2,1)S(1)} %all-to-all-done.2.mine_ref), channel_id=1, source_target_pairs={{0,1},{1,0},{2,3},{3,2},{4,5},{5,4},{6,7},{7,6},{8,9},{9,8},{10,11... | collective-permute-start | bytes 1376264 | tf_op jit(solution)/shard_map/ppermute | solution.py:113

commit v6 on v5

--- a/solution.py
+++ b/solution.py
@@ -29,12 +29,20 @@
     return {-1: (0, 1), 0: (1, 8), 1: (9, 1)}[d]
 
 
+def position():
+    core = lax.axis_index("core")
+    x, y = lax.axis_index("x"), lax.axis_index("y")
+    is_last = (x == lax.axis_size("x") - 1) & (y == lax.axis_size("y") - 1) & (core == 1)
+    return core, lax.rem(x, 2), is_last.astype(jnp.int32)
+
+
 def y_planes(value):
     value = value.astype(f32).reshape(CAP, 8, 8, 8, C)
     return [value[:, :, y].reshape(CAP * 64, C) for y in (0, 7)]
 
 
-def rims_kernel(place, x_ref, near_ref, far_ref, x_out):
+def rims_kernel(x_ref, near_ref, far_ref, x_out):
+    place = position()
     x_out[...] = x_ref[...]
     low, high = y_planes(x_ref[...])
     first = place[CORE] == 0
@@ -42,9 +50,9 @@
     far_ref[...] = jnp.where(first, low, high).astype(bf16)
 
 
-def rims_of(place, x):
+def rims_of(x):
     plane = jax.ShapeDtypeStruct((CAP * 64, C), bf16)
-    return small(rims_kernel, [plane, plane, BLOCK], 8, place, x)
+    return small(rims_kernel, [plane, plane, BLOCK], 8, None, x)
 
 
 def prepare_kernel(w_ref, codes_ref, w_out, codes_out, adjoint_ref, ends_ref, adjoint_ends_ref):
@@ -75,7 +83,8 @@
     return small(fetch_kernel, BLOCK, 8, None, value)
 
 
-def widen_kernel(place, near_ref, far_ref, x_ref, first_ref, second_ref):
+def widen_kernel(near_ref, far_ref, x_ref, first_ref, second_ref):
+    place = position()
     before, after = sides(place[CORE] == 0, near_ref, far_ref)
     wide = []
     for x in (0, 7):
@@ -87,9 +96,9 @@
     second_ref[...] = jnp.where(even, wide[0], wide[1]).astype(bf16)
 
 
-def widen(place, near, far, x):
+def widen(near, far, x):
     shapes = [jax.ShapeDtypeStruct((CAP * 80, C), bf16)] * 2
-    return small(widen_kernel, shapes, 8, place, near, far, x)
+    return small(widen_kernel, shapes, 8, None, near, far, x)
 
 
 def sides(first, one_ref, other_ref):
@@ -170,7 +179,8 @@
     return jnp.concatenate([*pieces, pair, rows[at + 16 :]], axis=0)
 
 
-def middle_kernel(codes, place, x_ref, w_ref, ends_ref, near_ref, far_ref, conv_ref, middle_ref, table, planes):
+def middle_kernel(codes, x_ref, w_ref, ends_ref, near_ref, far_ref, conv_ref, middle_ref, table, planes):
+    place = position()
     fill_own(place, table, x_ref[...], near_ref, far_ref, range(8))
     unfold(codes, table, planes, middle_ref, MIDDLE)
     for s in range(CAP):
@@ -180,7 +190,7 @@
         conv_ref[s, :448] += ends[64:, C:]
 
 
-def middle(codes, place, x, weights, ends, near, far, keep):
+def middle(codes, x, weights, ends, near, far, keep):
     vmem = pl.BlockSpec(memory_space=VMEM)
     smem = pl.BlockSpec(memory_space=pltpu.SMEM)
     conv = jax.ShapeDtypeStruct((CAP, 512, C), f32)
@@ -189,11 +199,11 @@
     return pl.pallas_call(
         middle_kernel,
         out_shape=[conv, jax.ShapeDtypeStruct(shape, bf16)] if keep else [conv],
-        in_specs=[smem] * 2 + [vmem] * 5,
+        in_specs=[smem] + [vmem] * 5,
         out_specs=[vmem] * (2 if keep else 1),
         scratch_shapes=scratch if keep else [VMEM(shape, bf16), *scratch],
         compiler_params=pltpu.CompilerParams(vmem_limit_bytes=24 * 2**20),
-    )(codes, place, x, weights, ends, near, far)
+    )(codes, x, weights, ends, near, far)
 
 
 def dot_rows(planes, matrix):
@@ -201,7 +211,8 @@
     return jnp.dot(planes.reshape(rows, planes.shape[2]), matrix, preferred_element_type=f32)
 
 
-def forward_kernel(codes, place, x_ref, dy_ref, w_ref, gain_ref, conv_ref, middle_ref, *refs):
+def forward_kernel(codes, x_ref, dy_ref, w_ref, gain_ref, conv_ref, middle_ref, *refs):
+    place = position()
     halo, refs = refs[:4], refs[4:]
     out_ref, pre_grad_ref, scaled_ref, keep_ref, send_ref, far_ref = refs[:6]
     table, planes, rim_planes, conv_all, shifted, shifted_rim, staged, sems = refs[6:]
@@ -269,7 +280,7 @@
     put(1, C * (HALF - 1), jnp.concatenate(rows, axis=0))
 
 
-def forward(codes, place, x, dy, weights, gain, conv, unfolded, halo):
+def forward(codes, x, dy, weights, gain, conv, unfolded, halo):
     vmem = pl.BlockSpec(memory_space=VMEM)
     smem = pl.BlockSpec(memory_space=pltpu.SMEM)
     return pl.pallas_call(
@@ -282,7 +293,7 @@
             jax.ShapeDtypeStruct((HALF * C + CAP * 64, C), bf16),
             jax.ShapeDtypeStruct((CAP * 64, C), bf16),
         ],
-        in_specs=[smem] * 2 + [vmem] * 10,
+        in_specs=[smem] + [vmem] * 10,
         out_specs=[pl.BlockSpec(memory_space=pltpu.HBM)] + [vmem] * 5,
         scratch_shapes=[
             VMEM((EMPTY + 1, 8, 64, C), f32),
@@ -295,10 +306,11 @@
             pltpu.SemaphoreType.DMA((CAP,)),
         ],
         compiler_params=pltpu.CompilerParams(vmem_limit_bytes=32 * 2**20),
-    )(codes, place, x, dy, weights, gain, conv, unfolded, *halo)
-
-
-def backward_kernel(codes, place, scaled_ref, w_ref, pre_grad_ref, conv_ref, *refs):
+    )(codes, x, dy, weights, gain, conv, unfolded, *halo)
+
+
+def backward_kernel(codes, scaled_ref, w_ref, pre_grad_ref, conv_ref, *refs):
+    place = position()
     halo, (grad_ref, table, planes, rim_planes, staged, total, sems) = refs[:4], refs[4:]
     fill_table(place, table, scaled_ref[...], halo)
     unfold(codes, table, planes, rim_planes, RIM)
@@ -311,12 +323,12 @@
     copy.wait()
 
 
-def backward(codes, place, scaled, weights, pre_grad, conv, halo):
+def backward(codes, scaled, weights, pre_grad, conv, halo):
     vmem = pl.BlockSpec(memory_space=VMEM)
     return pl.pallas_call(
         backward_kernel,
         out_shape=BLOCK,
-        in_specs=[pl.BlockSpec(memory_space=pltpu.SMEM)] * 2 + [vmem] * 8,
+        in_specs=[pl.BlockSpec(memory_space=pltpu.SMEM)] + [vmem] * 8,
         out_specs=pl.BlockSpec(memory_space=pltpu.HBM),
         scratch_shapes=[
             VMEM((EMPTY + 1, 8, 64, C), f32),
@@ -327,10 +339,11 @@
             pltpu.SemaphoreType.DMA,
         ],
         compiler_params=pltpu.CompilerParams(vmem_limit_bytes=32 * 2**20),
-    )(codes, place, scaled, weights, pre_grad, conv, *halo)
-
-
-def pair_kernel(place, keep_ref, arrived_ref, out_hbm, near_ref, staged, sems):
+    )(codes, scaled, weights, pre_grad, conv, *halo)
+
+
+def pair_kernel(keep_ref, arrived_ref, out_hbm, near_ref, staged, sems):
+    place = position()
     near_ref[...] = arrived_ref[HALF * C :]
     chunks, rows, _ = staged.shape
     copies = []
@@ -348,30 +361,32 @@
         copy.wait()
 
 
-def pair_sum(place, keep, arrived, chunks):
+def pair_sum(keep, arrived, chunks):
     smem, vmem, hbm = (pl.BlockSpec(memory_space=m) for m in (pltpu.SMEM, VMEM, pltpu.HBM))
     shape = (chunks, HALF * C // chunks, C)
     return pl.pallas_call(
         pair_kernel,
         out_shape=[jax.ShapeDtypeStruct(shape, bf16), jax.ShapeDtypeStruct((CAP * 64, C), bf16)],
-        in_specs=[smem, vmem, vmem],
+        in_specs=[vmem, vmem],
         out_specs=[hbm, vmem],
         scratch_shapes=[VMEM(shape, bf16), pltpu.SemaphoreType.DMA((PIECES,))],
         compiler_params=pltpu.CompilerParams(vmem_limit_bytes=8 * 2**20),
-    )(place, keep, arrived)
-
-
-def sum_kernel(place, parts_ref, out_ref):
+    )(keep, arrived)
+
+
+def sum_kernel(parts_ref, out_ref):
+    place = position()
     total = jnp.sum(parts_ref[...].astype(f32), axis=0)
     total = split_gain(total, total.shape[0] - C + GAIN_ROW, place[LAST] == 1)
     out_ref[...] = jnp.broadcast_to(total.astype(bf16)[None], out_ref.shape)
 
 
-def sum_of(place, parts, count):
-    return small(sum_kernel, jax.ShapeDtypeStruct((count, *parts.shape[1:]), bf16), 8, place, parts)
-
-
-def finish_kernel(place, mine_ref, other_ref, weight_hbm, gain_hbm, staged, sems, gain_ref, gain_sem):
+def sum_of(parts, count):
+    return small(sum_kernel, jax.ShapeDtypeStruct((count, *parts.shape[1:]), bf16), 8, None, parts)
+
+
+def finish_kernel(mine_ref, other_ref, weight_hbm, gain_hbm, staged, sems, gain_ref, gain_sem):
+    place = position()
     at = (HALF - 1) * C + GAIN_ROW
     gain_copy = pltpu.make_async_copy(gain_ref, gain_hbm, gain_sem)
     pieces = ((0, 0, 7), (0, 7, 14), (1, 0, 7), (1, 7, 13))
@@ -396,12 +411,12 @@
         copy.wait()
 
 
-def finish(place, mine, other):
+def finish(mine, other):
     smem, vmem, hbm = (pl.BlockSpec(memory_space=m) for m in (pltpu.SMEM, VMEM, pltpu.HBM))
     return pl.pallas_call(
         finish_kernel,
         out_shape=[jax.ShapeDtypeStruct((27, C, C), f32), jax.ShapeDtypeStruct((1, C), f32)],
-        in_specs=[smem, vmem, vmem],
+        in_specs=[vmem, vmem],
         out_specs=[hbm, hbm],
         scratch_shapes=[
             VMEM((27, C, C), f32),
@@ -410,7 +425,7 @@
             pltpu.SemaphoreType.DMA,
         ],
         compiler_params=pltpu.CompilerParams(vmem_limit_bytes=8 * 2**20),
-    )(place, mine, other)
+    )(mine, other)
 
 
 def small(kernel, out_shape, megabytes, scalars, *operands):
@@ -433,34 +448,31 @@
     together = lax.optimization_barrier
     plane, line = ("y", "x"), ("zl", "zh")
     n_plane, n_line = lax.axis_size(plane), lax.axis_size(line)
-    core = lax.axis_index("core")
-    last = core * (lax.axis_index(plane) == n_plane - 1)
-    place = jnp.stack([core, lax.axis_index("x") % 2, last]).astype(jnp.int32)
-    near, far, x = rims_of(place, features[0, 0])
+    near, far, x = rims_of(features[0, 0])
     near, far, (matrices, codes, adjoint, ends, adjoint_ends) = together(
         (swap_core(near), swap_far(far), prepare(weights, neighbours[0, 0]))
     )
-    first, second = widen(place, near, far, x)
-    conv, unfolded = middle(codes, place, x, matrices, ends, near, far, True)
+    first, second = widen(near, far, x)
+    conv, unfolded = middle(codes, x, matrices, ends, near, far, True)
     first, second, dy, conv, unfolded = together(
         (swap_x(first, 0), swap_x(second, 1), fetch(cotangent[0, 0]), conv, unfolded)
     )
     halo = (near, far, first, second)
     result, pre_grad, scaled, keep, send, far = forward(
-        codes, place, x, dy, matrices, channel_gain.reshape(1, C), conv, unfolded, halo
+        codes, x, dy, matrices, channel_gain.reshape(1, C), conv, unfolded, halo
     )
 
-    parts, near = pair_sum(place, keep, swap_core(send), n_plane)
+    parts, near = pair_sum(keep, swap_core(send), n_plane)
     far, parts = together((swap_far(far), trade(parts, plane)))
-    first, second = widen(place, near, far, scaled)
-    parts = sum_of(place, parts, n_line)
-    (conv,) = middle(codes, place, scaled, adjoint, adjoint_ends, near, far, False)
+    first, second = widen(near, far, scaled)
+    parts = sum_of(parts, n_line)
+    (conv,) = middle(codes, scaled, adjoint, adjoint_ends, near, far, False)
     first, conv, parts = together((swap_x(first, 0), conv, trade(parts, line)))
-    parts = sum_of(place, parts, n_plane)
+    parts = sum_of(parts, n_plane)
     second, mine = together((swap_x(second, 1), trade(parts, plane)))
-    grad = backward(codes, place, scaled, adjoint, pre_grad, conv, (near, far, first, second))
+    grad = backward(codes, scaled, adjoint, pre_grad, conv, (near, far, first, second))
     grad, other = together((grad, swap_core(mine)))
-    weight_grad, gain_grad = finish(place, mine, other)
+    weight_grad, gain_grad = finish(mine, other)
     return (result[None, None], grad[None, None], weight_grad, gain_grad.reshape(C))
 
 

time: 82.1 us -> 78.8 us (0.960)
  Pallas kernels: 17 us -> 13.2 us
    pallas_call x7, Pallas kernels: 4.8 us -> 2.11 us  [small(): pl.pallas_call(kernel, out_shape=out_shape, in_specs=[pl.BlockSpec(memory...]
where the time goes in v6:
time: 78.8 us; the launch traced here: 78.1 us
  starting transfers between devices  44.5 us (56%)
  waiting for transfers between devices  15.8 us (20%)
  Pallas kernels  13.2 us (17%)
  local copies, waits for them, and re-layouts  3.74 us (5%)
  between operations  0.83 us (1%)
    all_to_all x3, starting transfers between devices, trade(): return lax.all_to_all(parts, axes, 0, 0, tiled=True)  18.8 us
    ppermute x2, starting transfers between devices, swap_far(): lax.ppermute(value, ('zh', 'core'), pairs + [(b, a) for a, b in pairs])  10.3 us
    ppermute x4, starting transfers between devices, swap_x(): return lax.ppermute(value, axes, pairs + [(b, a) for a, b in pairs])  9.47 us
    all_to_all x3, waiting for transfers between devices, trade(): return lax.all_to_all(parts, axes, 0, 0, tiled=True)  8.84 us
    ppermute x3, starting transfers between devices, swap_core(): return lax.ppermute(value, 'core', [(0, 1), (1, 0)])  5.89 us
    pallas_call x2, Pallas kernels, middle(): pl.pallas_call(middle_kernel, out_shape=[conv, jax.ShapeDtypeStruct(shape...  4.21 us
    unnamed x10, local copies, waits for them, and re-layouts  3.74 us
    ppermute x4, waiting for transfers between devices, swap_x(): return lax.ppermute(value, axes, pairs + [(b, a) for a, b in pairs])  3.24 us
  transfers between devices with their start and end apart: 12, of which 8 were waited for; matrix products, arithmetic and copies ran while one was open for 0% of the time, Pallas kernels for 8%

profile of v6, /device:TPU:33, one launch (start us, length us, event | category | flops | bytes accessed | tf_op | source)
XLA Modules:
  0.0 78.1 jit_solution(3325680237037979199)
XLA Ops:
  0.6 0.0 copy-start.4
  0.6 0.0 copy-start.1
  0.7 0.9 %copy-done.1 = bf16[1,1,2,512,128]{4,3,2,1,0:T(8,128)(2,1)S(1)} copy-done((bf16[1,1,2,512,128]{4,3,2,1,0:T(8,128)(2,1)S(1)}, bf16[1,1,2,512,128]{4,3,2,1,0:T(8,128)(2,1)}, u32[]{:S(2)}) %copy-start.1) | copy-done | bytes 262168
  1.6 0.8 collective-permute-start
  2.4 4.8 %collective-permute-start.1 = (bf16[128,128]{1,0:T(8,128)(2,1)S(1)}, bf16[128,128]{1,0:T(8,128)(2,1)S(1)}, u32[]{:S(2)}, u32[]{:S(2)}) collective-permute-start(bf16[128,128]{1,0:T(8,128)(2,1)S(1)} %get-tuple-element.50), channel_id=1, source_target_pairs={{1,2},{3,4},{5,6},{2,1},{4,3},{6,5},{9,10},{11,12},{13,14},{10,9},... | collective-permute-start | bytes 98312 | tf_op jit(solution)/shard_map/ppermute | solution.py:112
  7.2 0.0 copy-start
  7.2 1.2 %copy-done = bf16[27,128,128]{2,1,0:T(8,128)(2,1)S(1)} copy-done((bf16[27,128,128]{2,1,0:T(8,128)(2,1)S(1)}, bf16[27,128,128]{2,1,0:T(8,128)(2,1)}, u32[]{:S(2)}) %copy-start) | copy-done | bytes 884760
  8.4 0.0 copy-start.3
  8.4 0.7 copy-done.3
  9.0 0.4 shard_map.85
  9.5 0.0 collective-permute-done.near_ref.refs_0_
  9.5 0.0 collective-permute-done.1.far_ref.refs_1_
  9.6 1.3 %collective-permute-start.2 = (bf16[160,128]{1,0:T(8,128)(2,1)S(1)}, bf16[160,128]{1,0:T(8,128)(2,1)S(1)}, u32[]{:S(2)}, u32[]{:S(2)}) collective-permute-start(bf16[160,128]{1,0:T(8,128)(2,1)S(1)} %get-tuple-element.60), channel_id=1, source_target_pairs={{0,8},{16,24},{32,40},{48,56},{64,72},{80,88},{96,104},{112,120},{... | collective-permute-start | bytes 122888 | tf_op jit(solution)/shard_map/ppermute | solution.py:118
  10.9 3.3 %collective-permute-start.3 = (bf16[160,128]{1,0:T(8,128)(2,1)S(1)}, bf16[160,128]{1,0:T(8,128)(2,1)S(1)}, u32[]{:S(2)}, u32[]{:S(2)}) collective-permute-start(bf16[160,128]{1,0:T(8,128)(2,1)S(1)} %get-tuple-element.61), channel_id=1, source_target_pairs={{8,16},{24,32},{40,48},{56,64},{72,80},{88,96},{104,112},{120,128}... | collective-permute-start | bytes 122888 | tf_op jit(solution)/shard_map/ppermute | solution.py:118
  14.1 0.0 copy-start.2
  14.1 0.9 %copy-done.2 = bf16[1,1,2,512,128]{4,3,2,1,0:T(8,128)(2,1)S(1)} copy-done((bf16[1,1,2,512,128]{4,3,2,1,0:T(8,128)(2,1)S(1)}, bf16[1,1,2,512,128]{4,3,2,1,0:T(8,128)(2,1)}, u32[]{:S(2)}) %copy-start.2) | copy-done | bytes 262168
  15.1 2.1 %shard_map.88 = (f32[2,512,128]{2,1,0:T(8,128)S(1)}, bf16[2,8,64,1152]{3,2,1,0:T(8,128)(2,1)S(1)}) custom-call(s32[2,27]{1,0:T(2,128)S(1)} %get-tuple-element.56.codes, bf16[2,512,128]{2,1,0:T(8,128)(2,1)S(1)} %get-tuple-element.57.x_ref, bf16[3,1152,128]{2,1,0:T(8,128)(2,1)S(1)} %get-tuple-element.62.w_ref, ...), custom_call_target="tpu_custom_call" | custom-call | tf_op jit(solution)/shard_map/pallas_call | solution.py:199
  17.2 0.0 collective-permute-done.2.refs_2_
  17.2 0.5 collective-permute-done.3.refs_3_
  17.7 0.0 copy-done.4
  17.7 3.2 %shard_map.89 = (bf16[2,512,128]{2,1,0:T(8,128)(2,1)}, f32[2,512,128]{2,1,0:T(8,128)S(1)}, bf16[2,512,128]{2,1,0:T(8,128)(2,1)S(1)}, f32[1792,128]{1,0:T(8,128)S...) custom-call(s32[2,27]{1,0:T(2,128)S(1)} %get-tuple-element.56.codes, ...), custom_call_target="tpu_custom_call" | custom-call | tf_op jit(solution)/shard_map/pallas_call | solution.py:286
  20.9 0.1 collective-permute-start.4
  21.0 1.9 %collective-permute-done.4.arrived_ref = bf16[1920,128]{1,0:T(8,128)(2,1)S(1)} collective-permute-done((bf16[1920,128]{1,0:T(8,128)(2,1)S(1)}, bf16[1920,128]{1,0:T(8,128)(2,1)S(1)}, u32[]{:S(2)}, u32[]{:S(2)}) %collective-permute-start.4) | collective-permute-done | bytes 491552 | tf_op jit(solution)/shard_map/ppermute | solution.py:122
  22.8 0.8 %shard_map.90 = (bf16[16,112,128]{2,1,0:T(8,128)(2,1)}, bf16[128,128]{1,0:T(8,128)(2,1)S(1)}) custom-call(f32[1792,128]{1,0:T(8,128)S(1)} %get-tuple-element.75.keep_ref, bf16[1920,128]{1,0:T(8,128)(2,1)S(1)} %collective-permute-done.4.arrived_ref), custom_call_target="tpu_custom_call" | custom-call | tf_op jit(solution)/shard_map/pallas_call | solution.py:367
  23.7 6.7 %all-to-all-start = ((bf16[16,112,128]{2,1,0:T(8,128)(2,1)}), bf16[16,112,128]{2,1,0:T(8,128)(2,1)S(1)}, u32[]{:S(2)}, u32[]{:S(2)}) async-start(bf16[16,112,128]{2,1,0:T(8,128)(2,1)} %get-tuple-element.79), calls=%async_computation | async-start | bytes 917504 | tf_op jit(solution)/shard_map/all_to_all | solution.py:444
  30.4 5.5 %collective-permute-start.5 = (bf16[128,128]{1,0:T(8,128)(2,1)S(1)}, bf16[128,128]{1,0:T(8,128)(2,1)S(1)}, u32[]{:S(2)}, u32[]{:S(2)}) collective-permute-start(bf16[128,128]{1,0:T(8,128)(2,1)S(1)} %get-tuple-element.78), channel_id=1, source_target_pairs={{1,2},{3,4},{5,6},{2,1},{4,3},{6,5},{9,10},{11,12},{13,14},{10,9},... | collective-permute-start | bytes 98312 | tf_op jit(solution)/shard_map/ppermute | solution.py:112
  35.9 1.9 %collective-permute-done.5.far_ref.refs_1_ = bf16[128,128]{1,0:T(8,128)(2,1)S(1)} collective-permute-done((bf16[128,128]{1,0:T(8,128)(2,1)S(1)}, bf16[128,128]{1,0:T(8,128)(2,1)S(1)}, u32[]{:S(2)}, u32[]{:S(2)}) %collective-permute-start.5) | collective-permute-done | bytes 32800 | tf_op jit(solution)/shard_map/ppermute | solution.py:112
  37.8 2.8 %all-to-all-done.parts_ref = bf16[16,112,128]{2,1,0:T(8,128)(2,1)S(1)} async-done(((bf16[16,112,128]{2,1,0:T(8,128)(2,1)}), bf16[16,112,128]{2,1,0:T(8,128)(2,1)S(1)}, u32[]{:S(2)}, u32[]{:S(2)}) %all-to-all-start) | async-done | bytes 458784 | tf_op jit(solution)/shard_map/all_to_all | solution.py:444
  40.6 0.8 shard_map.93
  41.4 8.5 %all-to-all-start.1 = ((bf16[8,112,128]{2,1,0:T(8,128)(2,1)}), bf16[8,112,128]{2,1,0:T(8,128)(2,1)S(1)}, u32[]{:S(2)}, u32[]{:S(2)}) async-start(bf16[8,112,128]{2,1,0:T(8,128)(2,1)} %shard_map.93), calls=%async_computation.1 | async-start | bytes 458752 | tf_op jit(solution)/shard_map/all_to_all | solution.py:444
  49.9 0.4 collective-permute-start.6
  50.3 2.1 %shard_map.92.conv_ref = f32[2,512,128]{2,1,0:T(8,128)S(1)} custom-call(s32[2,27]{1,0:T(2,128)S(1)} %get-tuple-element.56.codes, bf16[2,512,128]{2,1,0:T(8,128)(2,1)S(1)} %get-tuple-element.72.x_ref.scaled_ref, bf16[3,1152,128]{2,1,0:T(8,128)(2,1)S(1)} %get-tuple-element.73.w_ref, bf16[1152,256]{1,0:T(8,128)(2,1)S(1)} %get-tuple-element.82.ends_ref, ...), custom_call_target="tpu_custom_call" | custom-call | tf_op jit(solution)/shard_map/pallas_call | solution.py:199
  52.4 0.5 collective-permute-done.6.refs_2_
  52.9 4.2 %all-to-all-done.1.parts_ref = bf16[8,112,128]{2,1,0:T(8,128)(2,1)S(1)} async-done(((bf16[8,112,128]{2,1,0:T(8,128)(2,1)}), bf16[8,112,128]{2,1,0:T(8,128)(2,1)S(1)}, u32[]{:S(2)}, u32[]{:S(2)}) %all-to-all-start.1) | async-done | bytes 229408 | tf_op jit(solution)/shard_map/all_to_all | solution.py:444
  57.1 0.8 %shard_map.94 = bf16[16,112,128]{2,1,0:T(8,128)(2,1)} custom-call(bf16[8,112,128]{2,1,0:T(8,128)(2,1)S(1)} %all-to-all-done.1.parts_ref), custom_call_target="tpu_custom_call" | custom-call | tf_op jit(solution)/shard_map/pallas_call | solution.py:434
  57.9 3.6 %all-to-all-start.2 = ((bf16[16,112,128]{2,1,0:T(8,128)(2,1)}), bf16[16,112,128]{2,1,0:T(8,128)(2,1)S(1)}, u32[]{:S(2)}, u32[]{:S(2)}) async-start(bf16[16,112,128]{2,1,0:T(8,128)(2,1)} %shard_map.94), calls=%async_computation.2 | async-start | bytes 917504 | tf_op jit(solution)/shard_map/all_to_all | solution.py:444
  61.5 4.5 %collective-permute-start.7 = (bf16[160,128]{1,0:T(8,128)(2,1)S(1)}, bf16[160,128]{1,0:T(8,128)(2,1)S(1)}, u32[]{:S(2)}, u32[]{:S(2)}) collective-permute-start(bf16[160,128]{1,0:T(8,128)(2,1)S(1)} %get-tuple-element.86), channel_id=1, source_target_pairs={{8,16},{24,32},{40,48},{56,64},{72,80},{88,96},{104,112},{120,128}... | collective-permute-start | bytes 122888 | tf_op jit(solution)/shard_map/ppermute | solution.py:118
  66.0 2.3 %collective-permute-done.7.refs_3_ = bf16[160,128]{1,0:T(8,128)(2,1)S(1)} collective-permute-done((bf16[160,128]{1,0:T(8,128)(2,1)S(1)}, bf16[160,128]{1,0:T(8,128)(2,1)S(1)}, u32[]{:S(2)}, u32[]{:S(2)}) %collective-permute-start.7) | collective-permute-done | bytes 40992 | tf_op jit(solution)/shard_map/ppermute | solution.py:118
  68.3 1.8 %all-to-all-done.2.mine_ref = bf16[16,112,128]{2,1,0:T(8,128)(2,1)S(1)} async-done(((bf16[16,112,128]{2,1,0:T(8,128)(2,1)}), bf16[16,112,128]{2,1,0:T(8,128)(2,1)S(1)}, u32[]{:S(2)}, u32[]{:S(2)}) %all-to-all-start.2) | async-done | bytes 458784 | tf_op jit(solution)/shard_map/all_to_all | solution.py:444
  70.1 5.0 %collective-permute-start.8 = (bf16[16,112,128]{2,1,0:T(8,128)(2,1)S(1)}, bf16[16,112,128]{2,1,0:T(8,128)(2,1)S(1)}, u32[]{:S(2)}, u32[]{:S(2)}) collective-permute-start(bf16[16,112,128]{2,1,0:T(8,128)(2,1)S(1)} %all-to-all-done.2.mine_ref), channel_id=1, source_target_pairs={{0,1},{1,0},{2,3},{3,2},{4,5},{5,4},{6,7},{7,6},{8,9},{9,8},{10,11... | collective-permute-start | bytes 1376264 | tf_op jit(solution)/shard_map/ppermute | solution.py:122
  75.2 1.6 %shard_map.95 = bf16[2,512,128]{2,1,0:T(8,128)(2,1)} custom-call(s32[2,27]{1,0:T(2,128)S(1)} %get-tuple-element.56.codes, bf16[2,512,128]{2,1,0:T(8,128)(2,1)S(1)} %get-tuple-element.72.x_ref.scaled_ref, bf16[3,1152,128]{2,1,0:T(8,128)(2,1)S(1)} %get-tuple-element.73.w_ref, f32[2,512,128]{2,1,0:T(8,128)S(1)} %get-tuple-element.74.pre_grad_ref, ...), custom_call_target="tpu_custom_call" | custom-call | tf_op jit(solution)/shard_map/pallas_call | solution.py:328
  76.8 0.0 collective-permute-done.8.other_ref
  76.8 1.3 %shard_map.96 = (f32[27,128,128]{2,1,0:T(8,128)}, f32[1,128]{1,0:T(1,128)}) custom-call(bf16[16,112,128]{2,1,0:T(8,128)(2,1)S(1)} %all-to-all-done.2.mine_ref, bf16[16,112,128]{2,1,0:T(8,128)(2,1)S(1)} %collective-permute-done.8.other_ref), custom_call_target="tpu_custom_call" | custom-call | tf_op jit(solution)/shard_map/pallas_call | solution.py:416
  (4 shorter events, 0.1 us)
Async XLA Ops:
  0.6 17.1 %copy-start.4 = (f32[128]{0:T(128)S(1)}, f32[128]{0:T(128)}, u32[]{:S(2)}) copy-start(f32[128]{0:T(128)} %param.9) | copy-start | bytes 1540
  0.6 1.0 %copy-start.1 = (bf16[1,1,2,512,128]{4,3,2,1,0:T(8,128)(2,1)S(1)}, bf16[1,1,2,512,128]{4,3,2,1,0:T(8,128)(2,1)}, u32[]{:S(2)}) copy-start(bf16[1,1,2,512,128]{4,3,2,1,0:T(8,128)(2,1)} %param.5) | copy-start | bytes 786436
  1.6 7.9 %collective-permute-start = (bf16[128,128]{1,0:T(8,128)(2,1)S(1)}, bf16[128,128]{1,0:T(8,128)(2,1)S(1)}, u32[]{:S(2)}, u32[]{:S(2)}) collective-permute-start(bf16[128,128]{1,0:T(8,128)(2,1)S(1)} %get-tuple-element.49), channel_id=1, source_target_pairs={{0,1},{1,0},{2,3},{3,2},{4,5},{5,4},{6,7},{7,6},{8,9},{9,8},{10,11... | collective-permute-start | bytes 98312 | tf_op jit(solution)/shard_map/ppermute | solution.py:122
  2.4 7.1 %collective-permute-start.1 = (bf16[128,128]{1,0:T(8,128)(2,1)S(1)}, bf16[128,128]{1,0:T(8,128)(2,1)S(1)}, u32[]{:S(2)}, u32[]{:S(2)}) collective-permute-start(bf16[128,128]{1,0:T(8,128)(2,1)S(1)} %get-tuple-element.50), channel_id=1, source_target_pairs={{1,2},{3,4},{5,6},{2,1},{4,3},{6,5},{9,10},{11,12},{13,14},{10,9},... | collective-permute-start | bytes 98312 | tf_op jit(solution)/shard_map/ppermute | solution.py:112
  7.2 1.2 %copy-start = (bf16[27,128,128]{2,1,0:T(8,128)(2,1)S(1)}, bf16[27,128,128]{2,1,0:T(8,128)(2,1)}, u32[]{:S(2)}) copy-start(bf16[27,128,128]{2,1,0:T(8,128)(2,1)} %w_ref.1) | copy-start | bytes 2654212
  8.4 0.7 copy-start.3
  9.6 7.7 %collective-permute-start.2 = (bf16[160,128]{1,0:T(8,128)(2,1)S(1)}, bf16[160,128]{1,0:T(8,128)(2,1)S(1)}, u32[]{:S(2)}, u32[]{:S(2)}) collective-permute-start(bf16[160,128]{1,0:T(8,128)(2,1)S(1)} %get-tuple-element.60), channel_id=1, source_target_pairs={{0,8},{16,24},{32,40},{48,56},{64,72},{80,88},{96,104},{112,120},{... | collective-permute-start | bytes 122888 | tf_op jit(solution)/shard_map/ppermute | solution.py:118
  10.9 6.8 %collective-permute-start.3 = (bf16[160,128]{1,0:T(8,128)(2,1)S(1)}, bf16[160,128]{1,0:T(8,128)(2,1)S(1)}, u32[]{:S(2)}, u32[]{:S(2)}) collective-permute-start(bf16[160,128]{1,0:T(8,128)(2,1)S(1)} %get-tuple-element.61), channel_id=1, source_target_pairs={{8,16},{24,32},{40,48},{56,64},{72,80},{88,96},{104,112},{120,128}... | collective-permute-start | bytes 122888 | tf_op jit(solution)/shard_map/ppermute | solution.py:118
  14.1 1.0 %copy-start.2 = (bf16[1,1,2,512,128]{4,3,2,1,0:T(8,128)(2,1)S(1)}, bf16[1,1,2,512,128]{4,3,2,1,0:T(8,128)(2,1)}, u32[]{:S(2)}) copy-start(bf16[1,1,2,512,128]{4,3,2,1,0:T(8,128)(2,1)} %param.6) | copy-start | bytes 786436
  20.9 2.0 %collective-permute-start.4 = (bf16[1920,128]{1,0:T(8,128)(2,1)S(1)}, bf16[1920,128]{1,0:T(8,128)(2,1)S(1)}, u32[]{:S(2)}, u32[]{:S(2)}) collective-permute-start(bf16[1920,128]{1,0:T(8,128)(2,1)S(1)} %get-tuple-element.76), channel_id=1, source_target_pairs={{0,1},{1,0},{2,3},{3,2},{4,5},{5,4},{6,7},{7,6},{8,9},{9,8},{10,11... | collective-permute-start | bytes 1474568 | tf_op jit(solution)/shard_map/ppermute | solution.py:122
  23.7 17.0 %all-to-all-start = ((bf16[16,112,128]{2,1,0:T(8,128)(2,1)}), bf16[16,112,128]{2,1,0:T(8,128)(2,1)S(1)}, u32[]{:S(2)}, u32[]{:S(2)}) async-start(bf16[16,112,128]{2,1,0:T(8,128)(2,1)} %get-tuple-element.79), calls=%async_computation | async-start | bytes 917504 | tf_op jit(solution)/shard_map/all_to_all | solution.py:444
  30.4 7.4 %collective-permute-start.5 = (bf16[128,128]{1,0:T(8,128)(2,1)S(1)}, bf16[128,128]{1,0:T(8,128)(2,1)S(1)}, u32[]{:S(2)}, u32[]{:S(2)}) collective-permute-start(bf16[128,128]{1,0:T(8,128)(2,1)S(1)} %get-tuple-element.78), channel_id=1, source_target_pairs={{1,2},{3,4},{5,6},{2,1},{4,3},{6,5},{9,10},{11,12},{13,14},{10,9},... | collective-permute-start | bytes 98312 | tf_op jit(solution)/shard_map/ppermute | solution.py:112
  41.4 15.7 %all-to-all-start.1 = ((bf16[8,112,128]{2,1,0:T(8,128)(2,1)}), bf16[8,112,128]{2,1,0:T(8,128)(2,1)S(1)}, u32[]{:S(2)}, u32[]{:S(2)}) async-start(bf16[8,112,128]{2,1,0:T(8,128)(2,1)} %shard_map.93), calls=%async_computation.1 | async-start | bytes 458752 | tf_op jit(solution)/shard_map/all_to_all | solution.py:444
  49.9 2.9 %collective-permute-start.6 = (bf16[160,128]{1,0:T(8,128)(2,1)S(1)}, bf16[160,128]{1,0:T(8,128)(2,1)S(1)}, u32[]{:S(2)}, u32[]{:S(2)}) collective-permute-start(bf16[160,128]{1,0:T(8,128)(2,1)S(1)} %get-tuple-element.81), channel_id=1, source_target_pairs={{0,8},{16,24},{32,40},{48,56},{64,72},{80,88},{96,104},{112,120},{... | collective-permute-start | bytes 122888 | tf_op jit(solution)/shard_map/ppermute | solution.py:118
  57.9 12.2 %all-to-all-start.2 = ((bf16[16,112,128]{2,1,0:T(8,128)(2,1)}), bf16[16,112,128]{2,1,0:T(8,128)(2,1)S(1)}, u32[]{:S(2)}, u32[]{:S(2)}) async-start(bf16[16,112,128]{2,1,0:T(8,128)(2,1)} %shard_map.94), calls=%async_computation.2 | async-start | bytes 917504 | tf_op jit(solution)/shard_map/all_to_all | solution.py:444
  61.5 6.9 %collective-permute-start.7 = (bf16[160,128]{1,0:T(8,128)(2,1)S(1)}, bf16[160,128]{1,0:T(8,128)(2,1)S(1)}, u32[]{:S(2)}, u32[]{:S(2)}) collective-permute-start(bf16[160,128]{1,0:T(8,128)(2,1)S(1)} %get-tuple-element.86), channel_id=1, source_target_pairs={{8,16},{24,32},{40,48},{56,64},{72,80},{88,96},{104,112},{120,128}... | collective-permute-start | bytes 122888 | tf_op jit(solution)/shard_map/ppermute | solution.py:118
  70.1 6.7 %collective-permute-start.8 = (bf16[16,112,128]{2,1,0:T(8,128)(2,1)S(1)}, bf16[16,112,128]{2,1,0:T(8,128)(2,1)S(1)}, u32[]{:S(2)}, u32[]{:S(2)}) collective-permute-start(bf16[16,112,128]{2,1,0:T(8,128)(2,1)S(1)} %all-to-all-done.2.mine_ref), channel_id=1, source_target_pairs={{0,1},{1,0},{2,3},{3,2},{4,5},{5,4},{6,7},{7,6},{8,9},{9,8},{10,11... | collective-permute-start | bytes 1376264 | tf_op jit(solution)/shard_map/ppermute | solution.py:122
